TPU v7x, 32 devices: a whole 2x2x4 slice. The times are simulated.
32 devices in a mesh: feat: 4 (over x, core), rows: 8 (over z, y).
Axes of the slice: x: 2, y: 2, z: 4, core: 2. Of those that a mesh axis runs over, the one named last changes fastest.
Arguments:
- features: bfloat16 [16384, 4096], P('rows', 'feat'), may hold values from -6 to 6
- residual: float32 [16384, 1024], P('rows', 'feat'), may hold values from -8 to 8
- inverse_grams: float32 [4096, 1024], P('feat'), may hold values from -1 to 1, as said below
Outputs:
- increments: bfloat16 [1024, 4096], P(None, 'feat')
- final_residual: float32 [16384, 1024], P('rows', 'feat')
Inputs may be any that keep to these rules, and one draw needn't show every extreme that they name: `inverse_grams`: each block of 1024 rows is a symmetric positive definite matrix.
All inputs are finite; a program needn't handle non-finite values.
Results may differ from a plain program's by a relative error of at most 0.0051.
Values may be sent and summed in bfloat16 or wider, within the bound.
No kernel may reach another device: no remote copies, remote signals or barrier semaphores. Data moves between devices by JAX's collectives and lax.ppermute only.
A program may use at most 64 MiB of HBM per device.

v0:
```python
import jax
import jax.numpy as jnp
from jax import lax
from jax.sharding import PartitionSpec as P


def from_behind(value, axis, steps):
    count = lax.axis_size(axis)
    pairs = [(source, (source + steps) % count) for source in range(count)]
    return lax.ppermute(value, axis, pairs)


def on_device(features, residual, inverse_grams):
    block_total = lax.axis_size("feat")
    block_id = lax.axis_index("feat")
    piece_width = residual.shape[1]
    feat_width = features.shape[1]
    contract_rows = (((0,), (0,)), ((), ()))
    contract_cols = (((1,), (1,)), ((), ()))
    start_incr = jnp.zeros((piece_width * block_total, feat_width), jnp.bfloat16)

    def advance(visit, state_pair):
        current, increments = state_pair
        front_index = (block_id - visit) % block_total
        rounded = current.astype(jnp.bfloat16)
        partial_value = lax.dot_general(
            rounded, features, contract_rows, preferred_element_type=jnp.float32
        )
        summed_term = lax.psum(partial_value, "rows")
        update = lax.dot_general(
            summed_term, inverse_grams, contract_cols, precision=lax.Precision.HIGHEST
        ).astype(jnp.bfloat16)
        current = current - lax.dot_general(
            features, update, contract_cols, preferred_element_type=jnp.float32
        )
        increments = lax.dynamic_update_slice_in_dim(
            increments, update, front_index * piece_width, 0
        )
        current = from_behind(current, "feat", 1)
        return (current, increments)

    final_current, increments = lax.fori_loop(0, block_total, advance, (residual, start_incr))
    return (increments, final_current)


def solution(mesh):
    placed = (P("rows", "feat"), P("rows", "feat"), P("feat", None))
    return jax.shard_map(
        on_device,
        mesh=mesh,
        in_specs=placed,
        out_specs=(P(None, "feat"), P("rows", "feat")),
        check_vma=False,
    )
```

profile of v0, /device:TPU:0, one launch (start us, length us, event | category | flops | bytes accessed | tf_op | source)
XLA Modules:
  0.0 493.5 jit_solution(4223671391720553806)
XLA Ops:
  7.2 1.9 copy.5
  9.1 1.6 broadcast_in_dim.3
  10.7 474.5 %while.17 = (s32[]{:T(128)}, f32[2048,256]{0,1:T(8,128)S(1)}, bf16[1024,1024]{1,0:T(8,128)(2,1)}, bf16[2048,1024]{1,0:T(8,128)(2,1)}, f32[1024,1024]{1,0:T(8,128...) while((s32[]{:T(128)}, f32[2048,256]{0,1:T(8,128)S(1)}, ...), condition=%wide.region_2.3_spmd, body=%wide.region_0.2_spmd.sunk | while | flops 5370281984 | bytes 54002060 | solution.py:42
  10.7 0.0 all-reduce.2.cloned.1.call-start
  10.7 4.4 fusion.22
  15.1 0.0 all-reduce.2.cloned.1.call-update
  15.1 81.2 %all-reduce.2.cloned.1.call-done = f32[256,1024]{1,0:T(8,128)} async-done(((f32[256,1024]{1,0:T(8,128)}), f32[256,1024]{1,0:T(8,128)}) %all-reduce.2.cloned.1.call-update) | async-done | bytes 1048592 | tf_op jit(solution)/shard_map/while/body/eval_jaxpr/psum | solution.py:29
  96.3 0.0 copy-start
  96.3 7.1 %constant_dynamic-update-slice_fusion.2 = (bf16[1024,1024]{1,0:T(8,128)(2,1)}, bf16[256,1024]{1,0:T(8,128)(2,1)S(1)}) fusion(bf16[1024,1024]{1,0:T(8,128)(2,1)} %get-tuple-element.237, s32[]{:T(128)S(6)} %select_n.33, f32[256,1024]{1,0:T(8,128)} %all-reduce.2.cloned.1.call-done, f32[1024,1024]{1,0:T(8,128)} %get-tuple-element.251), kind=kOutput, calls=%fused_computation.5.clone.1 | convolution fusion | flops 3221487616 | bytes 6291460 | tf_op jit(solution)/shard_map/while/body/eval_jaxpr/dot_general | solution.py:30
  103.5 0.0 copy-done
  103.5 2.6 fusion.23
  106.1 0.0 collective-permute-start
  106.1 25.7 %collective-permute-done = f32[2048,256]{0,1:T(8,128)S(1)} collective-permute-done((f32[2048,256]{0,1:T(8,128)}, f32[2048,256]{0,1:T(8,128)S(1)}, u32[]{:S(2)}, u32[]{:S(2)}) %collective-permute-start) | collective-permute-done | bytes 2097184 | tf_op jit(solution)/shard_map/while/body/eval_jaxpr/ppermute | solution.py:10
  131.8 0.0 all-reduce.2.cloned.1.call-start
  131.8 4.4 fusion.22
  136.2 0.0 all-reduce.2.cloned.1.call-update
  136.2 78.1 %all-reduce.2.cloned.1.call-done = f32[256,1024]{1,0:T(8,128)} async-done(((f32[256,1024]{1,0:T(8,128)}), f32[256,1024]{1,0:T(8,128)}) %all-reduce.2.cloned.1.call-update) | async-done | bytes 1048592 | tf_op jit(solution)/shard_map/while/body/eval_jaxpr/psum | solution.py:29
  214.3 0.0 copy-start
  214.3 7.1 %constant_dynamic-update-slice_fusion.2 = (bf16[1024,1024]{1,0:T(8,128)(2,1)}, bf16[256,1024]{1,0:T(8,128)(2,1)S(1)}) fusion(bf16[1024,1024]{1,0:T(8,128)(2,1)} %get-tuple-element.237, s32[]{:T(128)S(6)} %select_n.33, f32[256,1024]{1,0:T(8,128)} %all-reduce.2.cloned.1.call-done, f32[1024,1024]{1,0:T(8,128)} %get-tuple-element.251), kind=kOutput, calls=%fused_computation.5.clone.1 | convolution fusion | flops 3221487616 | bytes 6291460 | tf_op jit(solution)/shard_map/while/body/eval_jaxpr/dot_general | solution.py:30
  221.5 0.0 copy-done
  221.5 2.6 fusion.23
  224.1 0.0 collective-permute-start
  224.1 25.7 %collective-permute-done = f32[2048,256]{0,1:T(8,128)S(1)} collective-permute-done((f32[2048,256]{0,1:T(8,128)}, f32[2048,256]{0,1:T(8,128)S(1)}, u32[]{:S(2)}, u32[]{:S(2)}) %collective-permute-start) | collective-permute-done | bytes 2097184 | tf_op jit(solution)/shard_map/while/body/eval_jaxpr/ppermute | solution.py:10
  249.7 0.0 all-reduce.2.cloned.1.call-start
  249.7 4.4 fusion.22
  254.1 0.0 all-reduce.2.cloned.1.call-update
  254.2 78.0 %all-reduce.2.cloned.1.call-done = f32[256,1024]{1,0:T(8,128)} async-done(((f32[256,1024]{1,0:T(8,128)}), f32[256,1024]{1,0:T(8,128)}) %all-reduce.2.cloned.1.call-update) | async-done | bytes 1048592 | tf_op jit(solution)/shard_map/while/body/eval_jaxpr/psum | solution.py:29
  332.2 0.0 copy-start
  332.2 7.1 %constant_dynamic-update-slice_fusion.2 = (bf16[1024,1024]{1,0:T(8,128)(2,1)}, bf16[256,1024]{1,0:T(8,128)(2,1)S(1)}) fusion(bf16[1024,1024]{1,0:T(8,128)(2,1)} %get-tuple-element.237, s32[]{:T(128)S(6)} %select_n.33, f32[256,1024]{1,0:T(8,128)} %all-reduce.2.cloned.1.call-done, f32[1024,1024]{1,0:T(8,128)} %get-tuple-element.251), kind=kOutput, calls=%fused_computation.5.clone.1 | convolution fusion | flops 3221487616 | bytes 6291460 | tf_op jit(solution)/shard_map/while/body/eval_jaxpr/dot_general | solution.py:30
  339.3 0.0 copy-done
  339.3 2.6 fusion.23
  341.9 0.0 collective-permute-start
  341.9 25.7 %collective-permute-done = f32[2048,256]{0,1:T(8,128)S(1)} collective-permute-done((f32[2048,256]{0,1:T(8,128)}, f32[2048,256]{0,1:T(8,128)S(1)}, u32[]{:S(2)}, u32[]{:S(2)}) %collective-permute-start) | collective-permute-done | bytes 2097184 | tf_op jit(solution)/shard_map/while/body/eval_jaxpr/ppermute | solution.py:10
  367.6 0.0 all-reduce.2.cloned.1.call-start
  367.6 4.4 fusion.22
  372.0 0.0 all-reduce.2.cloned.1.call-update
  372.1 77.7 %all-reduce.2.cloned.1.call-done = f32[256,1024]{1,0:T(8,128)} async-done(((f32[256,1024]{1,0:T(8,128)}), f32[256,1024]{1,0:T(8,128)}) %all-reduce.2.cloned.1.call-update) | async-done | bytes 1048592 | tf_op jit(solution)/shard_map/while/body/eval_jaxpr/psum | solution.py:29
  449.7 0.0 copy-start
  449.7 7.1 %constant_dynamic-update-slice_fusion.2 = (bf16[1024,1024]{1,0:T(8,128)(2,1)}, bf16[256,1024]{1,0:T(8,128)(2,1)S(1)}) fusion(bf16[1024,1024]{1,0:T(8,128)(2,1)} %get-tuple-element.237, s32[]{:T(128)S(6)} %select_n.33, f32[256,1024]{1,0:T(8,128)} %all-reduce.2.cloned.1.call-done, f32[1024,1024]{1,0:T(8,128)} %get-tuple-element.251), kind=kOutput, calls=%fused_computation.5.clone.1 | convolution fusion | flops 3221487616 | bytes 6291460 | tf_op jit(solution)/shard_map/while/body/eval_jaxpr/dot_general | solution.py:30
  456.9 0.0 copy-done
  456.9 2.6 fusion.23
  459.5 0.0 collective-permute-start
  459.5 25.7 %collective-permute-done = f32[2048,256]{0,1:T(8,128)S(1)} collective-permute-done((f32[2048,256]{0,1:T(8,128)}, f32[2048,256]{0,1:T(8,128)S(1)}, u32[]{:S(2)}, u32[]{:S(2)}) %collective-permute-start) | collective-permute-done | bytes 2097184 | tf_op jit(solution)/shard_map/while/body/eval_jaxpr/ppermute | solution.py:10
  485.2 1.8 copy.6
Async XLA Ops:
  10.7 85.7 %all-reduce.2.cloned.1.call-start = ((), (), s32[]{:S(2)}) async-start(), calls=%async_computation | async-start | bytes 2097152 | tf_op jit(solution)/shard_map/while/body/eval_jaxpr/psum | solution.py:29
  96.3 7.1 %copy-start = (bf16[2048,1024]{1,0:T(8,128)(2,1)S(1)}, bf16[2048,1024]{1,0:T(8,128)(2,1)}, u32[]{:S(2)}) copy-start(bf16[2048,1024]{1,0:T(8,128)(2,1)} %get-tuple-element.250) | copy-start | bytes 12582916 | tf_op jit(solution)/shard_map/while
  106.1 25.7 %collective-permute-start = (f32[2048,256]{0,1:T(8,128)}, f32[2048,256]{0,1:T(8,128)S(1)}, u32[]{:S(2)}, u32[]{:S(2)}) collective-permute-start(f32[2048,256]{0,1:T(8,128)} %fusion.23), channel_id=1, source_target_pairs={{0,8},{8,16},{16,24},{24,0},{1,9},{9,17},{17,25},{25,1},{2,10},{10... | collective-permute-start | bytes 6291464 | tf_op jit(solution)/shard_map/while/body/eval_jaxpr/ppermute | solution.py:10
  131.8 82.6 %all-reduce.2.cloned.1.call-start = ((), (), s32[]{:S(2)}) async-start(), calls=%async_computation | async-start | bytes 2097152 | tf_op jit(solution)/shard_map/while/body/eval_jaxpr/psum | solution.py:29
  214.3 7.1 %copy-start = (bf16[2048,1024]{1,0:T(8,128)(2,1)S(1)}, bf16[2048,1024]{1,0:T(8,128)(2,1)}, u32[]{:S(2)}) copy-start(bf16[2048,1024]{1,0:T(8,128)(2,1)} %get-tuple-element.250) | copy-start | bytes 12582916 | tf_op jit(solution)/shard_map/while
  224.1 25.7 %collective-permute-start = (f32[2048,256]{0,1:T(8,128)}, f32[2048,256]{0,1:T(8,128)S(1)}, u32[]{:S(2)}, u32[]{:S(2)}) collective-permute-start(f32[2048,256]{0,1:T(8,128)} %fusion.23), channel_id=1, source_target_pairs={{0,8},{8,16},{16,24},{24,0},{1,9},{9,17},{17,25},{25,1},{2,10},{10... | collective-permute-start | bytes 6291464 | tf_op jit(solution)/shard_map/while/body/eval_jaxpr/ppermute | solution.py:10
  249.7 82.4 %all-reduce.2.cloned.1.call-start = ((), (), s32[]{:S(2)}) async-start(), calls=%async_computation | async-start | bytes 2097152 | tf_op jit(solution)/shard_map/while/body/eval_jaxpr/psum | solution.py:29
  332.2 7.1 %copy-start = (bf16[2048,1024]{1,0:T(8,128)(2,1)S(1)}, bf16[2048,1024]{1,0:T(8,128)(2,1)}, u32[]{:S(2)}) copy-start(bf16[2048,1024]{1,0:T(8,128)(2,1)} %get-tuple-element.250) | copy-start | bytes 12582916 | tf_op jit(solution)/shard_map/while
  341.9 25.7 %collective-permute-start = (f32[2048,256]{0,1:T(8,128)}, f32[2048,256]{0,1:T(8,128)S(1)}, u32[]{:S(2)}, u32[]{:S(2)}) collective-permute-start(f32[2048,256]{0,1:T(8,128)} %fusion.23), channel_id=1, source_target_pairs={{0,8},{8,16},{16,24},{24,0},{1,9},{9,17},{17,25},{25,1},{2,10},{10... | collective-permute-start | bytes 6291464 | tf_op jit(solution)/shard_map/while/body/eval_jaxpr/ppermute | solution.py:10
  367.6 82.1 %all-reduce.2.cloned.1.call-start = ((), (), s32[]{:S(2)}) async-start(), calls=%async_computation | async-start | bytes 2097152 | tf_op jit(solution)/shard_map/while/body/eval_jaxpr/psum | solution.py:29
  449.7 7.1 %copy-start = (bf16[2048,1024]{1,0:T(8,128)(2,1)S(1)}, bf16[2048,1024]{1,0:T(8,128)(2,1)}, u32[]{:S(2)}) copy-start(bf16[2048,1024]{1,0:T(8,128)(2,1)} %get-tuple-element.250) | copy-start | bytes 12582916 | tf_op jit(solution)/shard_map/while
  459.5 25.7 %collective-permute-start = (f32[2048,256]{0,1:T(8,128)}, f32[2048,256]{0,1:T(8,128)S(1)}, u32[]{:S(2)}, u32[]{:S(2)}) collective-permute-start(f32[2048,256]{0,1:T(8,128)} %fusion.23), channel_id=1, source_target_pairs={{0,8},{8,16},{16,24},{24,0},{1,9},{9,17},{17,25},{25,1},{2,10},{10... | collective-permute-start | bytes 6291464 | tf_op jit(solution)/shard_map/while/body/eval_jaxpr/ppermute | solution.py:10
Sparse Core Ops, SparseCore 0:
  15.6 80.7 all-reduce.1
  136.7 77.6 all-reduce.1
  254.6 77.4 all-reduce.1
  372.2 77.4 all-reduce.1
where the time goes:
time: 494 us; the launch traced here: 493 us
  waiting for transfers between devices  418 us (85%)
  matrix products  56.6 us (11%)
  between operations  13.7 us (3%)
  local copies, waits for them, and re-layouts  5.33 us (1%)
    psum x4, waiting for transfers between devices, advance(): summed_term = lax.psum(partial_value, 'rows')  315 us
    ppermute x4, waiting for transfers between devices, from_behind(): return lax.ppermute(value, axis, pairs)  103 us
    dot_general x4, matrix products, advance(): lax.dot_general(summed_term, inverse_grams, contract_cols, precision=lax....  28.5 us
    dot_general x4, matrix products, advance(): lax.dot_general(rounded, features, contract_rows, preferred_element_type=...  17.6 us
    dot_general x4, matrix products, advance(): lax.dot_general(features, update, contract_cols, preferred_element_type=j...  10.4 us
  transfers between devices with their start and end apart: 8, of which 8 were waited for; matrix products, arithmetic and copies ran while one was open for 0% of the time, Pallas kernels for 0%

commit v1 on v0

v1 whole, which is shorter than its diff:
```python
import jax
import jax.numpy as jnp
from jax import lax
from jax.sharding import PartitionSpec as P

BF16 = jnp.bfloat16
F32 = jnp.float32


def send(value, axis, pairs):
    return lax.ppermute(value, axis, pairs)


def on_device(features, residual, inverse_grams):
    blocks = lax.axis_size("feat")
    block_id = lax.axis_index("feat")
    shards = lax.axis_size("rows")
    shard_id = lax.axis_index("rows")
    width = residual.shape[1]
    feat_width = features.shape[1]
    inner = 2
    outer = shards // inner
    inner_id = shard_id % inner
    outer_id = shard_id // inner
    half = width // inner
    piece = half // outer
    next_block = [(source, (source + 1) % blocks) for source in range(blocks)]
    partner = [(source, source ^ 1) for source in range(shards)]

    def outer_step(step):
        return [
            (o * inner + i, ((o + step) % outer) * inner + i)
            for o in range(outer)
            for i in range(inner)
        ]

    inverse_high = inverse_grams.astype(BF16)
    inverse_low = (inverse_grams - inverse_high.astype(F32)).astype(BF16)

    def project(current):
        return lax.dot_general(
            current, features, (((0,), (0,)), ((), ())), preferred_element_type=F32
        )

    def apply_inverse(projected):
        high = projected.astype(BF16)
        low = (projected - high.astype(F32)).astype(BF16)
        dims = (((1,), (1,)), ((), ()))
        dot = lambda a, b: lax.dot_general(a, b, dims, preferred_element_type=F32)
        both = dot(jnp.concatenate([high, low], 0), inverse_high)
        return (both[: high.shape[0]] + both[high.shape[0]:] + dot(high, inverse_low)).astype(BF16)

    def subtract(current, update):
        change = lax.dot_general(
            features, update, (((1,), (1,)), ((), ())), preferred_element_type=F32
        )
        return current.astype(F32) - change

    def reduce_outer(total):
        parts = [lax.dynamic_slice_in_dim(total, outer_id * piece, piece, 0)]
        for step in range(1, outer):
            target = (outer_id + step) % outer
            out = lax.dynamic_slice_in_dim(total, target * piece, piece, 0).astype(BF16)
            parts.append(send(out, "rows", outer_step(step)).astype(F32))
        return sum(parts[1:], parts[0])

    def gather_outer(update):
        full = jnp.zeros((half, feat_width), BF16)
        full = lax.dynamic_update_slice_in_dim(full, update, outer_id * piece, 0)
        for step in range(1, outer):
            source = (outer_id - step) % outer
            got = send(update, "rows", outer_step(step))
            full = lax.dynamic_update_slice_in_dim(full, got, source * piece, 0)
        return full

    increments = jnp.zeros((width * blocks, feat_width), BF16)
    halves = [lax.dynamic_slice_in_dim(residual, s * half, half, 1) for s in (1 - inner_id, inner_id)]
    lead = 1 - inner_id
    for visit in range(blocks):
        front = (block_id - visit) % blocks
        away, home = halves
        arrived = send(project(away.astype(BF16)).astype(BF16), "rows", partner)
        total = project(home.astype(BF16)) + arrived.astype(F32)
        update_home = gather_outer(apply_inverse(reduce_outer(total)))
        update_away = send(update_home, "rows", partner)
        home = subtract(home, update_home)
        away = subtract(away, update_away)
        start = front * width
        increments = lax.dynamic_update_slice_in_dim(increments, update_home, start + (1 - lead) * half, 0)
        increments = lax.dynamic_update_slice_in_dim(increments, update_away, start + lead * half, 0)
        halves = [send(part.astype(BF16), "feat", next_block) for part in (home, away)]
        lead = 1 - lead
    low = lead == 0
    first = jnp.where(low, halves[0], halves[1])
    second = jnp.where(low, halves[1], halves[0])
    return increments, jnp.concatenate([first, second], 1).astype(F32)


def solution(mesh):
    placed = (P("rows", "feat"), P("rows", "feat"), P("feat", None))
    return jax.shard_map(
        on_device,
        mesh=mesh,
        in_specs=placed,
        out_specs=(P(None, "feat"), P("rows", "feat")),
        check_vma=False,
    )
```

time: 494 us -> 178 us (0.36)
  waiting for transfers between devices: 418 us -> 84.9 us
  starting transfers between devices: 0.02 us -> 45.2 us
  matrix products: 56.6 us -> 37.9 us
  between operations: 13.7 us -> 1.24 us
    psum x4 -> x0, waiting for transfers between devices: 315 us -> none  [advance(): summed_term = lax.psum(partial_value, 'rows')]
    ppermute x4 -> x40, starting transfers between devices: 0.01 us -> 45.2 us  [send(): return lax.ppermute(value, axis, pairs)]
    dot_general x12 -> x24, matrix products: 56.6 us -> 37.9 us  [the longest x8 16.4 us: subtract(): lax.dot_general(features, update, (((1,), (1,)), ((), ())), preferred_ele...]
    ppermute x4 -> x40, waiting for transfers between devices: 103 us -> 84.9 us  [send(): return lax.ppermute(value, axis, pairs)]
  transfers between devices with their start and end apart: 8 -> 40, of which waited for: 8 -> 37; matrix products, arithmetic and copies ran while one was open for 0% -> 13% of each run, Pallas kernels for 0% -> 0%
where the time goes in v1:
time: 178 us
  waiting for transfers between devices  84.9 us (48%)
  starting transfers between devices  45.2 us (25%)
  matrix products  37.9 us (21%)
  local copies, waits for them, and re-layouts  5.01 us (3%)
  other arithmetic  3.57 us (2%)
    ppermute x40, waiting for transfers between devices, send(): return lax.ppermute(value, axis, pairs)  84.9 us
    ppermute x40, starting transfers between devices, send(): return lax.ppermute(value, axis, pairs)  45.2 us
    dot_general x8, matrix products, subtract(): lax.dot_general(features, update, (((1,), (1,)), ((), ())), preferred_ele...  16.4 us
    dot_general x8, matrix products, project(): lax.dot_general(current, features, (((0,), (0,)), ((), ())), preferred_el...  14 us
    dot_general x8, matrix products, apply_inverse(): dot = lambda a, b: lax.dot_general(a, b, dims, preferred_element_type=F32)  7.52 us
  transfers between devices with their start and end apart: 40, of which 37 were waited for; matrix products, arithmetic and copies ran while one was open for 13% of the time, Pallas kernels for 0%

profile of v1, /device:TPU:0, one launch (start us, length us, event | category | flops | bytes accessed | tf_op | source)
XLA Modules:
  0.0 177.8 jit_solution(18301617725295872190)
XLA Ops:
  0.7 1.7 constant_dynamic-slice_fusion.1
  2.7 3.6 %convolution_convert_fusion.3 = bf16[128,1024]{1,0:T(8,128)(2,1)} fusion(bf16[2048,1024]{1,0:T(8,128)(2,1)} %param.3, f32[2048,128]{0,1:T(8,128)S(1)} %copy.9), kind=kOutput, calls=%fused_computation.19 | convolution fusion | flops 537264128 | bytes 5505024 | tf_op jit(solution)/shard_map/dot_general | solution.py:41
  6.3 3.0 %collective-permute-start = (bf16[128,1024]{1,0:T(8,128)(2,1)}, bf16[128,1024]{1,0:T(8,128)(2,1)S(1)}, u32[]{:S(2)}, u32[]{:S(2)}) collective-permute-start(bf16[128,1024]{1,0:T(8,128)(2,1)} %convolution_convert_fusion.3), channel_id=1, source_target_pairs={{0,1},{1,0},{2,3},{3,2},{4,5},{5,4},{6,7},{7,6},{8,9},{9,8},{10,11... | collective-permute-start | bytes 786440 | tf_op jit(solution)/shard_map/ppermute | solution.py:11
  9.6 6.1 %collective-permute-done = bf16[128,1024]{1,0:T(8,128)(2,1)S(1)} collective-permute-done((bf16[128,1024]{1,0:T(8,128)(2,1)}, bf16[128,1024]{1,0:T(8,128)(2,1)S(1)}, u32[]{:S(2)}, u32[]{:S(2)}) %collective-permute-start) | collective-permute-done | bytes 262176 | tf_op jit(solution)/shard_map/ppermute | solution.py:11
  15.8 2.9 %convert_add_fusion = f32[128,1024]{1,0:T(8,128)S(1)} fusion(bf16[128,1024]{1,0:T(8,128)(2,1)S(1)} %collective-permute-done, bf16[2048,1024]{1,0:T(8,128)(2,1)} %param.3, f32[2048,128]{0,1:T(8,128)S(1)} %copy.8), kind=kOutput, calls=%fused_computation.35 | convolution fusion | flops 537395200 | bytes 6029312 | tf_op jit(solution)/shard_map/dot_general | solution.py:41
  18.7 1.9 %collective-permute-start.1 = (bf16[32,1024]{1,0:T(8,128)(2,1)S(1)}, bf16[32,1024]{1,0:T(8,128)(2,1)S(1)}, u32[]{:S(2)}, u32[]{:S(2)}) collective-permute-start(bf16[32,1024]{1,0:T(8,128)(2,1)S(1)} %get-tuple-element.27), channel_id=1, source_target_pairs={{0,2},{1,3},{2,4},{3,5},{4,6},{5,7},{6,0},{7,1},{8,10},{9,11},{10,... | collective-permute-start | bytes 196616 | tf_op jit(solution)/shard_map/ppermute | solution.py:11
  20.6 2.6 %collective-permute-start.2 = (bf16[32,1024]{1,0:T(8,128)(2,1)S(1)}, bf16[32,1024]{1,0:T(8,128)(2,1)S(1)}, u32[]{:S(2)}, u32[]{:S(2)}) collective-permute-start(bf16[32,1024]{1,0:T(8,128)(2,1)S(1)} %get-tuple-element.29), channel_id=1, source_target_pairs={{0,4},{1,5},{2,6},{3,7},{4,0},{5,1},{6,2},{7,3},{8,12},{9,13},{10,... | collective-permute-start | bytes 196616 | tf_op jit(solution)/shard_map/ppermute | solution.py:11
  23.2 1.3 collective-permute-start.3
  24.5 2.2 %subtract_convert_fusion = (bf16[1024,1024]{1,0:T(8,128)(2,1)S(1)}, bf16[1024,1024]{1,0:T(8,128)(2,1)}) fusion(f32[1024,1024]{1,0:T(8,128)S(1)} %copy-done.5), kind=kLoop, calls=%fused_computation | loop fusion | flops 4194304 | bytes 8388608 | tf_op jit(solution)/shard_map/convert_element_type | solution.py:38
  28.7 2.4 %fusion.13 = f32[64,1024]{1,0:T(8,128)S(1)} fusion(bf16[1024,1024]{1,0:T(8,128)(2,1)} %get-tuple-element.13, bf16[32,1024]{1,0:T(8,128)(2,1)S(1)} %get-tuple-element.10, bf16[32,1024]{1,0:T(8,128)(2,1)S(1)} %get-tuple-element.11), kind=kOutput, calls=%fused_computation.45 | convolution fusion | flops 134479872 | bytes 2490368 | tf_op jit(solution)/shard_map/dot_general | solution.py:49
  31.8 1.0 collective-permute-start.4
  32.7 2.5 %collective-permute-start.5 = (bf16[32,1024]{1,0:T(8,128)(2,1)S(1)}, bf16[32,1024]{1,0:T(8,128)(2,1)S(1)}, u32[]{:S(2)}, u32[]{:S(2)}) collective-permute-start(bf16[32,1024]{1,0:T(8,128)(2,1)S(1)} %get-tuple-element.31), channel_id=1, source_target_pairs={{0,4},{1,5},{2,6},{3,7},{4,0},{5,1},{6,2},{7,3},{8,12},{9,13},{10,... | collective-permute-start | bytes 196616 | tf_op jit(solution)/shard_map/ppermute | solution.py:11
  35.6 2.3 %collective-permute-done.4 = bf16[32,1024]{1,0:T(8,128)(2,1)S(1)} collective-permute-done((bf16[32,1024]{1,0:T(8,128)(2,1)S(1)}, bf16[32,1024]{1,0:T(8,128)(2,1)S(1)}, u32[]{:S(2)}, u32[]{:S(2)}) %collective-permute-start.4) | collective-permute-done | bytes 65568 | tf_op jit(solution)/shard_map/ppermute | solution.py:11
  38.0 1.5 collective-permute-done.5
  40.1 1.5 collective-permute-start.7
  41.6 4.0 %fusion.3 = bf16[2048,128]{0,1:T(8,128)(2,1)S(1)} fusion(f32[2048,128]{0,1:T(8,128)} %copy-done.4, bf16[128,1024]{1,0:T(8,128)(2,1)S(1)} %constant_dynamic-update-slice_fusion.20, bf16[2048,1024]{1,0:T(8,128)(2,1)} %param.3), kind=kOutput, calls=%fused_computation.12 | convolution fusion | flops 537395200 | bytes 6029312 | tf_op jit(solution)/shard_map/dot_general | solution.py:54
  46.6 1.5 fusion.2
  48.9 5.4 %collective-permute-done.9 = bf16[2048,128]{0,1:T(8,128)(2,1)S(1)} collective-permute-done((bf16[2048,128]{0,1:T(8,128)(2,1)S(1)}, bf16[2048,128]{0,1:T(8,128)(2,1)S(1)}, u32[]{:S(2)}, u32[]{:S(2)}) %collective-permute-start.9) | collective-permute-done | bytes 524320 | tf_op jit(solution)/shard_map/ppermute | solution.py:11
  55.0 1.0 collective-permute-start.10
  56.0 3.9 %collective-permute-done.8 = bf16[2048,128]{0,1:T(8,128)(2,1)S(1)} collective-permute-done((bf16[2048,128]{0,1:T(8,128)(2,1)S(1)}, bf16[2048,128]{0,1:T(8,128)(2,1)S(1)}, u32[]{:S(2)}, u32[]{:S(2)}) %collective-permute-start.8) | collective-permute-done | bytes 524320 | tf_op jit(solution)/shard_map/ppermute | solution.py:11
  59.9 2.5 %collective-permute-done.10 = bf16[128,1024]{1,0:T(8,128)(2,1)S(1)} collective-permute-done((bf16[128,1024]{1,0:T(8,128)(2,1)S(1)}, bf16[128,1024]{1,0:T(8,128)(2,1)S(1)}, u32[]{:S(2)}, u32[]{:S(2)}) %collective-permute-start.10) | collective-permute-done | bytes 262176 | tf_op jit(solution)/shard_map/ppermute | solution.py:11
  63.8 2.3 %collective-permute-start.12 = (bf16[32,1024]{1,0:T(8,128)(2,1)S(1)}, bf16[32,1024]{1,0:T(8,128)(2,1)S(1)}, u32[]{:S(2)}, u32[]{:S(2)}) collective-permute-start(bf16[32,1024]{1,0:T(8,128)(2,1)S(1)} %get-tuple-element.26), channel_id=1, source_target_pairs={{0,4},{1,5},{2,6},{3,7},{4,0},{5,1},{6,2},{7,3},{8,12},{9,13},{10,... | collective-permute-start | bytes 196616 | tf_op jit(solution)/shard_map/ppermute | solution.py:11
  67.1 2.3 %collective-permute-done.11 = bf16[32,1024]{1,0:T(8,128)(2,1)S(1)} collective-permute-done((bf16[32,1024]{1,0:T(8,128)(2,1)S(1)}, bf16[32,1024]{1,0:T(8,128)(2,1)S(1)}, u32[]{:S(2)}, u32[]{:S(2)}) %collective-permute-start.11) | collective-permute-done | bytes 65568 | tf_op jit(solution)/shard_map/ppermute | solution.py:11
  69.4 1.1 collective-permute-done.12
  72.3 1.2 collective-permute-start.14
  73.5 2.3 %collective-permute-start.15 = (bf16[32,1024]{1,0:T(8,128)(2,1)S(1)}, bf16[32,1024]{1,0:T(8,128)(2,1)S(1)}, u32[]{:S(2)}, u32[]{:S(2)}) collective-permute-start(bf16[32,1024]{1,0:T(8,128)(2,1)S(1)} %get-tuple-element.33), channel_id=1, source_target_pairs={{0,4},{1,5},{2,6},{3,7},{4,0},{5,1},{6,2},{7,3},{8,12},{9,13},{10,... | collective-permute-start | bytes 196616 | tf_op jit(solution)/shard_map/ppermute | solution.py:11
  76.1 2.3 %collective-permute-done.14 = bf16[32,1024]{1,0:T(8,128)(2,1)S(1)} collective-permute-done((bf16[32,1024]{1,0:T(8,128)(2,1)S(1)}, bf16[32,1024]{1,0:T(8,128)(2,1)S(1)}, u32[]{:S(2)}, u32[]{:S(2)}) %collective-permute-start.14) | collective-permute-done | bytes 65568 | tf_op jit(solution)/shard_map/ppermute | solution.py:11
  78.4 1.4 collective-permute-done.15
  81.3 1.5 subtract_convert_fusion.5
  83.1 3.8 %collective-permute-done.17 = bf16[128,1024]{1,0:T(8,128)(2,1)S(1)} collective-permute-done((bf16[128,1024]{1,0:T(8,128)(2,1)S(1)}, bf16[128,1024]{1,0:T(8,128)(2,1)S(1)}, u32[]{:S(2)}, u32[]{:S(2)}) %collective-permute-start.17) | collective-permute-done | bytes 262176 | tf_op jit(solution)/shard_map/ppermute | solution.py:11
  86.9 1.5 subtract_convert_fusion.6
  88.5 3.2 %collective-permute-done.19 = bf16[2048,128]{0,1:T(8,128)(2,1)S(1)} collective-permute-done((bf16[2048,128]{0,1:T(8,128)(2,1)S(1)}, bf16[2048,128]{0,1:T(8,128)(2,1)S(1)}, u32[]{:S(2)}, u32[]{:S(2)}) %collective-permute-start.19) | collective-permute-done | bytes 524320 | tf_op jit(solution)/shard_map/ppermute | solution.py:11
  92.4 1.3 collective-permute-start.20
  93.7 5.1 %collective-permute-done.20 = bf16[128,1024]{1,0:T(8,128)(2,1)S(1)} collective-permute-done((bf16[128,1024]{1,0:T(8,128)(2,1)S(1)}, bf16[128,1024]{1,0:T(8,128)(2,1)S(1)}, u32[]{:S(2)}, u32[]{:S(2)}) %collective-permute-start.20) | collective-permute-done | bytes 262176 | tf_op jit(solution)/shard_map/ppermute | solution.py:11
  100.3 2.4 %collective-permute-start.22 = (bf16[32,1024]{1,0:T(8,128)(2,1)S(1)}, bf16[32,1024]{1,0:T(8,128)(2,1)S(1)}, u32[]{:S(2)}, u32[]{:S(2)}) collective-permute-start(bf16[32,1024]{1,0:T(8,128)(2,1)S(1)} %get-tuple-element.23), channel_id=1, source_target_pairs={{0,4},{1,5},{2,6},{3,7},{4,0},{5,1},{6,2},{7,3},{8,12},{9,13},{10,... | collective-permute-start | bytes 196616 | tf_op jit(solution)/shard_map/ppermute | solution.py:11
  103.5 2.3 %collective-permute-done.21 = bf16[32,1024]{1,0:T(8,128)(2,1)S(1)} collective-permute-done((bf16[32,1024]{1,0:T(8,128)(2,1)S(1)}, bf16[32,1024]{1,0:T(8,128)(2,1)S(1)}, u32[]{:S(2)}, u32[]{:S(2)}) %collective-permute-start.21) | collective-permute-done | bytes 65568 | tf_op jit(solution)/shard_map/ppermute | solution.py:11
  105.8 1.1 collective-permute-done.22
  108.7 1.2 collective-permute-start.24
  109.9 2.8 %collective-permute-start.25 = (bf16[32,1024]{1,0:T(8,128)(2,1)S(1)}, bf16[32,1024]{1,0:T(8,128)(2,1)S(1)}, u32[]{:S(2)}, u32[]{:S(2)}) collective-permute-start(bf16[32,1024]{1,0:T(8,128)(2,1)S(1)} %get-tuple-element.35), channel_id=1, source_target_pairs={{0,4},{1,5},{2,6},{3,7},{4,0},{5,1},{6,2},{7,3},{8,12},{9,13},{10,... | collective-permute-start | bytes 196616 | tf_op jit(solution)/shard_map/ppermute | solution.py:11
  112.7 2.1 %collective-permute-done.24 = bf16[32,1024]{1,0:T(8,128)(2,1)S(1)} collective-permute-done((bf16[32,1024]{1,0:T(8,128)(2,1)S(1)}, bf16[32,1024]{1,0:T(8,128)(2,1)S(1)}, u32[]{:S(2)}, u32[]{:S(2)}) %collective-permute-start.24) | collective-permute-done | bytes 65568 | tf_op jit(solution)/shard_map/ppermute | solution.py:11
  114.9 1.3 collective-permute-done.25
  117.0 1.4 collective-permute-start.27
  118.4 1.5 subtract_convert_fusion.3
  119.9 3.5 %collective-permute-done.27 = bf16[128,1024]{1,0:T(8,128)(2,1)S(1)} collective-permute-done((bf16[128,1024]{1,0:T(8,128)(2,1)S(1)}, bf16[128,1024]{1,0:T(8,128)(2,1)S(1)}, u32[]{:S(2)}, u32[]{:S(2)}) %collective-permute-start.27) | collective-permute-done | bytes 262176 | tf_op jit(solution)/shard_map/ppermute | solution.py:11
  123.5 2.3 %subtract_convert_fusion.4 = bf16[2048,128]{0,1:T(8,128)(2,1)} fusion(bf16[2048,128]{0,1:T(8,128)(2,1)S(1)} %collective-permute-done.19, bf16[128,1024]{1,0:T(8,128)(2,1)S(1)} %collective-permute-done.27, bf16[2048,1024]{1,0:T(8,128)(2,1)S(1)} %copy-done), kind=kOutput, calls=%fused_computation.32 | convolution fusion | flops 537657344 | bytes 5505024 | tf_op jit(solution)/shard_map/dot_general | solution.py:54
  125.8 2.8 %collective-permute-done.29 = bf16[2048,128]{0,1:T(8,128)(2,1)S(1)} collective-permute-done((bf16[2048,128]{0,1:T(8,128)(2,1)S(1)}, bf16[2048,128]{0,1:T(8,128)(2,1)S(1)}, u32[]{:S(2)}, u32[]{:S(2)}) %collective-permute-start.29) | collective-permute-done | bytes 524320 | tf_op jit(solution)/shard_map/ppermute | solution.py:11
  128.5 1.4 convolution_convert_fusion
  131.0 6.4 %collective-permute-done.30 = bf16[128,1024]{1,0:T(8,128)(2,1)} collective-permute-done((bf16[128,1024]{1,0:T(8,128)(2,1)}, bf16[128,1024]{1,0:T(8,128)(2,1)}, u32[]{:S(2)}, u32[]{:S(2)}) %collective-permute-start.30) | collective-permute-done | bytes 262176 | tf_op jit(solution)/shard_map/ppermute | solution.py:11
  137.4 3.1 %convolution_add_fusion = f32[128,1024]{1,0:T(8,128)S(1)} fusion(bf16[2048,128]{0,1:T(8,128)(2,1)} %collective-permute-done.28, bf16[2048,1024]{1,0:T(8,128)(2,1)} %param.3, bf16[128,1024]{1,0:T(8,128)(2,1)} %collective-permute-done.30), kind=kOutput, calls=%fused_computation.13 | convolution fusion | flops 537133056 | bytes 5505024 | tf_op jit(solution)/shard_map/dot_general | solution.py:41
  141.1 2.3 %collective-permute-start.32 = (bf16[32,1024]{1,0:T(8,128)(2,1)S(1)}, bf16[32,1024]{1,0:T(8,128)(2,1)S(1)}, u32[]{:S(2)}, u32[]{:S(2)}) collective-permute-start(bf16[32,1024]{1,0:T(8,128)(2,1)S(1)} %get-tuple-element.20), channel_id=1, source_target_pairs={{0,4},{1,5},{2,6},{3,7},{4,0},{5,1},{6,2},{7,3},{8,12},{9,13},{10,... | collective-permute-start | bytes 196616 | tf_op jit(solution)/shard_map/ppermute | solution.py:11
  143.4 1.0 collective-permute-start.33
  144.4 2.3 %collective-permute-done.31 = bf16[32,1024]{1,0:T(8,128)(2,1)S(1)} collective-permute-done((bf16[32,1024]{1,0:T(8,128)(2,1)S(1)}, bf16[32,1024]{1,0:T(8,128)(2,1)S(1)}, u32[]{:S(2)}, u32[]{:S(2)}) %collective-permute-start.31) | collective-permute-done | bytes 65568 | tf_op jit(solution)/shard_map/ppermute | solution.py:11
  146.7 1.1 collective-permute-done.32
  149.5 1.3 collective-permute-start.34
  150.9 2.3 %collective-permute-start.35 = (bf16[32,1024]{1,0:T(8,128)(2,1)S(1)}, bf16[32,1024]{1,0:T(8,128)(2,1)S(1)}, u32[]{:S(2)}, u32[]{:S(2)}) collective-permute-start(bf16[32,1024]{1,0:T(8,128)(2,1)S(1)} %get-tuple-element.37), channel_id=1, source_target_pairs={{0,4},{1,5},{2,6},{3,7},{4,0},{5,1},{6,2},{7,3},{8,12},{9,13},{10,... | collective-permute-start | bytes 196616 | tf_op jit(solution)/shard_map/ppermute | solution.py:11
  153.5 2.1 %collective-permute-done.34 = bf16[32,1024]{1,0:T(8,128)(2,1)S(1)} collective-permute-done((bf16[32,1024]{1,0:T(8,128)(2,1)S(1)}, bf16[32,1024]{1,0:T(8,128)(2,1)S(1)}, u32[]{:S(2)}, u32[]{:S(2)}) %collective-permute-start.34) | collective-permute-done | bytes 65568 | tf_op jit(solution)/shard_map/ppermute | solution.py:11
  155.6 1.4 collective-permute-done.35
  157.7 1.1 collective-permute-start.37
  158.8 2.6 %subtract_convert_fusion.2 = bf16[2048,128]{0,1:T(8,128)(2,1)S(1)} fusion(bf16[2048,128]{0,1:T(8,128)(2,1)} %collective-permute-done.28, bf16[128,1024]{1,0:T(8,128)(2,1)S(1)} %constant_dynamic-update-slice_fusion.2, bf16[2048,1024]{1,0:T(8,128)(2,1)S(1)} %copy-done.1), kind=kOutput, calls=%fused_computation.30 | convolution fusion | flops 537657344 | bytes 5505024 | tf_op jit(solution)/shard_map/dot_general | solution.py:54
  161.5 2.7 %collective-permute-done.37 = bf16[128,1024]{1,0:T(8,128)(2,1)S(1)} collective-permute-done((bf16[128,1024]{1,0:T(8,128)(2,1)S(1)}, bf16[128,1024]{1,0:T(8,128)(2,1)S(1)}, u32[]{:S(2)}, u32[]{:S(2)}) %collective-permute-start.37) | collective-permute-done | bytes 262176 | tf_op jit(solution)/shard_map/ppermute | solution.py:11
  164.2 1.5 subtract_convert_fusion.1
  165.9 4.1 %collective-permute-done.38 = bf16[2048,128]{0,1:T(8,128)(2,1)S(1)} collective-permute-done((bf16[2048,128]{0,1:T(8,128)(2,1)S(1)}, bf16[2048,128]{0,1:T(8,128)(2,1)S(1)}, u32[]{:S(2)}, u32[]{:S(2)}) %collective-permute-start.38) | collective-permute-done | bytes 524320 | tf_op jit(solution)/shard_map/ppermute | solution.py:11
  170.0 5.6 %collective-permute-done.39 = bf16[2048,128]{0,1:T(8,128)(2,1)S(1)} collective-permute-done((bf16[2048,128]{0,1:T(8,128)(2,1)S(1)}, bf16[2048,128]{0,1:T(8,128)(2,1)S(1)}, u32[]{:S(2)}, u32[]{:S(2)}) %collective-permute-start.39) | collective-permute-done | bytes 524320 | tf_op jit(solution)/shard_map/ppermute | solution.py:11
  176.0 1.8 %copy.7 = f32[2048,256]{1,0:T(8,128)} copy(f32[2048,256]{0,1:T(8,128)S(1)} %maximum_convert_fusion) | data formatting | bytes 4194304
  (108 shorter events, 23.7 us)
Async XLA Ops:
  6.3 9.5 %collective-permute-start = (bf16[128,1024]{1,0:T(8,128)(2,1)}, bf16[128,1024]{1,0:T(8,128)(2,1)S(1)}, u32[]{:S(2)}, u32[]{:S(2)}) collective-permute-start(bf16[128,1024]{1,0:T(8,128)(2,1)} %convolution_convert_fusion.3), channel_id=1, source_target_pairs={{0,1},{1,0},{2,3},{3,2},{4,5},{5,4},{6,7},{7,6},{8,9},{9,8},{10,11... | collective-permute-start | bytes 786440 | tf_op jit(solution)/shard_map/ppermute | solution.py:11
  9.6 9.1 %copy-start.4 = (f32[2048,128]{0,1:T(8,128)}, f32[2048,128]{0,1:T(8,128)S(1)}, u32[]{:S(2)}) copy-start(f32[2048,128]{0,1:T(8,128)S(1)} %copy.8) | copy-start | bytes 3145732
  9.6 14.9 %copy-start.5 = (f32[1024,1024]{1,0:T(8,128)S(1)}, f32[1024,1024]{1,0:T(8,128)}, u32[]{:S(2)}) copy-start(f32[1024,1024]{1,0:T(8,128)} %param.5) | copy-start | bytes 12582916
  18.7 4.5 %copy-start.7 = (f32[128,1024]{1,0:T(8,128)}, f32[128,1024]{1,0:T(8,128)S(1)}, u32[]{:S(2)}) copy-start(f32[128,1024]{1,0:T(8,128)S(1)} %convert_add_fusion) | copy-start | bytes 1572868
  18.7 8.0 %collective-permute-start.1 = (bf16[32,1024]{1,0:T(8,128)(2,1)S(1)}, bf16[32,1024]{1,0:T(8,128)(2,1)S(1)}, u32[]{:S(2)}, u32[]{:S(2)}) collective-permute-start(bf16[32,1024]{1,0:T(8,128)(2,1)S(1)} %get-tuple-element.27), channel_id=1, source_target_pairs={{0,2},{1,3},{2,4},{3,5},{4,6},{5,7},{6,0},{7,1},{8,10},{9,11},{10,... | collective-permute-start | bytes 196616 | tf_op jit(solution)/shard_map/ppermute | solution.py:11
  20.6 6.9 %collective-permute-start.2 = (bf16[32,1024]{1,0:T(8,128)(2,1)S(1)}, bf16[32,1024]{1,0:T(8,128)(2,1)S(1)}, u32[]{:S(2)}, u32[]{:S(2)}) collective-permute-start(bf16[32,1024]{1,0:T(8,128)(2,1)S(1)} %get-tuple-element.29), channel_id=1, source_target_pairs={{0,4},{1,5},{2,6},{3,7},{4,0},{5,1},{6,2},{7,3},{8,12},{9,13},{10,... | collective-permute-start | bytes 196616 | tf_op jit(solution)/shard_map/ppermute | solution.py:11
  23.2 4.5 %collective-permute-start.3 = (bf16[32,1024]{1,0:T(8,128)(2,1)S(1)}, bf16[32,1024]{1,0:T(8,128)(2,1)S(1)}, u32[]{:S(2)}, u32[]{:S(2)}) collective-permute-start(bf16[32,1024]{1,0:T(8,128)(2,1)S(1)} %get-tuple-element.28), channel_id=1, source_target_pairs={{0,6},{1,7},{2,0},{3,1},{4,2},{5,3},{6,4},{7,5},{8,14},{9,15},{10,... | collective-permute-start | bytes 196616 | tf_op jit(solution)/shard_map/ppermute | solution.py:11
  31.8 6.2 %collective-permute-start.4 = (bf16[32,1024]{1,0:T(8,128)(2,1)S(1)}, bf16[32,1024]{1,0:T(8,128)(2,1)S(1)}, u32[]{:S(2)}, u32[]{:S(2)}) collective-permute-start(bf16[32,1024]{1,0:T(8,128)(2,1)S(1)} %get-tuple-element.31), channel_id=1, source_target_pairs={{0,2},{1,3},{2,4},{3,5},{4,6},{5,7},{6,0},{7,1},{8,10},{9,11},{10,... | collective-permute-start | bytes 196616 | tf_op jit(solution)/shard_map/ppermute | solution.py:11
  32.7 6.7 %collective-permute-start.5 = (bf16[32,1024]{1,0:T(8,128)(2,1)S(1)}, bf16[32,1024]{1,0:T(8,128)(2,1)S(1)}, u32[]{:S(2)}, u32[]{:S(2)}) collective-permute-start(bf16[32,1024]{1,0:T(8,128)(2,1)S(1)} %get-tuple-element.31), channel_id=1, source_target_pairs={{0,4},{1,5},{2,6},{3,7},{4,0},{5,1},{6,2},{7,3},{8,12},{9,13},{10,... | collective-permute-start | bytes 196616 | tf_op jit(solution)/shard_map/ppermute | solution.py:11
  35.3 4.8 %collective-permute-start.6 = (bf16[32,1024]{1,0:T(8,128)(2,1)S(1)}, bf16[32,1024]{1,0:T(8,128)(2,1)S(1)}, u32[]{:S(2)}, u32[]{:S(2)}) collective-permute-start(bf16[32,1024]{1,0:T(8,128)(2,1)S(1)} %get-tuple-element.31), channel_id=1, source_target_pairs={{0,6},{1,7},{2,0},{3,1},{4,2},{5,3},{6,4},{7,5},{8,14},{9,15},{10,... | collective-permute-start | bytes 196616 | tf_op jit(solution)/shard_map/ppermute | solution.py:11
  40.1 6.5 %copy-start = (bf16[2048,1024]{1,0:T(8,128)(2,1)S(1)}, bf16[2048,1024]{1,0:T(8,128)(2,1)}, u32[]{:S(2)}) copy-start(bf16[2048,1024]{1,0:T(8,128)(2,1)} %param.3) | copy-start | bytes 12582916
  40.1 6.4 %collective-permute-start.7 = (bf16[128,1024]{1,0:T(8,128)(2,1)S(1)}, bf16[128,1024]{1,0:T(8,128)(2,1)S(1)}, u32[]{:S(2)}, u32[]{:S(2)}) collective-permute-start(bf16[128,1024]{1,0:T(8,128)(2,1)S(1)} %constant_dynamic-update-slice_fusion.20), channel_id=1, source_target_pairs={{0,1},{1,0},{2,3},{3,2},{4,5},{5,4},{6,7},{7,6},{8,9},{9,8},{10,11... | collective-permute-start | bytes 786440 | tf_op jit(solution)/shard_map/ppermute | solution.py:11
  45.6 8.7 %collective-permute-start.9 = (bf16[2048,128]{0,1:T(8,128)(2,1)S(1)}, bf16[2048,128]{0,1:T(8,128)(2,1)S(1)}, u32[]{:S(2)}, u32[]{:S(2)}) collective-permute-start(bf16[2048,128]{0,1:T(8,128)(2,1)S(1)} %fusion.3), channel_id=1, source_target_pairs={{0,8},{8,16},{16,24},{24,0},{1,9},{9,17},{17,25},{25,1},{2,10},{10... | collective-permute-start | bytes 1572872 | tf_op jit(solution)/shard_map/ppermute | solution.py:11
  46.6 1.5 copy-start.8
  48.1 11.8 %collective-permute-start.8 = (bf16[2048,128]{0,1:T(8,128)(2,1)S(1)}, bf16[2048,128]{0,1:T(8,128)(2,1)S(1)}, u32[]{:S(2)}, u32[]{:S(2)}) collective-permute-start(bf16[2048,128]{0,1:T(8,128)(2,1)S(1)} %fusion.2), channel_id=1, source_target_pairs={{0,8},{8,16},{16,24},{24,0},{1,9},{9,17},{17,25},{25,1},{2,10},{10... | collective-permute-start | bytes 1572872 | tf_op jit(solution)/shard_map/ppermute | solution.py:11
  55.0 15.7 %copy-start.2 = (bf16[1024,1024]{1,0:T(8,128)(2,1)S(1)}, bf16[1024,1024]{1,0:T(8,128)(2,1)}, u32[]{:S(2)}) copy-start(bf16[1024,1024]{1,0:T(8,128)(2,1)} %get-tuple-element.13) | copy-start | bytes 6291460
  55.0 7.4 %collective-permute-start.10 = (bf16[128,1024]{1,0:T(8,128)(2,1)S(1)}, bf16[128,1024]{1,0:T(8,128)(2,1)S(1)}, u32[]{:S(2)}, u32[]{:S(2)}) collective-permute-start(bf16[128,1024]{1,0:T(8,128)(2,1)S(1)} %convolution_convert_fusion.2), channel_id=1, source_target_pairs={{0,1},{1,0},{2,3},{3,2},{4,5},{5,4},{6,7},{7,6},{8,9},{9,8},{10,11... | collective-permute-start | bytes 786440 | tf_op jit(solution)/shard_map/ppermute | solution.py:11
  63.2 6.2 %collective-permute-start.11 = (bf16[32,1024]{1,0:T(8,128)(2,1)S(1)}, bf16[32,1024]{1,0:T(8,128)(2,1)S(1)}, u32[]{:S(2)}, u32[]{:S(2)}) collective-permute-start(bf16[32,1024]{1,0:T(8,128)(2,1)S(1)} %get-tuple-element.24), channel_id=1, source_target_pairs={{0,2},{1,3},{2,4},{3,5},{4,6},{5,7},{6,0},{7,1},{8,10},{9,11},{10,... | collective-permute-start | bytes 196616 | tf_op jit(solution)/shard_map/ppermute | solution.py:11
  63.8 6.7 %collective-permute-start.12 = (bf16[32,1024]{1,0:T(8,128)(2,1)S(1)}, bf16[32,1024]{1,0:T(8,128)(2,1)S(1)}, u32[]{:S(2)}, u32[]{:S(2)}) collective-permute-start(bf16[32,1024]{1,0:T(8,128)(2,1)S(1)} %get-tuple-element.26), channel_id=1, source_target_pairs={{0,4},{1,5},{2,6},{3,7},{4,0},{5,1},{6,2},{7,3},{8,12},{9,13},{10,... | collective-permute-start | bytes 196616 | tf_op jit(solution)/shard_map/ppermute | solution.py:11
  66.1 4.5 %collective-permute-start.13 = (bf16[32,1024]{1,0:T(8,128)(2,1)S(1)}, bf16[32,1024]{1,0:T(8,128)(2,1)S(1)}, u32[]{:S(2)}, u32[]{:S(2)}) collective-permute-start(bf16[32,1024]{1,0:T(8,128)(2,1)S(1)} %get-tuple-element.25), channel_id=1, source_target_pairs={{0,6},{1,7},{2,0},{3,1},{4,2},{5,3},{6,4},{7,5},{8,14},{9,15},{10,... | collective-permute-start | bytes 196616 | tf_op jit(solution)/shard_map/ppermute | solution.py:11
  72.3 6.1 %collective-permute-start.14 = (bf16[32,1024]{1,0:T(8,128)(2,1)S(1)}, bf16[32,1024]{1,0:T(8,128)(2,1)S(1)}, u32[]{:S(2)}, u32[]{:S(2)}) collective-permute-start(bf16[32,1024]{1,0:T(8,128)(2,1)S(1)} %get-tuple-element.33), channel_id=1, source_target_pairs={{0,2},{1,3},{2,4},{3,5},{4,6},{5,7},{6,0},{7,1},{8,10},{9,11},{10,... | collective-permute-start | bytes 196616 | tf_op jit(solution)/shard_map/ppermute | solution.py:11
  73.5 6.3 %collective-permute-start.15 = (bf16[32,1024]{1,0:T(8,128)(2,1)S(1)}, bf16[32,1024]{1,0:T(8,128)(2,1)S(1)}, u32[]{:S(2)}, u32[]{:S(2)}) collective-permute-start(bf16[32,1024]{1,0:T(8,128)(2,1)S(1)} %get-tuple-element.33), channel_id=1, source_target_pairs={{0,4},{1,5},{2,6},{3,7},{4,0},{5,1},{6,2},{7,3},{8,12},{9,13},{10,... | collective-permute-start | bytes 196616 | tf_op jit(solution)/shard_map/ppermute | solution.py:11
  75.8 4.7 %collective-permute-start.16 = (bf16[32,1024]{1,0:T(8,128)(2,1)S(1)}, bf16[32,1024]{1,0:T(8,128)(2,1)S(1)}, u32[]{:S(2)}, u32[]{:S(2)}) collective-permute-start(bf16[32,1024]{1,0:T(8,128)(2,1)S(1)} %get-tuple-element.33), channel_id=1, source_target_pairs={{0,6},{1,7},{2,0},{3,1},{4,2},{5,3},{6,4},{7,5},{8,14},{9,15},{10,... | collective-permute-start | bytes 196616 | tf_op jit(solution)/shard_map/ppermute | solution.py:11
  80.5 6.4 %collective-permute-start.17 = (bf16[128,1024]{1,0:T(8,128)(2,1)S(1)}, bf16[128,1024]{1,0:T(8,128)(2,1)S(1)}, u32[]{:S(2)}, u32[]{:S(2)}) collective-permute-start(bf16[128,1024]{1,0:T(8,128)(2,1)S(1)} %constant_dynamic-update-slice_fusion.14), channel_id=1, source_target_pairs={{0,1},{1,0},{2,3},{3,2},{4,5},{5,4},{6,7},{7,6},{8,9},{9,8},{10,11... | collective-permute-start | bytes 786440 | tf_op jit(solution)/shard_map/ppermute | solution.py:11
  82.8 8.8 %collective-permute-start.19 = (bf16[2048,128]{0,1:T(8,128)(2,1)S(1)}, bf16[2048,128]{0,1:T(8,128)(2,1)S(1)}, u32[]{:S(2)}, u32[]{:S(2)}) collective-permute-start(bf16[2048,128]{0,1:T(8,128)(2,1)S(1)} %subtract_convert_fusion.5), channel_id=1, source_target_pairs={{0,8},{8,16},{16,24},{24,0},{1,9},{9,17},{17,25},{25,1},{2,10},{10... | collective-permute-start | bytes 1572872 | tf_op jit(solution)/shard_map/ppermute | solution.py:11
  86.9 1.5 copy-start.10
  88.4 10.4 %collective-permute-start.18 = (bf16[2048,128]{0,1:T(8,128)(2,1)S(1)}, bf16[2048,128]{0,1:T(8,128)(2,1)S(1)}, u32[]{:S(2)}, u32[]{:S(2)}) collective-permute-start(bf16[2048,128]{0,1:T(8,128)(2,1)S(1)} %subtract_convert_fusion.6), channel_id=1, source_target_pairs={{0,8},{8,16},{16,24},{24,0},{1,9},{9,17},{17,25},{25,1},{2,10},{10... | collective-permute-start | bytes 1572872 | tf_op jit(solution)/shard_map/ppermute | solution.py:11
  92.4 6.4 %collective-permute-start.20 = (bf16[128,1024]{1,0:T(8,128)(2,1)S(1)}, bf16[128,1024]{1,0:T(8,128)(2,1)S(1)}, u32[]{:S(2)}, u32[]{:S(2)}) collective-permute-start(bf16[128,1024]{1,0:T(8,128)(2,1)S(1)} %convolution_convert_fusion.1), channel_id=1, source_target_pairs={{0,1},{1,0},{2,3},{3,2},{4,5},{5,4},{6,7},{7,6},{8,9},{9,8},{10,11... | collective-permute-start | bytes 786440 | tf_op jit(solution)/shard_map/ppermute | solution.py:11
  99.6 6.2 %collective-permute-start.21 = (bf16[32,1024]{1,0:T(8,128)(2,1)S(1)}, bf16[32,1024]{1,0:T(8,128)(2,1)S(1)}, u32[]{:S(2)}, u32[]{:S(2)}) collective-permute-start(bf16[32,1024]{1,0:T(8,128)(2,1)S(1)} %get-tuple-element.21), channel_id=1, source_target_pairs={{0,2},{1,3},{2,4},{3,5},{4,6},{5,7},{6,0},{7,1},{8,10},{9,11},{10,... | collective-permute-start | bytes 196616 | tf_op jit(solution)/shard_map/ppermute | solution.py:11
  100.3 6.7 %collective-permute-start.22 = (bf16[32,1024]{1,0:T(8,128)(2,1)S(1)}, bf16[32,1024]{1,0:T(8,128)(2,1)S(1)}, u32[]{:S(2)}, u32[]{:S(2)}) collective-permute-start(bf16[32,1024]{1,0:T(8,128)(2,1)S(1)} %get-tuple-element.23), channel_id=1, source_target_pairs={{0,4},{1,5},{2,6},{3,7},{4,0},{5,1},{6,2},{7,3},{8,12},{9,13},{10,... | collective-permute-start | bytes 196616 | tf_op jit(solution)/shard_map/ppermute | solution.py:11
  102.6 4.5 %collective-permute-start.23 = (bf16[32,1024]{1,0:T(8,128)(2,1)S(1)}, bf16[32,1024]{1,0:T(8,128)(2,1)S(1)}, u32[]{:S(2)}, u32[]{:S(2)}) collective-permute-start(bf16[32,1024]{1,0:T(8,128)(2,1)S(1)} %get-tuple-element.22), channel_id=1, source_target_pairs={{0,6},{1,7},{2,0},{3,1},{4,2},{5,3},{6,4},{7,5},{8,14},{9,15},{10,... | collective-permute-start | bytes 196616 | tf_op jit(solution)/shard_map/ppermute | solution.py:11
  108.7 6.1 %collective-permute-start.24 = (bf16[32,1024]{1,0:T(8,128)(2,1)S(1)}, bf16[32,1024]{1,0:T(8,128)(2,1)S(1)}, u32[]{:S(2)}, u32[]{:S(2)}) collective-permute-start(bf16[32,1024]{1,0:T(8,128)(2,1)S(1)} %get-tuple-element.35), channel_id=1, source_target_pairs={{0,2},{1,3},{2,4},{3,5},{4,6},{5,7},{6,0},{7,1},{8,10},{9,11},{10,... | collective-permute-start | bytes 196616 | tf_op jit(solution)/shard_map/ppermute | solution.py:11
  109.9 6.3 %collective-permute-start.25 = (bf16[32,1024]{1,0:T(8,128)(2,1)S(1)}, bf16[32,1024]{1,0:T(8,128)(2,1)S(1)}, u32[]{:S(2)}, u32[]{:S(2)}) collective-permute-start(bf16[32,1024]{1,0:T(8,128)(2,1)S(1)} %get-tuple-element.35), channel_id=1, source_target_pairs={{0,4},{1,5},{2,6},{3,7},{4,0},{5,1},{6,2},{7,3},{8,12},{9,13},{10,... | collective-permute-start | bytes 196616 | tf_op jit(solution)/shard_map/ppermute | solution.py:11
  112.7 4.3 %collective-permute-start.26 = (bf16[32,1024]{1,0:T(8,128)(2,1)S(1)}, bf16[32,1024]{1,0:T(8,128)(2,1)S(1)}, u32[]{:S(2)}, u32[]{:S(2)}) collective-permute-start(bf16[32,1024]{1,0:T(8,128)(2,1)S(1)} %get-tuple-element.35), channel_id=1, source_target_pairs={{0,6},{1,7},{2,0},{3,1},{4,2},{5,3},{6,4},{7,5},{8,14},{9,15},{10,... | collective-permute-start | bytes 196616 | tf_op jit(solution)/shard_map/ppermute | solution.py:11
  117.0 6.4 %collective-permute-start.27 = (bf16[128,1024]{1,0:T(8,128)(2,1)S(1)}, bf16[128,1024]{1,0:T(8,128)(2,1)S(1)}, u32[]{:S(2)}, u32[]{:S(2)}) collective-permute-start(bf16[128,1024]{1,0:T(8,128)(2,1)S(1)} %constant_dynamic-update-slice_fusion.8), channel_id=1, source_target_pairs={{0,1},{1,0},{2,3},{3,2},{4,5},{5,4},{6,7},{7,6},{8,9},{9,8},{10,11... | collective-permute-start | bytes 786440 | tf_op jit(solution)/shard_map/ppermute | solution.py:11
  119.9 8.7 %collective-permute-start.29 = (bf16[2048,128]{0,1:T(8,128)(2,1)S(1)}, bf16[2048,128]{0,1:T(8,128)(2,1)S(1)}, u32[]{:S(2)}, u32[]{:S(2)}) collective-permute-start(bf16[2048,128]{0,1:T(8,128)(2,1)S(1)} %subtract_convert_fusion.3), channel_id=1, source_target_pairs={{0,8},{8,16},{16,24},{24,0},{1,9},{9,17},{17,25},{25,1},{2,10},{10... | collective-permute-start | bytes 1572872 | tf_op jit(solution)/shard_map/ppermute | solution.py:11
  123.5 2.3 %copy-start.12 = (bf16[128,1024]{1,0:T(8,128)(2,1)}, bf16[128,1024]{1,0:T(8,128)(2,1)S(1)}, u32[]{:S(2)}) copy-start(bf16[128,1024]{1,0:T(8,128)(2,1)S(1)} %collective-permute-done.27) | copy-start | bytes 786436
  125.8 11.6 %collective-permute-start.28 = (bf16[2048,128]{0,1:T(8,128)(2,1)}, bf16[2048,128]{0,1:T(8,128)(2,1)}, u32[]{:S(2)}, u32[]{:S(2)}) collective-permute-start(bf16[2048,128]{0,1:T(8,128)(2,1)} %subtract_convert_fusion.4), channel_id=1, source_target_pairs={{0,8},{8,16},{16,24},{24,0},{1,9},{9,17},{17,25},{25,1},{2,10},{10... | collective-permute-start | bytes 1572872 | tf_op jit(solution)/shard_map/ppermute | solution.py:11
  130.0 7.4 %collective-permute-start.30 = (bf16[128,1024]{1,0:T(8,128)(2,1)}, bf16[128,1024]{1,0:T(8,128)(2,1)}, u32[]{:S(2)}, u32[]{:S(2)}) collective-permute-start(bf16[128,1024]{1,0:T(8,128)(2,1)} %convolution_convert_fusion), channel_id=1, source_target_pairs={{0,1},{1,0},{2,3},{3,2},{4,5},{5,4},{6,7},{7,6},{8,9},{9,8},{10,11... | collective-permute-start | bytes 786440 | tf_op jit(solution)/shard_map/ppermute | solution.py:11
  131.0 13.4 %copy-start.9 = (bf16[128,1024]{1,0:T(8,128)(2,1)S(1)}, bf16[128,1024]{1,0:T(8,128)(2,1)}, u32[]{:S(2)}) copy-start(bf16[128,1024]{1,0:T(8,128)(2,1)} %copy-done.8) | copy-start | bytes 786436
  131.0 17.0 %copy-start.3 = (bf16[1024,1024]{1,0:T(8,128)(2,1)S(1)}, bf16[1024,1024]{1,0:T(8,128)(2,1)}, u32[]{:S(2)}) copy-start(bf16[1024,1024]{1,0:T(8,128)(2,1)} %get-tuple-element.13) | copy-start | bytes 6291460
  140.5 6.2 %collective-permute-start.31 = (bf16[32,1024]{1,0:T(8,128)(2,1)S(1)}, bf16[32,1024]{1,0:T(8,128)(2,1)S(1)}, u32[]{:S(2)}, u32[]{:S(2)}) collective-permute-start(bf16[32,1024]{1,0:T(8,128)(2,1)S(1)} %get-tuple-element.18), channel_id=1, source_target_pairs={{0,2},{1,3},{2,4},{3,5},{4,6},{5,7},{6,0},{7,1},{8,10},{9,11},{10,... | collective-permute-start | bytes 196616 | tf_op jit(solution)/shard_map/ppermute | solution.py:11
  141.1 6.7 %collective-permute-start.32 = (bf16[32,1024]{1,0:T(8,128)(2,1)S(1)}, bf16[32,1024]{1,0:T(8,128)(2,1)S(1)}, u32[]{:S(2)}, u32[]{:S(2)}) collective-permute-start(bf16[32,1024]{1,0:T(8,128)(2,1)S(1)} %get-tuple-element.20), channel_id=1, source_target_pairs={{0,4},{1,5},{2,6},{3,7},{4,0},{5,1},{6,2},{7,3},{8,12},{9,13},{10,... | collective-permute-start | bytes 196616 | tf_op jit(solution)/shard_map/ppermute | solution.py:11
  143.4 4.5 %collective-permute-start.33 = (bf16[32,1024]{1,0:T(8,128)(2,1)S(1)}, bf16[32,1024]{1,0:T(8,128)(2,1)S(1)}, u32[]{:S(2)}, u32[]{:S(2)}) collective-permute-start(bf16[32,1024]{1,0:T(8,128)(2,1)S(1)} %get-tuple-element.19), channel_id=1, source_target_pairs={{0,6},{1,7},{2,0},{3,1},{4,2},{5,3},{6,4},{7,5},{8,14},{9,15},{10,... | collective-permute-start | bytes 196616 | tf_op jit(solution)/shard_map/ppermute | solution.py:11
  148.0 10.8 %copy-start.1 = (bf16[2048,1024]{1,0:T(8,128)(2,1)S(1)}, bf16[2048,1024]{1,0:T(8,128)(2,1)}, u32[]{:S(2)}) copy-start(bf16[2048,1024]{1,0:T(8,128)(2,1)} %param.3) | copy-start | bytes 12582916
  149.5 6.1 %collective-permute-start.34 = (bf16[32,1024]{1,0:T(8,128)(2,1)S(1)}, bf16[32,1024]{1,0:T(8,128)(2,1)S(1)}, u32[]{:S(2)}, u32[]{:S(2)}) collective-permute-start(bf16[32,1024]{1,0:T(8,128)(2,1)S(1)} %get-tuple-element.37), channel_id=1, source_target_pairs={{0,2},{1,3},{2,4},{3,5},{4,6},{5,7},{6,0},{7,1},{8,10},{9,11},{10,... | collective-permute-start | bytes 196616 | tf_op jit(solution)/shard_map/ppermute | solution.py:11
  150.9 6.2 %collective-permute-start.35 = (bf16[32,1024]{1,0:T(8,128)(2,1)S(1)}, bf16[32,1024]{1,0:T(8,128)(2,1)S(1)}, u32[]{:S(2)}, u32[]{:S(2)}) collective-permute-start(bf16[32,1024]{1,0:T(8,128)(2,1)S(1)} %get-tuple-element.37), channel_id=1, source_target_pairs={{0,4},{1,5},{2,6},{3,7},{4,0},{5,1},{6,2},{7,3},{8,12},{9,13},{10,... | collective-permute-start | bytes 196616 | tf_op jit(solution)/shard_map/ppermute | solution.py:11
  153.1 4.6 %collective-permute-start.36 = (bf16[32,1024]{1,0:T(8,128)(2,1)S(1)}, bf16[32,1024]{1,0:T(8,128)(2,1)S(1)}, u32[]{:S(2)}, u32[]{:S(2)}) collective-permute-start(bf16[32,1024]{1,0:T(8,128)(2,1)S(1)} %get-tuple-element.37), channel_id=1, source_target_pairs={{0,6},{1,7},{2,0},{3,1},{4,2},{5,3},{6,4},{7,5},{8,14},{9,15},{10,... | collective-permute-start | bytes 196616 | tf_op jit(solution)/shard_map/ppermute | solution.py:11
  157.7 6.4 %collective-permute-start.37 = (bf16[128,1024]{1,0:T(8,128)(2,1)S(1)}, bf16[128,1024]{1,0:T(8,128)(2,1)S(1)}, u32[]{:S(2)}, u32[]{:S(2)}) collective-permute-start(bf16[128,1024]{1,0:T(8,128)(2,1)S(1)} %constant_dynamic-update-slice_fusion.2), channel_id=1, source_target_pairs={{0,1},{1,0},{2,3},{3,2},{4,5},{5,4},{6,7},{7,6},{8,9},{9,8},{10,11... | collective-permute-start | bytes 786440 | tf_op jit(solution)/shard_map/ppermute | solution.py:11
  161.4 4.4 %copy-start.11 = (bf16[128,1024]{1,0:T(8,128)(2,1)S(1)}, bf16[128,1024]{1,0:T(8,128)(2,1)}, u32[]{:S(2)}) copy-start(bf16[128,1024]{1,0:T(8,128)(2,1)} %copy-done.10) | copy-start | bytes 786436
  161.4 4.4 %copy-start.13 = (bf16[128,1024]{1,0:T(8,128)(2,1)S(1)}, bf16[128,1024]{1,0:T(8,128)(2,1)}, u32[]{:S(2)}) copy-start(bf16[128,1024]{1,0:T(8,128)(2,1)} %copy-done.12) | copy-start | bytes 786436
  161.4 8.7 %collective-permute-start.38 = (bf16[2048,128]{0,1:T(8,128)(2,1)S(1)}, bf16[2048,128]{0,1:T(8,128)(2,1)S(1)}, u32[]{:S(2)}, u32[]{:S(2)}) collective-permute-start(bf16[2048,128]{0,1:T(8,128)(2,1)S(1)} %subtract_convert_fusion.2), channel_id=1, source_target_pairs={{0,8},{8,16},{16,24},{24,0},{1,9},{9,17},{17,25},{25,1},{2,10},{10... | collective-permute-start | bytes 1572872 | tf_op jit(solution)/shard_map/ppermute | solution.py:11
  165.7 10.0 %collective-permute-start.39 = (bf16[2048,128]{0,1:T(8,128)(2,1)S(1)}, bf16[2048,128]{0,1:T(8,128)(2,1)S(1)}, u32[]{:S(2)}, u32[]{:S(2)}) collective-permute-start(bf16[2048,128]{0,1:T(8,128)(2,1)S(1)} %subtract_convert_fusion.1), channel_id=1, source_target_pairs={{0,8},{8,16},{16,24},{24,0},{1,9},{9,17},{17,25},{25,1},{2,10},{10... | collective-permute-start | bytes 1572872 | tf_op jit(solution)/shard_map/ppermute | solution.py:11
  165.9 9.8 %copy-start.6 = (bf16[1024,1024]{1,0:T(8,128)(2,1)}, bf16[1024,1024]{1,0:T(8,128)(2,1)S(1)}, u32[]{:S(2)}) copy-start(bf16[1024,1024]{1,0:T(8,128)(2,1)S(1)} %constant_dynamic-update-slice_fusion) | copy-start | bytes 6291460

commit v2 on v1

v2 whole, which is shorter than its diff:
```python
import jax
import jax.numpy as jnp
from jax import lax
from jax.sharding import PartitionSpec as P

BF16 = jnp.bfloat16
F32 = jnp.float32


def split_high_low(value):
    high = lax.reduce_precision(value, 8, 7)
    return high.astype(BF16), (value - high).astype(BF16)


def on_device(features, residual, inverse_grams):
    blocks = lax.axis_size("feat")
    block_id = lax.axis_index("feat")
    shards = lax.axis_size("rows")
    shard_id = lax.axis_index("rows")
    width = residual.shape[1]
    feat_width = features.shape[1]
    inner = 2
    outer = shards // inner
    inner_id = shard_id % inner
    outer_id = shard_id // inner
    half = width // inner
    piece = half // outer
    next_block = [(source, (source + 1) % blocks) for source in range(blocks)]
    partner = [(source, source ^ 1) for source in range(shards)]
    outer_groups = [[o * inner + i for o in range(outer)] for i in range(inner)]
    direct = outer == 4

    def outer_step(step):
        return [(o * inner + i, (o ^ step) * inner + i) for o in range(outer) for i in range(inner)]

    def project(current):
        return lax.dot_general(
            current, features, (((1,), (0,)), ((), ())), preferred_element_type=F32
        )

    def apply_inverse(projected, inverse_high, inverse_low):
        high, low = split_high_low(projected)
        dims = (((1,), (1,)), ((), ()))
        dot = lambda a, b: lax.dot_general(a, b, dims, preferred_element_type=F32)
        both = dot(jnp.concatenate([high, low], 0), inverse_high)
        return (both[: high.shape[0]] + both[high.shape[0]:] + dot(high, inverse_low)).astype(BF16)

    def subtract(current, update):
        change = lax.dot_general(
            update, features, (((1,), (1,)), ((), ())), preferred_element_type=F32
        )
        return current.astype(F32) - change

    def reduce_outer(total):
        if not direct:
            parts = lax.all_to_all(
                total.astype(BF16), "rows", 0, 0, tiled=True, axis_index_groups=outer_groups
            )
            return jnp.sum(parts.reshape(outer, piece, feat_width).astype(F32), axis=0)
        parts = [lax.dynamic_slice_in_dim(total, outer_id * piece, piece, 0)]
        for step in range(outer - 1, 0, -1):
            out = lax.dynamic_slice_in_dim(total, (outer_id ^ step) * piece, piece, 0)
            parts.append(lax.ppermute(out.astype(BF16), "rows", outer_step(step)).astype(F32))
        return sum(parts[1:], parts[0])

    def gather_outer(update):
        if not direct:
            repeated = jnp.concatenate([update] * outer, 0)
            return lax.all_to_all(
                repeated, "rows", 0, 0, tiled=True, axis_index_groups=outer_groups
            )
        full = jnp.zeros((half, feat_width), BF16)
        full = lax.dynamic_update_slice_in_dim(full, update, outer_id * piece, 0)
        for step in range(outer - 1, 0, -1):
            got = lax.ppermute(update, "rows", outer_step(step))
            full = lax.dynamic_update_slice_in_dim(full, got, (outer_id ^ step) * piece, 0)
        return full

    increments = jnp.zeros((width * blocks, feat_width), BF16)
    halves = [
        lax.dynamic_slice_in_dim(residual, s * half, half, 1).T for s in (1 - inner_id, inner_id)
    ]
    lead = 1 - inner_id
    for visit in range(blocks):
        front = (block_id - visit) % blocks
        away, home = halves
        arrived = lax.ppermute(project(away.astype(BF16)).astype(BF16), "rows", partner)
        kept = project(home.astype(BF16))
        if visit == 0:
            inverse_high, inverse_low = split_high_low(inverse_grams)
        arrived, kept = lax.optimization_barrier((arrived, kept))
        total = kept + arrived.astype(F32)
        update_home = gather_outer(apply_inverse(reduce_outer(total), inverse_high, inverse_low))
        update_away = lax.ppermute(update_home, "rows", partner)
        home = subtract(home, update_home)
        away = subtract(away, update_away)
        start = front * width
        increments = lax.dynamic_update_slice_in_dim(
            increments, update_home, start + (1 - lead) * half, 0
        )
        increments = lax.dynamic_update_slice_in_dim(
            increments, update_away, start + lead * half, 0
        )
        halves = [lax.ppermute(part.astype(BF16), "feat", next_block) for part in (home, away)]
        lead = 1 - lead
    first = jnp.where(lead == 0, halves[0], halves[1])
    second = jnp.where(lead == 0, halves[1], halves[0])
    return increments, jnp.concatenate([first, second], 0).astype(F32).T


def solution(mesh):
    placed = (P("rows", "feat"), P("rows", "feat"), P("feat", None))
    return jax.shard_map(
        on_device,
        mesh=mesh,
        in_specs=placed,
        out_specs=(P(None, "feat"), P("rows", "feat")),
        check_vma=False,
    )
```

time: 178 us -> 172 us (0.966)
  waiting for transfers between devices: 84.9 us -> 75.4 us
  starting transfers between devices: 45.2 us -> 47.4 us
    ppermute x40, waiting for transfers between devices: 84.9 us -> 75.4 us  [the longest x8 29.3 us: on_device(): lax.ppermute(part.astype(BF16), 'feat', next_block)]
    ppermute x40, starting transfers between devices: 45.2 us -> 47.4 us  [the longest x12 17.9 us: reduce_outer(): lax.ppermute(out.astype(BF16), 'rows', outer_step(step)).astype(F32)]
  transfers between devices with their start and end apart: 40 -> 40, of which waited for: 37 -> 31; matrix products, arithmetic and copies ran while one was open for 13% -> 17% of each run, Pallas kernels for 0% -> 0%
where the time goes in v2:
time: 172 us
  waiting for transfers between devices  75.4 us (44%)
  starting transfers between devices  47.4 us (28%)
  matrix products  36.9 us (21%)
  local copies, waits for them, and re-layouts  6.04 us (4%)
  other arithmetic  4.69 us (3%)
    ppermute x8, waiting for transfers between devices, on_device(): lax.ppermute(part.astype(BF16), 'feat', next_block)  29.3 us
    ppermute x12, starting transfers between devices, reduce_outer(): lax.ppermute(out.astype(BF16), 'rows', outer_step(step)).astype(F32)  17.9 us
    ppermute x12, starting transfers between devices, gather_outer(): got = lax.ppermute(update, 'rows', outer_step(step))  17.8 us
    dot_general x8, matrix products, subtract(): lax.dot_general(update, features, (((1,), (1,)), ((), ())), preferred_ele...  14.7 us
    dot_general x8, matrix products, project(): lax.dot_general(current, features, (((1,), (0,)), ((), ())), preferred_el...  14.5 us
    ppermute x4, waiting for transfers between devices, on_device(): update_away = lax.ppermute(update_home, 'rows', partner)  13.2 us
    ppermute x12, waiting for transfers between devices, gather_outer(): got = lax.ppermute(update, 'rows', outer_step(step))  12.7 us
    ppermute x12, waiting for transfers between devices, reduce_outer(): lax.ppermute(out.astype(BF16), 'rows', outer_step(step)).astype(F32)  12 us
  transfers between devices with their start and end apart: 40, of which 31 were waited for; matrix products, arithmetic and copies ran while one was open for 17% of the time, Pallas kernels for 0%

profile of v2, /device:TPU:0, one launch (start us, length us, event | category | flops | bytes accessed | tf_op | source)
XLA Modules:
  0.0 171.6 jit_solution(1415696009968044993)
XLA Ops:
  0.7 1.7 constant_dynamic-slice_fusion
  2.7 3.6 %fusion.36 = bf16[128,1024]{1,0:T(8,128)(2,1)} fusion(bf16[2048,1024]{1,0:T(8,128)(2,1)} %param.3, f32[2048,128]{0,1:T(8,128)S(1)} %copy.8), kind=kOutput, calls=%fused_computation.115 | convolution fusion | flops 536870912 | bytes 5505024 | tf_op jit(solution)/shard_map/dot_general | solution.py:37
  6.3 3.0 %collective-permute-start = (bf16[128,1024]{1,0:T(8,128)(2,1)}, bf16[128,1024]{1,0:T(8,128)(2,1)S(1)}, u32[]{:S(2)}, u32[]{:S(2)}) collective-permute-start(bf16[128,1024]{1,0:T(8,128)(2,1)} %fusion.36), channel_id=1, source_target_pairs={{0,1},{1,0},{2,3},{3,2},{4,5},{5,4},{6,7},{7,6},{8,9},{9,8},{10,11... | collective-permute-start | bytes 786440 | tf_op jit(solution)/shard_map/ppermute | solution.py:87
  9.6 3.3 %fusion.34 = f32[128,1024]{1,0:T(8,128)S(1)} fusion(bf16[2048,1024]{1,0:T(8,128)(2,1)} %param.3, f32[2048,128]{0,1:T(8,128)S(1)} %copy.9), kind=kOutput, calls=%fused_computation.113 | convolution fusion | flops 536870912 | bytes 5767168 | tf_op jit(solution)/shard_map/dot_general | solution.py:37
  13.0 2.8 %collective-permute-done = bf16[128,1024]{1,0:T(8,128)(2,1)S(1)} collective-permute-done((bf16[128,1024]{1,0:T(8,128)(2,1)}, bf16[128,1024]{1,0:T(8,128)(2,1)S(1)}, u32[]{:S(2)}, u32[]{:S(2)}) %collective-permute-start) | collective-permute-done | bytes 262176 | tf_op jit(solution)/shard_map/ppermute | solution.py:87
  17.7 3.9 %collective-permute-start.1 = (bf16[32,1024]{1,0:T(8,128)(2,1)S(1)}, bf16[32,1024]{1,0:T(8,128)(2,1)S(1)}, u32[]{:S(2)}, u32[]{:S(2)}) collective-permute-start(bf16[32,1024]{1,0:T(8,128)(2,1)S(1)} %get-tuple-element.43), channel_id=1, source_target_pairs={{0,6},{1,7},{2,4},{3,5},{4,2},{5,3},{6,0},{7,1},{8,14},{9,15},{10,... | collective-permute-start | bytes 196616 | tf_op jit(solution)/shard_map/ppermute | solution.py:63
  22.2 2.3 %reduce-precision_convert_fusion = (bf16[1024,1024]{1,0:T(8,128)(2,1)}, bf16[1024,1024]{1,0:T(8,128)(2,1)S(1)}) fusion(f32[1024,1024]{1,0:T(8,128)S(1)} %copy-done.6), kind=kLoop, calls=%fused_computation.1 | loop fusion | flops 4194304 | bytes 8388608 | tf_op jit(solution)/shard_map/convert_element_type | solution.py:12
  24.5 2.5 %collective-permute-done.2 = bf16[32,1024]{1,0:T(8,128)(2,1)S(1)} collective-permute-done((bf16[32,1024]{1,0:T(8,128)(2,1)S(1)}, bf16[32,1024]{1,0:T(8,128)(2,1)S(1)}, u32[]{:S(2)}, u32[]{:S(2)}) %collective-permute-start.2) | collective-permute-done | bytes 65568 | tf_op jit(solution)/shard_map/ppermute | solution.py:63
  27.9 2.5 %fusion.12 = f32[64,1024]{1,0:T(8,128)S(1)} fusion(bf16[1024,1024]{1,0:T(8,128)(2,1)} %get-tuple-element.20, bf16[32,1024]{1,0:T(8,128)(2,1)S(1)} %get-tuple-element.32, bf16[32,1024]{1,0:T(8,128)(2,1)S(1)} %get-tuple-element.33), kind=kOutput, calls=%fused_computation.51 | convolution fusion | flops 134479872 | bytes 2490368 | tf_op jit(solution)/shard_map/dot_general | solution.py:44
  31.2 2.3 %collective-permute-start.4 = (bf16[32,1024]{1,0:T(8,128)(2,1)S(1)}, bf16[32,1024]{1,0:T(8,128)(2,1)S(1)}, u32[]{:S(2)}, u32[]{:S(2)}) collective-permute-start(bf16[32,1024]{1,0:T(8,128)(2,1)S(1)} %get-tuple-element.47), channel_id=1, source_target_pairs={{0,6},{1,7},{2,4},{3,5},{4,2},{5,3},{6,0},{7,1},{8,14},{9,15},{10,... | collective-permute-start | bytes 196616 | tf_op jit(solution)/shard_map/ppermute | solution.py:75
  33.4 2.2 %collective-permute-start.6 = (bf16[32,1024]{1,0:T(8,128)(2,1)S(1)}, bf16[32,1024]{1,0:T(8,128)(2,1)S(1)}, u32[]{:S(2)}, u32[]{:S(2)}) collective-permute-start(bf16[32,1024]{1,0:T(8,128)(2,1)S(1)} %get-tuple-element.47), channel_id=1, source_target_pairs={{0,2},{1,3},{2,0},{3,1},{4,6},{5,7},{6,4},{7,5},{8,10},{9,11},{10,... | collective-permute-start | bytes 196616 | tf_op jit(solution)/shard_map/ppermute | solution.py:75
  35.6 1.8 %collective-permute-done.4 = bf16[32,1024]{1,0:T(8,128)(2,1)S(1)} collective-permute-done((bf16[32,1024]{1,0:T(8,128)(2,1)S(1)}, bf16[32,1024]{1,0:T(8,128)(2,1)S(1)}, u32[]{:S(2)}, u32[]{:S(2)}) %collective-permute-start.4) | collective-permute-done | bytes 65568 | tf_op jit(solution)/shard_map/ppermute | solution.py:75
  37.4 1.5 collective-permute-done.5
  39.0 1.6 collective-permute-start.7
  40.6 1.5 fusion.1
  42.1 3.3 %collective-permute-done.7 = bf16[128,1024]{1,0:T(8,128)(2,1)S(1)} collective-permute-done((bf16[128,1024]{1,0:T(8,128)(2,1)S(1)}, bf16[128,1024]{1,0:T(8,128)(2,1)S(1)}, u32[]{:S(2)}, u32[]{:S(2)}) %collective-permute-start.7) | collective-permute-done | bytes 262176 | tf_op jit(solution)/shard_map/ppermute | solution.py:94
  45.4 1.5 fusion.2
  47.0 3.7 %collective-permute-done.8 = bf16[128,2048]{1,0:T(8,128)(2,1)S(1)} collective-permute-done((bf16[128,2048]{1,0:T(8,128)(2,1)S(1)}, bf16[128,2048]{1,0:T(8,128)(2,1)S(1)}, u32[]{:S(2)}, u32[]{:S(2)}) %collective-permute-start.8) | collective-permute-done | bytes 524320 | tf_op jit(solution)/shard_map/ppermute | solution.py:104
  52.0 4.3 %collective-permute-done.10 = bf16[128,2048]{1,0:T(8,128)(2,1)S(1)} collective-permute-done((bf16[128,2048]{1,0:T(8,128)(2,1)S(1)}, bf16[128,2048]{1,0:T(8,128)(2,1)S(1)}, u32[]{:S(2)}, u32[]{:S(2)}) %collective-permute-start.10) | collective-permute-done | bytes 524320 | tf_op jit(solution)/shard_map/ppermute | solution.py:104
  57.1 1.8 %collective-permute-done.9 = bf16[128,1024]{1,0:T(8,128)(2,1)S(1)} collective-permute-done((bf16[128,1024]{1,0:T(8,128)(2,1)S(1)}, bf16[128,1024]{1,0:T(8,128)(2,1)S(1)}, u32[]{:S(2)}, u32[]{:S(2)}) %collective-permute-start.9) | collective-permute-done | bytes 262176 | tf_op jit(solution)/shard_map/ppermute | solution.py:87
  59.0 2.1 %collective-permute-start.11 = (bf16[32,1024]{1,0:T(8,128)(2,1)S(1)}, bf16[32,1024]{1,0:T(8,128)(2,1)S(1)}, u32[]{:S(2)}, u32[]{:S(2)}) collective-permute-start(bf16[32,1024]{1,0:T(8,128)(2,1)S(1)} %get-tuple-element.40), channel_id=1, source_target_pairs={{0,6},{1,7},{2,4},{3,5},{4,2},{5,3},{6,0},{7,1},{8,14},{9,15},{10,... | collective-permute-start | bytes 196616 | tf_op jit(solution)/shard_map/ppermute | solution.py:63
  61.4 2.0 %collective-permute-start.13 = (bf16[32,1024]{1,0:T(8,128)(2,1)S(1)}, bf16[32,1024]{1,0:T(8,128)(2,1)S(1)}, u32[]{:S(2)}, u32[]{:S(2)}) collective-permute-start(bf16[32,1024]{1,0:T(8,128)(2,1)S(1)} %get-tuple-element.41), channel_id=1, source_target_pairs={{0,2},{1,3},{2,0},{3,1},{4,6},{5,7},{6,4},{7,5},{8,10},{9,11},{10,... | collective-permute-start | bytes 196616 | tf_op jit(solution)/shard_map/ppermute | solution.py:63
  63.4 1.7 %collective-permute-done.11 = bf16[32,1024]{1,0:T(8,128)(2,1)S(1)} collective-permute-done((bf16[32,1024]{1,0:T(8,128)(2,1)S(1)}, bf16[32,1024]{1,0:T(8,128)(2,1)S(1)}, u32[]{:S(2)}, u32[]{:S(2)}) %collective-permute-start.11) | collective-permute-done | bytes 65568 | tf_op jit(solution)/shard_map/ppermute | solution.py:63
  68.2 2.1 %collective-permute-start.14 = (bf16[32,1024]{1,0:T(8,128)(2,1)S(1)}, bf16[32,1024]{1,0:T(8,128)(2,1)S(1)}, u32[]{:S(2)}, u32[]{:S(2)}) collective-permute-start(bf16[32,1024]{1,0:T(8,128)(2,1)S(1)} %get-tuple-element.49), channel_id=1, source_target_pairs={{0,6},{1,7},{2,4},{3,5},{4,2},{5,3},{6,0},{7,1},{8,14},{9,15},{10,... | collective-permute-start | bytes 196616 | tf_op jit(solution)/shard_map/ppermute | solution.py:75
  70.8 1.8 %collective-permute-start.16 = (bf16[32,1024]{1,0:T(8,128)(2,1)S(1)}, bf16[32,1024]{1,0:T(8,128)(2,1)S(1)}, u32[]{:S(2)}, u32[]{:S(2)}) collective-permute-start(bf16[32,1024]{1,0:T(8,128)(2,1)S(1)} %get-tuple-element.49), channel_id=1, source_target_pairs={{0,2},{1,3},{2,0},{3,1},{4,6},{5,7},{6,4},{7,5},{8,10},{9,11},{10,... | collective-permute-start | bytes 196616 | tf_op jit(solution)/shard_map/ppermute | solution.py:75
  72.6 1.7 collective-permute-done.14
  74.3 1.5 collective-permute-done.15
  76.4 1.5 subtract_convert_fusion.5
  78.1 4.1 %collective-permute-done.17 = bf16[128,1024]{1,0:T(8,128)(2,1)S(1)} collective-permute-done((bf16[128,1024]{1,0:T(8,128)(2,1)S(1)}, bf16[128,1024]{1,0:T(8,128)(2,1)S(1)}, u32[]{:S(2)}, u32[]{:S(2)}) %collective-permute-start.17) | collective-permute-done | bytes 262176 | tf_op jit(solution)/shard_map/ppermute | solution.py:94
  82.2 1.5 subtract_convert_fusion.4
  83.8 2.9 %collective-permute-done.18 = bf16[128,2048]{1,0:T(8,128)(2,1)S(1)} collective-permute-done((bf16[128,2048]{1,0:T(8,128)(2,1)S(1)}, bf16[128,2048]{1,0:T(8,128)(2,1)S(1)}, u32[]{:S(2)}, u32[]{:S(2)}) %collective-permute-start.18) | collective-permute-done | bytes 524320 | tf_op jit(solution)/shard_map/ppermute | solution.py:104
  87.4 1.6 collective-permute-start.19
  89.0 3.4 %collective-permute-done.20 = bf16[128,2048]{1,0:T(8,128)(2,1)S(1)} collective-permute-done((bf16[128,2048]{1,0:T(8,128)(2,1)S(1)}, bf16[128,2048]{1,0:T(8,128)(2,1)S(1)}, u32[]{:S(2)}, u32[]{:S(2)}) %collective-permute-start.20) | collective-permute-done | bytes 524320 | tf_op jit(solution)/shard_map/ppermute | solution.py:104
  94.0 2.1 %collective-permute-start.21 = (bf16[32,1024]{1,0:T(8,128)(2,1)S(1)}, bf16[32,1024]{1,0:T(8,128)(2,1)S(1)}, u32[]{:S(2)}, u32[]{:S(2)}) collective-permute-start(bf16[32,1024]{1,0:T(8,128)(2,1)S(1)} %get-tuple-element.37), channel_id=1, source_target_pairs={{0,6},{1,7},{2,4},{3,5},{4,2},{5,3},{6,0},{7,1},{8,14},{9,15},{10,... | collective-permute-start | bytes 196616 | tf_op jit(solution)/shard_map/ppermute | solution.py:63
  96.6 1.8 %collective-permute-start.23 = (bf16[32,1024]{1,0:T(8,128)(2,1)S(1)}, bf16[32,1024]{1,0:T(8,128)(2,1)S(1)}, u32[]{:S(2)}, u32[]{:S(2)}) collective-permute-start(bf16[32,1024]{1,0:T(8,128)(2,1)S(1)} %get-tuple-element.38), channel_id=1, source_target_pairs={{0,2},{1,3},{2,0},{3,1},{4,6},{5,7},{6,4},{7,5},{8,10},{9,11},{10,... | collective-permute-start | bytes 196616 | tf_op jit(solution)/shard_map/ppermute | solution.py:63
  98.5 1.7 collective-permute-done.21
  100.1 1.5 collective-permute-done.22
  103.2 2.1 %collective-permute-start.24 = (bf16[32,1024]{1,0:T(8,128)(2,1)S(1)}, bf16[32,1024]{1,0:T(8,128)(2,1)S(1)}, u32[]{:S(2)}, u32[]{:S(2)}) collective-permute-start(bf16[32,1024]{1,0:T(8,128)(2,1)S(1)} %get-tuple-element.51), channel_id=1, source_target_pairs={{0,6},{1,7},{2,4},{3,5},{4,2},{5,3},{6,0},{7,1},{8,14},{9,15},{10,... | collective-permute-start | bytes 196616 | tf_op jit(solution)/shard_map/ppermute | solution.py:75
  105.8 1.8 %collective-permute-start.26 = (bf16[32,1024]{1,0:T(8,128)(2,1)S(1)}, bf16[32,1024]{1,0:T(8,128)(2,1)S(1)}, u32[]{:S(2)}, u32[]{:S(2)}) collective-permute-start(bf16[32,1024]{1,0:T(8,128)(2,1)S(1)} %get-tuple-element.51), channel_id=1, source_target_pairs={{0,2},{1,3},{2,0},{3,1},{4,6},{5,7},{6,4},{7,5},{8,10},{9,11},{10,... | collective-permute-start | bytes 196616 | tf_op jit(solution)/shard_map/ppermute | solution.py:75
  107.6 1.7 collective-permute-done.24
  109.3 1.5 collective-permute-done.25
  110.8 1.6 collective-permute-start.27
  112.4 2.3 %subtract_convert_fusion.3 = bf16[128,2048]{1,0:T(8,128)(2,1)} fusion(bf16[128,2048]{1,0:T(8,128)(2,1)S(1)} %collective-permute-done.20, bf16[128,1024]{1,0:T(8,128)(2,1)S(1)} %constant_dynamic-update-slice_fusion.8, bf16[2048,1024]{1,0:T(8,128)(2,1)S(1)} %copy-done), kind=kOutput, calls=%fused_computation.25 | convolution fusion | flops 537657344 | bytes 5505024 | tf_op jit(solution)/shard_map/dot_general | solution.py:49
  114.7 2.6 %collective-permute-done.27 = bf16[128,1024]{1,0:T(8,128)(2,1)S(1)} collective-permute-done((bf16[128,1024]{1,0:T(8,128)(2,1)S(1)}, bf16[128,1024]{1,0:T(8,128)(2,1)S(1)}, u32[]{:S(2)}, u32[]{:S(2)}) %collective-permute-start.27) | collective-permute-done | bytes 262176 | tf_op jit(solution)/shard_map/ppermute | solution.py:94
  117.3 2.3 %subtract_convert_fusion.2 = bf16[128,2048]{1,0:T(8,128)(2,1)} fusion(bf16[128,2048]{1,0:T(8,128)(2,1)S(1)} %collective-permute-done.18, bf16[128,1024]{1,0:T(8,128)(2,1)S(1)} %collective-permute-done.27, bf16[2048,1024]{1,0:T(8,128)(2,1)S(1)} %copy-done), kind=kOutput, calls=%fused_computation.24 | convolution fusion | flops 537657344 | bytes 5505024 | tf_op jit(solution)/shard_map/dot_general | solution.py:49
  119.9 3.6 %collective-permute-done.28 = bf16[128,2048]{1,0:T(8,128)(2,1)S(1)} collective-permute-done((bf16[128,2048]{1,0:T(8,128)(2,1)}, bf16[128,2048]{1,0:T(8,128)(2,1)S(1)}, u32[]{:S(2)}, u32[]{:S(2)}) %collective-permute-start.28) | collective-permute-done | bytes 524320 | tf_op jit(solution)/shard_map/ppermute | solution.py:104
  123.5 2.9 %convolution_convert_fusion = bf16[128,1024]{1,0:T(8,128)(2,1)S(1)} fusion(bf16[128,2048]{1,0:T(8,128)(2,1)S(1)} %collective-permute-done.28, bf16[2048,1024]{1,0:T(8,128)(2,1)} %param.3), kind=kOutput, calls=%fused_computation.8 | convolution fusion | flops 537001984 | bytes 4980736 | tf_op jit(solution)/shard_map/dot_general | solution.py:37
  127.0 2.2 %collective-permute-done.30 = bf16[128,2048]{1,0:T(8,128)(2,1)} collective-permute-done((bf16[128,2048]{1,0:T(8,128)(2,1)}, bf16[128,2048]{1,0:T(8,128)(2,1)}, u32[]{:S(2)}, u32[]{:S(2)}) %collective-permute-start.30) | collective-permute-done | bytes 524320 | tf_op jit(solution)/shard_map/ppermute | solution.py:104
  129.2 1.8 %fusion.42 = f32[128,1024]{1,0:T(8,128)S(1)} fusion(bf16[128,2048]{1,0:T(8,128)(2,1)} %collective-permute-done.30, bf16[2048,1024]{1,0:T(8,128)(2,1)S(1)} %copy-done.1), kind=kOutput, calls=%fused_computation.119 | convolution fusion | flops 536870912 | bytes 5242880 | tf_op jit(solution)/shard_map/dot_general | solution.py:37
  131.0 2.9 %collective-permute-done.29 = bf16[128,1024]{1,0:T(8,128)(2,1)S(1)} collective-permute-done((bf16[128,1024]{1,0:T(8,128)(2,1)S(1)}, bf16[128,1024]{1,0:T(8,128)(2,1)S(1)}, u32[]{:S(2)}, u32[]{:S(2)}) %collective-permute-start.29) | collective-permute-done | bytes 262176 | tf_op jit(solution)/shard_map/ppermute | solution.py:87
  134.0 2.1 %collective-permute-start.31 = (bf16[32,1024]{1,0:T(8,128)(2,1)S(1)}, bf16[32,1024]{1,0:T(8,128)(2,1)S(1)}, u32[]{:S(2)}, u32[]{:S(2)}) collective-permute-start(bf16[32,1024]{1,0:T(8,128)(2,1)S(1)} %get-tuple-element.34), channel_id=1, source_target_pairs={{0,6},{1,7},{2,4},{3,5},{4,2},{5,3},{6,0},{7,1},{8,14},{9,15},{10,... | collective-permute-start | bytes 196616 | tf_op jit(solution)/shard_map/ppermute | solution.py:63
  136.6 1.9 %collective-permute-start.33 = (bf16[32,1024]{1,0:T(8,128)(2,1)S(1)}, bf16[32,1024]{1,0:T(8,128)(2,1)S(1)}, u32[]{:S(2)}, u32[]{:S(2)}) collective-permute-start(bf16[32,1024]{1,0:T(8,128)(2,1)S(1)} %get-tuple-element.35), channel_id=1, source_target_pairs={{0,2},{1,3},{2,0},{3,1},{4,6},{5,7},{6,4},{7,5},{8,10},{9,11},{10,... | collective-permute-start | bytes 196616 | tf_op jit(solution)/shard_map/ppermute | solution.py:63
  138.5 1.8 %collective-permute-done.31 = bf16[32,1024]{1,0:T(8,128)(2,1)S(1)} collective-permute-done((bf16[32,1024]{1,0:T(8,128)(2,1)S(1)}, bf16[32,1024]{1,0:T(8,128)(2,1)S(1)}, u32[]{:S(2)}, u32[]{:S(2)}) %collective-permute-start.31) | collective-permute-done | bytes 65568 | tf_op jit(solution)/shard_map/ppermute | solution.py:63
  143.3 2.1 %collective-permute-start.34 = (bf16[32,1024]{1,0:T(8,128)(2,1)S(1)}, bf16[32,1024]{1,0:T(8,128)(2,1)S(1)}, u32[]{:S(2)}, u32[]{:S(2)}) collective-permute-start(bf16[32,1024]{1,0:T(8,128)(2,1)S(1)} %get-tuple-element.53), channel_id=1, source_target_pairs={{0,6},{1,7},{2,4},{3,5},{4,2},{5,3},{6,0},{7,1},{8,14},{9,15},{10,... | collective-permute-start | bytes 196616 | tf_op jit(solution)/shard_map/ppermute | solution.py:75
  145.9 1.9 %collective-permute-start.36 = (bf16[32,1024]{1,0:T(8,128)(2,1)S(1)}, bf16[32,1024]{1,0:T(8,128)(2,1)S(1)}, u32[]{:S(2)}, u32[]{:S(2)}) collective-permute-start(bf16[32,1024]{1,0:T(8,128)(2,1)S(1)} %get-tuple-element.53), channel_id=1, source_target_pairs={{0,2},{1,3},{2,0},{3,1},{4,6},{5,7},{6,4},{7,5},{8,10},{9,11},{10,... | collective-permute-start | bytes 196616 | tf_op jit(solution)/shard_map/ppermute | solution.py:75
  147.8 1.6 collective-permute-done.34
  149.4 1.5 collective-permute-done.35
  150.9 1.7 collective-permute-start.37
  152.6 2.6 %subtract_convert_fusion.1 = bf16[128,2048]{1,0:T(8,128)(2,1)S(1)} fusion(bf16[128,2048]{1,0:T(8,128)(2,1)} %collective-permute-done.30, bf16[128,1024]{1,0:T(8,128)(2,1)S(1)} %constant_dynamic-update-slice_fusion.2, bf16[2048,1024]{1,0:T(8,128)(2,1)S(1)} %copy-done.1), kind=kOutput, calls=%fused_computation.23 | convolution fusion | flops 537657344 | bytes 5505024 | tf_op jit(solution)/shard_map/dot_general | solution.py:49
  155.3 3.3 %collective-permute-done.37 = bf16[128,1024]{1,0:T(8,128)(2,1)S(1)} collective-permute-done((bf16[128,1024]{1,0:T(8,128)(2,1)S(1)}, bf16[128,1024]{1,0:T(8,128)(2,1)S(1)}, u32[]{:S(2)}, u32[]{:S(2)}) %collective-permute-start.37) | collective-permute-done | bytes 262176 | tf_op jit(solution)/shard_map/ppermute | solution.py:94
  158.6 1.5 subtract_convert_fusion
  160.3 3.5 %collective-permute-done.38 = bf16[128,2048]{1,0:T(8,128)(2,1)S(1)} collective-permute-done((bf16[128,2048]{1,0:T(8,128)(2,1)S(1)}, bf16[128,2048]{1,0:T(8,128)(2,1)S(1)}, u32[]{:S(2)}, u32[]{:S(2)}) %collective-permute-start.38) | collective-permute-done | bytes 524320 | tf_op jit(solution)/shard_map/ppermute | solution.py:104
  163.9 5.6 %collective-permute-done.39 = bf16[128,2048]{1,0:T(8,128)(2,1)S(1)} collective-permute-done((bf16[128,2048]{1,0:T(8,128)(2,1)S(1)}, bf16[128,2048]{1,0:T(8,128)(2,1)S(1)}, u32[]{:S(2)}, u32[]{:S(2)}) %collective-permute-start.39) | collective-permute-done | bytes 524320 | tf_op jit(solution)/shard_map/ppermute | solution.py:104
  169.8 1.8 %copy.7 = f32[2048,256]{1,0:T(8,128)} copy(f32[2048,256]{0,1:T(8,128)S(1)} %convert_bitcast_fusion) | data formatting | bytes 4194304
  (112 shorter events, 22.6 us)
Async XLA Ops:
  6.3 9.5 %collective-permute-start = (bf16[128,1024]{1,0:T(8,128)(2,1)}, bf16[128,1024]{1,0:T(8,128)(2,1)S(1)}, u32[]{:S(2)}, u32[]{:S(2)}) collective-permute-start(bf16[128,1024]{1,0:T(8,128)(2,1)} %fusion.36), channel_id=1, source_target_pairs={{0,1},{1,0},{2,3},{3,2},{4,5},{5,4},{6,7},{7,6},{8,9},{9,8},{10,11... | collective-permute-start | bytes 786440 | tf_op jit(solution)/shard_map/ppermute | solution.py:87
  9.6 3.4 %copy-start.4 = (f32[2048,128]{0,1:T(8,128)}, f32[2048,128]{0,1:T(8,128)S(1)}, u32[]{:S(2)}) copy-start(f32[2048,128]{0,1:T(8,128)S(1)} %copy.9) | copy-start | bytes 3145732
  9.6 12.6 %copy-start.6 = (f32[1024,1024]{1,0:T(8,128)S(1)}, f32[1024,1024]{1,0:T(8,128)}, u32[]{:S(2)}) copy-start(f32[1024,1024]{1,0:T(8,128)} %param.5) | copy-start | bytes 12582916
  17.7 6.8 %collective-permute-start.1 = (bf16[32,1024]{1,0:T(8,128)(2,1)S(1)}, bf16[32,1024]{1,0:T(8,128)(2,1)S(1)}, u32[]{:S(2)}, u32[]{:S(2)}) collective-permute-start(bf16[32,1024]{1,0:T(8,128)(2,1)S(1)} %get-tuple-element.43), channel_id=1, source_target_pairs={{0,6},{1,7},{2,4},{3,5},{4,2},{5,3},{6,0},{7,1},{8,14},{9,15},{10,... | collective-permute-start | bytes 196616 | tf_op jit(solution)/shard_map/ppermute | solution.py:63
  21.6 5.4 %collective-permute-start.2 = (bf16[32,1024]{1,0:T(8,128)(2,1)S(1)}, bf16[32,1024]{1,0:T(8,128)(2,1)S(1)}, u32[]{:S(2)}, u32[]{:S(2)}) collective-permute-start(bf16[32,1024]{1,0:T(8,128)(2,1)S(1)} %get-tuple-element.45), channel_id=1, source_target_pairs={{0,4},{1,5},{2,6},{3,7},{4,0},{5,1},{6,2},{7,3},{8,12},{9,13},{10,... | collective-permute-start | bytes 196616 | tf_op jit(solution)/shard_map/ppermute | solution.py:63
  21.6 5.4 %collective-permute-start.3 = (bf16[32,1024]{1,0:T(8,128)(2,1)S(1)}, bf16[32,1024]{1,0:T(8,128)(2,1)S(1)}, u32[]{:S(2)}, u32[]{:S(2)}) collective-permute-start(bf16[32,1024]{1,0:T(8,128)(2,1)S(1)} %get-tuple-element.44), channel_id=1, source_target_pairs={{0,2},{1,3},{2,0},{3,1},{4,6},{5,7},{6,4},{7,5},{8,10},{9,11},{10,... | collective-permute-start | bytes 196616 | tf_op jit(solution)/shard_map/ppermute | solution.py:63
  27.9 12.6 %copy-start = (bf16[2048,1024]{1,0:T(8,128)(2,1)S(1)}, bf16[2048,1024]{1,0:T(8,128)(2,1)}, u32[]{:S(2)}) copy-start(bf16[2048,1024]{1,0:T(8,128)(2,1)} %param.3) | copy-start | bytes 12582916
  30.4 10.1 %copy-start.5 = (f32[2048,128]{0,1:T(8,128)S(1)}, f32[2048,128]{0,1:T(8,128)}, u32[]{:S(2)}) copy-start(f32[2048,128]{0,1:T(8,128)} %copy-done.4) | copy-start | bytes 3145732
  31.2 6.2 %collective-permute-start.4 = (bf16[32,1024]{1,0:T(8,128)(2,1)S(1)}, bf16[32,1024]{1,0:T(8,128)(2,1)S(1)}, u32[]{:S(2)}, u32[]{:S(2)}) collective-permute-start(bf16[32,1024]{1,0:T(8,128)(2,1)S(1)} %get-tuple-element.47), channel_id=1, source_target_pairs={{0,6},{1,7},{2,4},{3,5},{4,2},{5,3},{6,0},{7,1},{8,14},{9,15},{10,... | collective-permute-start | bytes 196616 | tf_op jit(solution)/shard_map/ppermute | solution.py:75
  33.4 5.5 %collective-permute-start.5 = (bf16[32,1024]{1,0:T(8,128)(2,1)S(1)}, bf16[32,1024]{1,0:T(8,128)(2,1)S(1)}, u32[]{:S(2)}, u32[]{:S(2)}) collective-permute-start(bf16[32,1024]{1,0:T(8,128)(2,1)S(1)} %get-tuple-element.47), channel_id=1, source_target_pairs={{0,4},{1,5},{2,6},{3,7},{4,0},{5,1},{6,2},{7,3},{8,12},{9,13},{10,... | collective-permute-start | bytes 196616 | tf_op jit(solution)/shard_map/ppermute | solution.py:75
  33.4 5.5 %collective-permute-start.6 = (bf16[32,1024]{1,0:T(8,128)(2,1)S(1)}, bf16[32,1024]{1,0:T(8,128)(2,1)S(1)}, u32[]{:S(2)}, u32[]{:S(2)}) collective-permute-start(bf16[32,1024]{1,0:T(8,128)(2,1)S(1)} %get-tuple-element.47), channel_id=1, source_target_pairs={{0,2},{1,3},{2,0},{3,1},{4,6},{5,7},{6,4},{7,5},{8,10},{9,11},{10,... | collective-permute-start | bytes 196616 | tf_op jit(solution)/shard_map/ppermute | solution.py:75
  39.0 6.4 %collective-permute-start.7 = (bf16[128,1024]{1,0:T(8,128)(2,1)S(1)}, bf16[128,1024]{1,0:T(8,128)(2,1)S(1)}, u32[]{:S(2)}, u32[]{:S(2)}) collective-permute-start(bf16[128,1024]{1,0:T(8,128)(2,1)S(1)} %constant_dynamic-update-slice_fusion.20), channel_id=1, source_target_pairs={{0,1},{1,0},{2,3},{3,2},{4,5},{5,4},{6,7},{7,6},{8,9},{9,8},{10,11... | collective-permute-start | bytes 786440 | tf_op jit(solution)/shard_map/ppermute | solution.py:94
  42.1 8.7 %collective-permute-start.8 = (bf16[128,2048]{1,0:T(8,128)(2,1)S(1)}, bf16[128,2048]{1,0:T(8,128)(2,1)S(1)}, u32[]{:S(2)}, u32[]{:S(2)}) collective-permute-start(bf16[128,2048]{1,0:T(8,128)(2,1)S(1)} %fusion.1), channel_id=1, source_target_pairs={{0,8},{8,16},{16,24},{24,0},{1,9},{9,17},{17,25},{25,1},{2,10},{10... | collective-permute-start | bytes 1572872 | tf_op jit(solution)/shard_map/ppermute | solution.py:104
  45.4 1.5 copy-start.8
  46.9 9.4 %collective-permute-start.10 = (bf16[128,2048]{1,0:T(8,128)(2,1)S(1)}, bf16[128,2048]{1,0:T(8,128)(2,1)S(1)}, u32[]{:S(2)}, u32[]{:S(2)}) collective-permute-start(bf16[128,2048]{1,0:T(8,128)(2,1)S(1)} %fusion.2), channel_id=1, source_target_pairs={{0,8},{8,16},{16,24},{24,0},{1,9},{9,17},{17,25},{25,1},{2,10},{10... | collective-permute-start | bytes 1572872 | tf_op jit(solution)/shard_map/ppermute | solution.py:104
  51.5 7.4 %collective-permute-start.9 = (bf16[128,1024]{1,0:T(8,128)(2,1)S(1)}, bf16[128,1024]{1,0:T(8,128)(2,1)S(1)}, u32[]{:S(2)}, u32[]{:S(2)}) collective-permute-start(bf16[128,1024]{1,0:T(8,128)(2,1)S(1)} %convolution_convert_fusion.2), channel_id=1, source_target_pairs={{0,1},{1,0},{2,3},{3,2},{4,5},{5,4},{6,7},{7,6},{8,9},{9,8},{10,11... | collective-permute-start | bytes 786440 | tf_op jit(solution)/shard_map/ppermute | solution.py:87
  57.1 9.5 %copy-start.2 = (bf16[1024,1024]{1,0:T(8,128)(2,1)S(1)}, bf16[1024,1024]{1,0:T(8,128)(2,1)}, u32[]{:S(2)}) copy-start(bf16[1024,1024]{1,0:T(8,128)(2,1)} %get-tuple-element.20) | copy-start | bytes 6291460
  59.0 6.2 %collective-permute-start.11 = (bf16[32,1024]{1,0:T(8,128)(2,1)S(1)}, bf16[32,1024]{1,0:T(8,128)(2,1)S(1)}, u32[]{:S(2)}, u32[]{:S(2)}) collective-permute-start(bf16[32,1024]{1,0:T(8,128)(2,1)S(1)} %get-tuple-element.40), channel_id=1, source_target_pairs={{0,6},{1,7},{2,4},{3,5},{4,2},{5,3},{6,0},{7,1},{8,14},{9,15},{10,... | collective-permute-start | bytes 196616 | tf_op jit(solution)/shard_map/ppermute | solution.py:63
  61.1 5.5 %collective-permute-start.12 = (bf16[32,1024]{1,0:T(8,128)(2,1)S(1)}, bf16[32,1024]{1,0:T(8,128)(2,1)S(1)}, u32[]{:S(2)}, u32[]{:S(2)}) collective-permute-start(bf16[32,1024]{1,0:T(8,128)(2,1)S(1)} %get-tuple-element.42), channel_id=1, source_target_pairs={{0,4},{1,5},{2,6},{3,7},{4,0},{5,1},{6,2},{7,3},{8,12},{9,13},{10,... | collective-permute-start | bytes 196616 | tf_op jit(solution)/shard_map/ppermute | solution.py:63
  61.4 5.2 %collective-permute-start.13 = (bf16[32,1024]{1,0:T(8,128)(2,1)S(1)}, bf16[32,1024]{1,0:T(8,128)(2,1)S(1)}, u32[]{:S(2)}, u32[]{:S(2)}) collective-permute-start(bf16[32,1024]{1,0:T(8,128)(2,1)S(1)} %get-tuple-element.41), channel_id=1, source_target_pairs={{0,2},{1,3},{2,0},{3,1},{4,6},{5,7},{6,4},{7,5},{8,10},{9,11},{10,... | collective-permute-start | bytes 196616 | tf_op jit(solution)/shard_map/ppermute | solution.py:63
  68.2 6.1 %collective-permute-start.14 = (bf16[32,1024]{1,0:T(8,128)(2,1)S(1)}, bf16[32,1024]{1,0:T(8,128)(2,1)S(1)}, u32[]{:S(2)}, u32[]{:S(2)}) collective-permute-start(bf16[32,1024]{1,0:T(8,128)(2,1)S(1)} %get-tuple-element.49), channel_id=1, source_target_pairs={{0,6},{1,7},{2,4},{3,5},{4,2},{5,3},{6,0},{7,1},{8,14},{9,15},{10,... | collective-permute-start | bytes 196616 | tf_op jit(solution)/shard_map/ppermute | solution.py:75
  70.2 5.5 %collective-permute-start.15 = (bf16[32,1024]{1,0:T(8,128)(2,1)S(1)}, bf16[32,1024]{1,0:T(8,128)(2,1)S(1)}, u32[]{:S(2)}, u32[]{:S(2)}) collective-permute-start(bf16[32,1024]{1,0:T(8,128)(2,1)S(1)} %get-tuple-element.49), channel_id=1, source_target_pairs={{0,4},{1,5},{2,6},{3,7},{4,0},{5,1},{6,2},{7,3},{8,12},{9,13},{10,... | collective-permute-start | bytes 196616 | tf_op jit(solution)/shard_map/ppermute | solution.py:75
  70.8 5.0 %collective-permute-start.16 = (bf16[32,1024]{1,0:T(8,128)(2,1)S(1)}, bf16[32,1024]{1,0:T(8,128)(2,1)S(1)}, u32[]{:S(2)}, u32[]{:S(2)}) collective-permute-start(bf16[32,1024]{1,0:T(8,128)(2,1)S(1)} %get-tuple-element.49), channel_id=1, source_target_pairs={{0,2},{1,3},{2,0},{3,1},{4,6},{5,7},{6,4},{7,5},{8,10},{9,11},{10,... | collective-permute-start | bytes 196616 | tf_op jit(solution)/shard_map/ppermute | solution.py:75
  75.8 6.4 %collective-permute-start.17 = (bf16[128,1024]{1,0:T(8,128)(2,1)S(1)}, bf16[128,1024]{1,0:T(8,128)(2,1)S(1)}, u32[]{:S(2)}, u32[]{:S(2)}) collective-permute-start(bf16[128,1024]{1,0:T(8,128)(2,1)S(1)} %constant_dynamic-update-slice_fusion.14), channel_id=1, source_target_pairs={{0,1},{1,0},{2,3},{3,2},{4,5},{5,4},{6,7},{7,6},{8,9},{9,8},{10,11... | collective-permute-start | bytes 786440 | tf_op jit(solution)/shard_map/ppermute | solution.py:94
  77.9 8.8 %collective-permute-start.18 = (bf16[128,2048]{1,0:T(8,128)(2,1)S(1)}, bf16[128,2048]{1,0:T(8,128)(2,1)S(1)}, u32[]{:S(2)}, u32[]{:S(2)}) collective-permute-start(bf16[128,2048]{1,0:T(8,128)(2,1)S(1)} %subtract_convert_fusion.5), channel_id=1, source_target_pairs={{0,8},{8,16},{16,24},{24,0},{1,9},{9,17},{17,25},{25,1},{2,10},{10... | collective-permute-start | bytes 1572872 | tf_op jit(solution)/shard_map/ppermute | solution.py:104
  82.2 1.5 copy-start.10
  83.7 8.7 %collective-permute-start.20 = (bf16[128,2048]{1,0:T(8,128)(2,1)S(1)}, bf16[128,2048]{1,0:T(8,128)(2,1)S(1)}, u32[]{:S(2)}, u32[]{:S(2)}) collective-permute-start(bf16[128,2048]{1,0:T(8,128)(2,1)S(1)} %subtract_convert_fusion.4), channel_id=1, source_target_pairs={{0,8},{8,16},{16,24},{24,0},{1,9},{9,17},{17,25},{25,1},{2,10},{10... | collective-permute-start | bytes 1572872 | tf_op jit(solution)/shard_map/ppermute | solution.py:104
  87.4 6.4 %collective-permute-start.19 = (bf16[128,1024]{1,0:T(8,128)(2,1)S(1)}, bf16[128,1024]{1,0:T(8,128)(2,1)S(1)}, u32[]{:S(2)}, u32[]{:S(2)}) collective-permute-start(bf16[128,1024]{1,0:T(8,128)(2,1)S(1)} %convolution_convert_fusion.1), channel_id=1, source_target_pairs={{0,1},{1,0},{2,3},{3,2},{4,5},{5,4},{6,7},{7,6},{8,9},{9,8},{10,11... | collective-permute-start | bytes 786440 | tf_op jit(solution)/shard_map/ppermute | solution.py:87
  94.0 6.1 %collective-permute-start.21 = (bf16[32,1024]{1,0:T(8,128)(2,1)S(1)}, bf16[32,1024]{1,0:T(8,128)(2,1)S(1)}, u32[]{:S(2)}, u32[]{:S(2)}) collective-permute-start(bf16[32,1024]{1,0:T(8,128)(2,1)S(1)} %get-tuple-element.37), channel_id=1, source_target_pairs={{0,6},{1,7},{2,4},{3,5},{4,2},{5,3},{6,0},{7,1},{8,14},{9,15},{10,... | collective-permute-start | bytes 196616 | tf_op jit(solution)/shard_map/ppermute | solution.py:63
  96.1 5.5 %collective-permute-start.22 = (bf16[32,1024]{1,0:T(8,128)(2,1)S(1)}, bf16[32,1024]{1,0:T(8,128)(2,1)S(1)}, u32[]{:S(2)}, u32[]{:S(2)}) collective-permute-start(bf16[32,1024]{1,0:T(8,128)(2,1)S(1)} %get-tuple-element.39), channel_id=1, source_target_pairs={{0,4},{1,5},{2,6},{3,7},{4,0},{5,1},{6,2},{7,3},{8,12},{9,13},{10,... | collective-permute-start | bytes 196616 | tf_op jit(solution)/shard_map/ppermute | solution.py:63
  96.6 5.0 %collective-permute-start.23 = (bf16[32,1024]{1,0:T(8,128)(2,1)S(1)}, bf16[32,1024]{1,0:T(8,128)(2,1)S(1)}, u32[]{:S(2)}, u32[]{:S(2)}) collective-permute-start(bf16[32,1024]{1,0:T(8,128)(2,1)S(1)} %get-tuple-element.38), channel_id=1, source_target_pairs={{0,2},{1,3},{2,0},{3,1},{4,6},{5,7},{6,4},{7,5},{8,10},{9,11},{10,... | collective-permute-start | bytes 196616 | tf_op jit(solution)/shard_map/ppermute | solution.py:63
  103.2 6.1 %collective-permute-start.24 = (bf16[32,1024]{1,0:T(8,128)(2,1)S(1)}, bf16[32,1024]{1,0:T(8,128)(2,1)S(1)}, u32[]{:S(2)}, u32[]{:S(2)}) collective-permute-start(bf16[32,1024]{1,0:T(8,128)(2,1)S(1)} %get-tuple-element.51), channel_id=1, source_target_pairs={{0,6},{1,7},{2,4},{3,5},{4,2},{5,3},{6,0},{7,1},{8,14},{9,15},{10,... | collective-permute-start | bytes 196616 | tf_op jit(solution)/shard_map/ppermute | solution.py:75
  105.2 5.5 %collective-permute-start.25 = (bf16[32,1024]{1,0:T(8,128)(2,1)S(1)}, bf16[32,1024]{1,0:T(8,128)(2,1)S(1)}, u32[]{:S(2)}, u32[]{:S(2)}) collective-permute-start(bf16[32,1024]{1,0:T(8,128)(2,1)S(1)} %get-tuple-element.51), channel_id=1, source_target_pairs={{0,4},{1,5},{2,6},{3,7},{4,0},{5,1},{6,2},{7,3},{8,12},{9,13},{10,... | collective-permute-start | bytes 196616 | tf_op jit(solution)/shard_map/ppermute | solution.py:75
  105.8 5.0 %collective-permute-start.26 = (bf16[32,1024]{1,0:T(8,128)(2,1)S(1)}, bf16[32,1024]{1,0:T(8,128)(2,1)S(1)}, u32[]{:S(2)}, u32[]{:S(2)}) collective-permute-start(bf16[32,1024]{1,0:T(8,128)(2,1)S(1)} %get-tuple-element.51), channel_id=1, source_target_pairs={{0,2},{1,3},{2,0},{3,1},{4,6},{5,7},{6,4},{7,5},{8,10},{9,11},{10,... | collective-permute-start | bytes 196616 | tf_op jit(solution)/shard_map/ppermute | solution.py:75
  110.8 6.4 %collective-permute-start.27 = (bf16[128,1024]{1,0:T(8,128)(2,1)S(1)}, bf16[128,1024]{1,0:T(8,128)(2,1)S(1)}, u32[]{:S(2)}, u32[]{:S(2)}) collective-permute-start(bf16[128,1024]{1,0:T(8,128)(2,1)S(1)} %constant_dynamic-update-slice_fusion.8), channel_id=1, source_target_pairs={{0,1},{1,0},{2,3},{3,2},{4,5},{5,4},{6,7},{7,6},{8,9},{9,8},{10,11... | collective-permute-start | bytes 786440 | tf_op jit(solution)/shard_map/ppermute | solution.py:94
  114.7 8.8 %collective-permute-start.28 = (bf16[128,2048]{1,0:T(8,128)(2,1)}, bf16[128,2048]{1,0:T(8,128)(2,1)S(1)}, u32[]{:S(2)}, u32[]{:S(2)}) collective-permute-start(bf16[128,2048]{1,0:T(8,128)(2,1)} %subtract_convert_fusion.3), channel_id=1, source_target_pairs={{0,8},{8,16},{16,24},{24,0},{1,9},{9,17},{17,25},{25,1},{2,10},{10... | collective-permute-start | bytes 1572872 | tf_op jit(solution)/shard_map/ppermute | solution.py:104
  117.2 2.3 %copy-start.12 = (bf16[128,1024]{1,0:T(8,128)(2,1)}, bf16[128,1024]{1,0:T(8,128)(2,1)S(1)}, u32[]{:S(2)}) copy-start(bf16[128,1024]{1,0:T(8,128)(2,1)S(1)} %collective-permute-done.27) | copy-start | bytes 786436
  119.5 9.7 %collective-permute-start.30 = (bf16[128,2048]{1,0:T(8,128)(2,1)}, bf16[128,2048]{1,0:T(8,128)(2,1)}, u32[]{:S(2)}, u32[]{:S(2)}) collective-permute-start(bf16[128,2048]{1,0:T(8,128)(2,1)} %subtract_convert_fusion.2), channel_id=1, source_target_pairs={{0,8},{8,16},{16,24},{24,0},{1,9},{9,17},{17,25},{25,1},{2,10},{10... | collective-permute-start | bytes 1572872 | tf_op jit(solution)/shard_map/ppermute | solution.py:104
  119.8 9.4 %copy-start.1 = (bf16[2048,1024]{1,0:T(8,128)(2,1)S(1)}, bf16[2048,1024]{1,0:T(8,128)(2,1)}, u32[]{:S(2)}) copy-start(bf16[2048,1024]{1,0:T(8,128)(2,1)} %param.3) | copy-start | bytes 12582916
  126.4 12.1 %copy-start.9 = (bf16[128,1024]{1,0:T(8,128)(2,1)S(1)}, bf16[128,1024]{1,0:T(8,128)(2,1)}, u32[]{:S(2)}) copy-start(bf16[128,1024]{1,0:T(8,128)(2,1)} %copy-done.8) | copy-start | bytes 786436
  126.4 7.5 %collective-permute-start.29 = (bf16[128,1024]{1,0:T(8,128)(2,1)S(1)}, bf16[128,1024]{1,0:T(8,128)(2,1)S(1)}, u32[]{:S(2)}, u32[]{:S(2)}) collective-permute-start(bf16[128,1024]{1,0:T(8,128)(2,1)S(1)} %convolution_convert_fusion), channel_id=1, source_target_pairs={{0,1},{1,0},{2,3},{3,2},{4,5},{5,4},{6,7},{7,6},{8,9},{9,8},{10,11... | collective-permute-start | bytes 786440 | tf_op jit(solution)/shard_map/ppermute | solution.py:87
  131.0 10.7 %copy-start.3 = (bf16[1024,1024]{1,0:T(8,128)(2,1)S(1)}, bf16[1024,1024]{1,0:T(8,128)(2,1)}, u32[]{:S(2)}) copy-start(bf16[1024,1024]{1,0:T(8,128)(2,1)} %get-tuple-element.20) | copy-start | bytes 6291460
  134.0 6.3 %collective-permute-start.31 = (bf16[32,1024]{1,0:T(8,128)(2,1)S(1)}, bf16[32,1024]{1,0:T(8,128)(2,1)S(1)}, u32[]{:S(2)}, u32[]{:S(2)}) collective-permute-start(bf16[32,1024]{1,0:T(8,128)(2,1)S(1)} %get-tuple-element.34), channel_id=1, source_target_pairs={{0,6},{1,7},{2,4},{3,5},{4,2},{5,3},{6,0},{7,1},{8,14},{9,15},{10,... | collective-permute-start | bytes 196616 | tf_op jit(solution)/shard_map/ppermute | solution.py:63
  136.1 5.6 %collective-permute-start.32 = (bf16[32,1024]{1,0:T(8,128)(2,1)S(1)}, bf16[32,1024]{1,0:T(8,128)(2,1)S(1)}, u32[]{:S(2)}, u32[]{:S(2)}) collective-permute-start(bf16[32,1024]{1,0:T(8,128)(2,1)S(1)} %get-tuple-element.36), channel_id=1, source_target_pairs={{0,4},{1,5},{2,6},{3,7},{4,0},{5,1},{6,2},{7,3},{8,12},{9,13},{10,... | collective-permute-start | bytes 196616 | tf_op jit(solution)/shard_map/ppermute | solution.py:63
  136.6 5.1 %collective-permute-start.33 = (bf16[32,1024]{1,0:T(8,128)(2,1)S(1)}, bf16[32,1024]{1,0:T(8,128)(2,1)S(1)}, u32[]{:S(2)}, u32[]{:S(2)}) collective-permute-start(bf16[32,1024]{1,0:T(8,128)(2,1)S(1)} %get-tuple-element.35), channel_id=1, source_target_pairs={{0,2},{1,3},{2,0},{3,1},{4,6},{5,7},{6,4},{7,5},{8,10},{9,11},{10,... | collective-permute-start | bytes 196616 | tf_op jit(solution)/shard_map/ppermute | solution.py:63
  143.3 6.1 %collective-permute-start.34 = (bf16[32,1024]{1,0:T(8,128)(2,1)S(1)}, bf16[32,1024]{1,0:T(8,128)(2,1)S(1)}, u32[]{:S(2)}, u32[]{:S(2)}) collective-permute-start(bf16[32,1024]{1,0:T(8,128)(2,1)S(1)} %get-tuple-element.53), channel_id=1, source_target_pairs={{0,6},{1,7},{2,4},{3,5},{4,2},{5,3},{6,0},{7,1},{8,14},{9,15},{10,... | collective-permute-start | bytes 196616 | tf_op jit(solution)/shard_map/ppermute | solution.py:75
  145.4 5.5 %collective-permute-start.35 = (bf16[32,1024]{1,0:T(8,128)(2,1)S(1)}, bf16[32,1024]{1,0:T(8,128)(2,1)S(1)}, u32[]{:S(2)}, u32[]{:S(2)}) collective-permute-start(bf16[32,1024]{1,0:T(8,128)(2,1)S(1)} %get-tuple-element.53), channel_id=1, source_target_pairs={{0,4},{1,5},{2,6},{3,7},{4,0},{5,1},{6,2},{7,3},{8,12},{9,13},{10,... | collective-permute-start | bytes 196616 | tf_op jit(solution)/shard_map/ppermute | solution.py:75
  145.9 5.0 %collective-permute-start.36 = (bf16[32,1024]{1,0:T(8,128)(2,1)S(1)}, bf16[32,1024]{1,0:T(8,128)(2,1)S(1)}, u32[]{:S(2)}, u32[]{:S(2)}) collective-permute-start(bf16[32,1024]{1,0:T(8,128)(2,1)S(1)} %get-tuple-element.53), channel_id=1, source_target_pairs={{0,2},{1,3},{2,0},{3,1},{4,6},{5,7},{6,4},{7,5},{8,10},{9,11},{10,... | collective-permute-start | bytes 196616 | tf_op jit(solution)/shard_map/ppermute | solution.py:75
  150.9 7.6 %collective-permute-start.37 = (bf16[128,1024]{1,0:T(8,128)(2,1)S(1)}, bf16[128,1024]{1,0:T(8,128)(2,1)S(1)}, u32[]{:S(2)}, u32[]{:S(2)}) collective-permute-start(bf16[128,1024]{1,0:T(8,128)(2,1)S(1)} %constant_dynamic-update-slice_fusion.2), channel_id=1, source_target_pairs={{0,1},{1,0},{2,3},{3,2},{4,5},{5,4},{6,7},{7,6},{8,9},{9,8},{10,11... | collective-permute-start | bytes 786440 | tf_op jit(solution)/shard_map/ppermute | solution.py:94
  155.2 4.9 %copy-start.11 = (bf16[128,1024]{1,0:T(8,128)(2,1)S(1)}, bf16[128,1024]{1,0:T(8,128)(2,1)}, u32[]{:S(2)}) copy-start(bf16[128,1024]{1,0:T(8,128)(2,1)} %copy-done.10) | copy-start | bytes 786436
  155.2 5.0 %copy-start.13 = (bf16[128,1024]{1,0:T(8,128)(2,1)S(1)}, bf16[128,1024]{1,0:T(8,128)(2,1)}, u32[]{:S(2)}) copy-start(bf16[128,1024]{1,0:T(8,128)(2,1)} %copy-done.12) | copy-start | bytes 786436
  155.2 8.7 %collective-permute-start.38 = (bf16[128,2048]{1,0:T(8,128)(2,1)S(1)}, bf16[128,2048]{1,0:T(8,128)(2,1)S(1)}, u32[]{:S(2)}, u32[]{:S(2)}) collective-permute-start(bf16[128,2048]{1,0:T(8,128)(2,1)S(1)} %subtract_convert_fusion.1), channel_id=1, source_target_pairs={{0,8},{8,16},{16,24},{24,0},{1,9},{9,17},{17,25},{25,1},{2,10},{10... | collective-permute-start | bytes 1572872 | tf_op jit(solution)/shard_map/ppermute | solution.py:104
  160.1 9.4 %collective-permute-start.39 = (bf16[128,2048]{1,0:T(8,128)(2,1)S(1)}, bf16[128,2048]{1,0:T(8,128)(2,1)S(1)}, u32[]{:S(2)}, u32[]{:S(2)}) collective-permute-start(bf16[128,2048]{1,0:T(8,128)(2,1)S(1)} %subtract_convert_fusion), channel_id=1, source_target_pairs={{0,8},{8,16},{16,24},{24,0},{1,9},{9,17},{17,25},{25,1},{2,10},{10... | collective-permute-start | bytes 1572872 | tf_op jit(solution)/shard_map/ppermute | solution.py:104
  160.3 9.2 %copy-start.7 = (bf16[1024,1024]{1,0:T(8,128)(2,1)}, bf16[1024,1024]{1,0:T(8,128)(2,1)S(1)}, u32[]{:S(2)}) copy-start(bf16[1024,1024]{1,0:T(8,128)(2,1)S(1)} %constant_dynamic-update-slice_fusion) | copy-start | bytes 6291460

commit v3 on v2

--- a/solution.py
+++ b/solution.py
@@ -1,6 +1,10 @@
+import functools
+
 import jax
 import jax.numpy as jnp
 from jax import lax
+from jax.experimental import pallas as pl
+from jax.experimental.pallas import tpu as pltpu
 from jax.sharding import PartitionSpec as P
 
 BF16 = jnp.bfloat16
@@ -10,6 +14,100 @@
 def split_high_low(value):
     high = lax.reduce_precision(value, 8, 7)
     return high.astype(BF16), (value - high).astype(BF16)
+
+
+CHUNK = 1024
+LANES = 128
+FIRST_VMEM = 56 * 1024 * 1024
+SCATTER_VMEM = 12 * 1024 * 1024
+
+
+def first_kernel(lead_ref, away_ref, home_ref, x_ref, term_ref, kept_ref, away_out, home_out, acc):
+    step = pl.program_id(0)
+    half = away_ref.shape[1]
+    away = away_ref[...].T
+    home = home_ref[...].T
+    away_out[...] = away
+    home_out[...] = home
+    both = jnp.concatenate([away, home], 0).astype(BF16)
+    product = jnp.dot(both, x_ref[...], preferred_element_type=F32)
+
+    @pl.when(step == 0)
+    def _():
+        acc[...] = product
+
+    @pl.when(step > 0)
+    def _():
+        acc[...] += product
+
+    @pl.when(step == pl.num_programs(0) - 1)
+    def _():
+        term_ref[...] = acc[:half, :].astype(BF16)
+        kept_ref[...] = acc[half:, :]
+
+
+def first_projection(features, residual, lead):
+    rows, feat_width = features.shape
+    half = residual.shape[1] // 2
+    return pl.pallas_call(
+        first_kernel,
+        out_shape=(
+            jax.ShapeDtypeStruct((half, feat_width), BF16),
+            jax.ShapeDtypeStruct((half, feat_width), F32),
+            jax.ShapeDtypeStruct((half, rows), F32),
+            jax.ShapeDtypeStruct((half, rows), F32),
+        ),
+        grid_spec=pltpu.PrefetchScalarGridSpec(
+            num_scalar_prefetch=1,
+            grid=(rows // CHUNK,),
+            in_specs=[
+                pl.BlockSpec((CHUNK, half), lambda i, lead: (i, lead[0])),
+                pl.BlockSpec((CHUNK, half), lambda i, lead: (i, 1 - lead[0])),
+                pl.BlockSpec((CHUNK, feat_width), lambda i, lead: (i, 0)),
+            ],
+            out_specs=[
+                pl.BlockSpec((half, feat_width), lambda i, lead: (0, 0)),
+                pl.BlockSpec((half, feat_width), lambda i, lead: (0, 0)),
+                pl.BlockSpec((half, CHUNK), lambda i, lead: (0, i)),
+                pl.BlockSpec((half, CHUNK), lambda i, lead: (0, i)),
+            ],
+            scratch_shapes=[pltpu.VMEM((2 * half, feat_width), F32)],
+        ),
+        compiler_params=pltpu.CompilerParams(vmem_limit_bytes=FIRST_VMEM),
+        cost_estimate=pl.CostEstimate(
+            flops=4 * rows * half * feat_width,
+            bytes_accessed=2 * rows * feat_width + 16 * rows * half + 6 * half * feat_width,
+            transcendentals=0,
+        ),
+    )(lead.reshape(1), residual, residual, features)
+
+
+def scatter_kernel(pieces, start_ref, *refs):
+    updates, out_ref = refs[:pieces], refs[pieces]
+    height = updates[0].shape[0]
+    for at in range(pieces):
+        rows = pl.ds(pl.multiple_of(start_ref[at] * height, height), height)
+        out_ref[rows, :] = updates[at][...]
+
+
+def scatter_rows(updates, starts):
+    pieces = len(updates)
+    height, feat_width = updates[0].shape
+    whole = lambda i, starts: (0, 0)
+    return pl.pallas_call(
+        functools.partial(scatter_kernel, pieces),
+        out_shape=jax.ShapeDtypeStruct((pieces * height, feat_width), BF16),
+        grid_spec=pltpu.PrefetchScalarGridSpec(
+            num_scalar_prefetch=1,
+            grid=(1,),
+            in_specs=[pl.BlockSpec((height, feat_width), whole)] * pieces,
+            out_specs=pl.BlockSpec((pieces * height, feat_width), whole),
+        ),
+        compiler_params=pltpu.CompilerParams(vmem_limit_bytes=SCATTER_VMEM),
+        cost_estimate=pl.CostEstimate(
+            flops=0, bytes_accessed=4 * pieces * height * feat_width, transcendentals=0
+        ),
+    )(jnp.stack(starts).astype(jnp.int32), *updates)
 
 
 def on_device(features, residual, inverse_grams):
@@ -76,33 +174,45 @@
             full = lax.dynamic_update_slice_in_dim(full, got, (outer_id ^ step) * piece, 0)
         return full
 
-    increments = jnp.zeros((width * blocks, feat_width), BF16)
-    halves = [
-        lax.dynamic_slice_in_dim(residual, s * half, half, 1).T for s in (1 - inner_id, inner_id)
-    ]
+    updates, starts = [], []
+    kernels = half % LANES == 0 and features.shape[0] % CHUNK == 0 and feat_width % LANES == 0
+    if kernels:
+        term, kept, *halves = first_projection(features, residual, 1 - inner_id)
+    else:
+        halves = [
+            lax.dynamic_slice_in_dim(residual, s * half, half, 1).T
+            for s in (1 - inner_id, inner_id)
+        ]
     lead = 1 - inner_id
     for visit in range(blocks):
         front = (block_id - visit) % blocks
         away, home = halves
-        arrived = lax.ppermute(project(away.astype(BF16)).astype(BF16), "rows", partner)
-        kept = project(home.astype(BF16))
+        if visit > 0 or not kernels:
+            term = project(away.astype(BF16)).astype(BF16)
+            kept = project(home.astype(BF16))
+        arrived = lax.ppermute(term, "rows", partner)
         if visit == 0:
             inverse_high, inverse_low = split_high_low(inverse_grams)
-        arrived, kept = lax.optimization_barrier((arrived, kept))
+            arrived, kept, inverse_high, inverse_low = lax.optimization_barrier(
+                (arrived, kept, inverse_high, inverse_low)
+            )
+        else:
+            arrived, kept = lax.optimization_barrier((arrived, kept))
         total = kept + arrived.astype(F32)
         update_home = gather_outer(apply_inverse(reduce_outer(total), inverse_high, inverse_low))
         update_away = lax.ppermute(update_home, "rows", partner)
         home = subtract(home, update_home)
         away = subtract(away, update_away)
-        start = front * width
-        increments = lax.dynamic_update_slice_in_dim(
-            increments, update_home, start + (1 - lead) * half, 0
-        )
-        increments = lax.dynamic_update_slice_in_dim(
-            increments, update_away, start + lead * half, 0
-        )
+        updates += [update_home, update_away]
+        starts += [front * inner + (1 - lead), front * inner + lead]
         halves = [lax.ppermute(part.astype(BF16), "feat", next_block) for part in (home, away)]
         lead = 1 - lead
+    if kernels:
+        increments = scatter_rows(updates, starts)
+    else:
+        increments = jnp.zeros((width * blocks, feat_width), BF16)
+        for update, start in zip(updates, starts):
+            increments = lax.dynamic_update_slice_in_dim(increments, update, start * half, 0)
     first = jnp.where(lead == 0, halves[0], halves[1])
     second = jnp.where(lead == 0, halves[1], halves[0])
     return increments, jnp.concatenate([first, second], 0).astype(F32).T

time: 172 us -> 164 us (0.953)
  matrix products: 36.9 us -> 25.4 us
  Pallas kernels: 0 us -> 7.08 us
  local copies, waits for them, and re-layouts: 6.04 us -> 2.28 us
    dot_general x8 -> x6, matrix products: 14.5 us -> 4.32 us  [project(): lax.dot_general(current, features, (((1,), (0,)), ((), ())), preferred_el...]
    pallas_call x0 -> x2, Pallas kernels: none -> 7.08 us  [the longest x1 5.08 us: first_projection(): pl.pallas_call(first_kernel, out_shape=(jax.ShapeDtypeStruct((half, feat_...]
    ppermute x4, waiting for transfers between devices: 8.22 us -> 6.02 us  [on_device(): arrived = lax.ppermute(term, 'rows', partner)]
    ppermute x12, waiting for transfers between devices: 12 us -> 14.1 us  [reduce_outer(): lax.ppermute(out.astype(BF16), 'rows', outer_step(step)).astype(F32)]
  transfers between devices with their start and end apart: 40 -> 40, of which waited for: 31 -> 32; matrix products, arithmetic and copies ran while one was open for 17% -> 14% of each run, Pallas kernels for 0% -> 1%
where the time goes in v3:
time: 164 us
  waiting for transfers between devices  76.4 us (47%)
  starting transfers between devices  46.2 us (28%)
  matrix products  25.4 us (15%)
  Pallas kernels  7.08 us (4%)
  other arithmetic  5.22 us (3%)
  local copies, waits for them, and re-layouts  2.28 us (1%)
    ppermute x8, waiting for transfers between devices, on_device(): lax.ppermute(part.astype(BF16), 'feat', next_block)  29.1 us
    ppermute x12, starting transfers between devices, reduce_outer(): lax.ppermute(out.astype(BF16), 'rows', outer_step(step)).astype(F32)  17.9 us
    ppermute x12, starting transfers between devices, gather_outer(): got = lax.ppermute(update, 'rows', outer_step(step))  17.7 us
    ppermute x4, waiting for transfers between devices, on_device(): update_away = lax.ppermute(update_home, 'rows', partner)  14.4 us
    ppermute x12, waiting for transfers between devices, reduce_outer(): lax.ppermute(out.astype(BF16), 'rows', outer_step(step)).astype(F32)  14.1 us
    dot_general x8, matrix products, subtract(): lax.dot_general(update, features, (((1,), (1,)), ((), ())), preferred_ele...  13.6 us
    ppermute x12, waiting for transfers between devices, gather_outer(): got = lax.ppermute(update, 'rows', outer_step(step))  12.8 us
    dot_general x8, matrix products, apply_inverse(): dot = lambda a, b: lax.dot_general(a, b, dims, preferred_element_type=F32)  7.52 us
  transfers between devices with their start and end apart: 40, of which 32 were waited for; matrix products, arithmetic and copies ran while one was open for 14% of the time, Pallas kernels for 1%

profile of v3, /device:TPU:0, one launch (start us, length us, event | category | flops | bytes accessed | tf_op | source)
XLA Modules:
  0.0 163.7 jit_solution(15548556698094900513)
XLA Ops:
  0.6 5.1 %shard_map.50 = (bf16[128,1024]{1,0:T(8,128)(2,1)}, f32[128,1024]{1,0:T(8,128)}, f32[128,2048]{1,0:T(8,128)}, f32[128,2048]{1,0:T(8,128)}) custom-call(s32[1]{0:T(128)} %bitcast.8.lead_ref, f32[2048,256]{1,0:T(8,128)} %home_ref.1, f32[2048,256]{1,0:T(8,128)} %home_ref.1, bf16[2048,1024]{1,0:T(8,128)(2,1)} %x_ref.1), custom_call_target="tpu_custom_call" | custom-call | flops 1073741824 | bytes 9175040 | tf_op jit(solution)/shard_map/pallas_call | solution.py:52
  5.7 3.0 %collective-permute-start = (bf16[128,1024]{1,0:T(8,128)(2,1)}, bf16[128,1024]{1,0:T(8,128)(2,1)S(1)}, u32[]{:S(2)}, u32[]{:S(2)}) collective-permute-start(bf16[128,1024]{1,0:T(8,128)(2,1)} %get-tuple-element.16), channel_id=1, source_target_pairs={{0,1},{1,0},{2,3},{3,2},{4,5},{5,4},{6,7},{7,6},{8,9},{9,8},{10,11... | collective-permute-start | bytes 786440 | tf_op jit(solution)/shard_map/ppermute | solution.py:193
  8.7 4.5 %fusion = (bf16[1024,1024]{1,0:T(8,128)(2,1)S(1)}, bf16[1024,1024]{1,0:T(8,128)(2,1)}) fusion(f32[1024,1024]{1,0:T(8,128)} %param.5), kind=kLoop, calls=%fused_computation.2 | loop fusion | flops 4194304 | bytes 8388608 | tf_op jit(solution)/shard_map/convert_element_type | solution.py:16
  13.2 2.0 %collective-permute-done = bf16[128,1024]{1,0:T(8,128)(2,1)S(1)} collective-permute-done((bf16[128,1024]{1,0:T(8,128)(2,1)}, bf16[128,1024]{1,0:T(8,128)(2,1)S(1)}, u32[]{:S(2)}, u32[]{:S(2)}) %collective-permute-start) | collective-permute-done | bytes 262176 | tf_op jit(solution)/shard_map/ppermute | solution.py:193
  15.3 3.9 %collective-permute-start.1 = (bf16[32,1024]{1,0:T(8,128)(2,1)S(1)}, bf16[32,1024]{1,0:T(8,128)(2,1)S(1)}, u32[]{:S(2)}, u32[]{:S(2)}) collective-permute-start(bf16[32,1024]{1,0:T(8,128)(2,1)S(1)} %get-tuple-element.53), channel_id=1, source_target_pairs={{0,6},{1,7},{2,4},{3,5},{4,2},{5,3},{6,0},{7,1},{8,14},{9,15},{10,... | collective-permute-start | bytes 196616 | tf_op jit(solution)/shard_map/ppermute | solution.py:161
  19.9 2.0 %collective-permute-done.1 = bf16[32,1024]{1,0:T(8,128)(2,1)S(1)} collective-permute-done((bf16[32,1024]{1,0:T(8,128)(2,1)S(1)}, bf16[32,1024]{1,0:T(8,128)(2,1)S(1)}, u32[]{:S(2)}, u32[]{:S(2)}) %collective-permute-start.1) | collective-permute-done | bytes 65568 | tf_op jit(solution)/shard_map/ppermute | solution.py:161
  21.9 2.7 %collective-permute-done.2 = bf16[32,1024]{1,0:T(8,128)(2,1)S(1)} collective-permute-done((bf16[32,1024]{1,0:T(8,128)(2,1)S(1)}, bf16[32,1024]{1,0:T(8,128)(2,1)S(1)}, u32[]{:S(2)}, u32[]{:S(2)}) %collective-permute-start.2) | collective-permute-done | bytes 65568 | tf_op jit(solution)/shard_map/ppermute | solution.py:161
  24.6 2.3 %fusion.11 = f32[64,1024]{1,0:T(8,128)S(1)} fusion(bf16[1024,1024]{1,0:T(8,128)(2,1)} %get-tuple-element.20, bf16[32,1024]{1,0:T(8,128)(2,1)S(1)} %get-tuple-element.42, bf16[32,1024]{1,0:T(8,128)(2,1)S(1)} %get-tuple-element.43), kind=kOutput, calls=%fused_computation.47 | convolution fusion | flops 134479872 | bytes 2490368 | tf_op jit(solution)/shard_map/dot_general | solution.py:142
  27.7 2.3 %collective-permute-start.4 = (bf16[32,1024]{1,0:T(8,128)(2,1)S(1)}, bf16[32,1024]{1,0:T(8,128)(2,1)S(1)}, u32[]{:S(2)}, u32[]{:S(2)}) collective-permute-start(bf16[32,1024]{1,0:T(8,128)(2,1)S(1)} %get-tuple-element.57), channel_id=1, source_target_pairs={{0,6},{1,7},{2,4},{3,5},{4,2},{5,3},{6,0},{7,1},{8,14},{9,15},{10,... | collective-permute-start | bytes 196616 | tf_op jit(solution)/shard_map/ppermute | solution.py:173
  30.0 2.2 %collective-permute-start.6 = (bf16[32,1024]{1,0:T(8,128)(2,1)S(1)}, bf16[32,1024]{1,0:T(8,128)(2,1)S(1)}, u32[]{:S(2)}, u32[]{:S(2)}) collective-permute-start(bf16[32,1024]{1,0:T(8,128)(2,1)S(1)} %get-tuple-element.57), channel_id=1, source_target_pairs={{0,2},{1,3},{2,0},{3,1},{4,6},{5,7},{6,4},{7,5},{8,10},{9,11},{10,... | collective-permute-start | bytes 196616 | tf_op jit(solution)/shard_map/ppermute | solution.py:173
  32.2 1.7 %collective-permute-done.4 = bf16[32,1024]{1,0:T(8,128)(2,1)S(1)} collective-permute-done((bf16[32,1024]{1,0:T(8,128)(2,1)S(1)}, bf16[32,1024]{1,0:T(8,128)(2,1)S(1)}, u32[]{:S(2)}, u32[]{:S(2)}) %collective-permute-start.4) | collective-permute-done | bytes 65568 | tf_op jit(solution)/shard_map/ppermute | solution.py:173
  33.9 1.6 collective-permute-done.5
  35.5 1.6 collective-permute-start.7
  37.1 1.5 fusion.1
  38.7 3.3 %collective-permute-done.7.refs_1_ = bf16[128,1024]{1,0:T(8,128)(2,1)S(1)} collective-permute-done((bf16[128,1024]{1,0:T(8,128)(2,1)S(1)}, bf16[128,1024]{1,0:T(8,128)(2,1)S(1)}, u32[]{:S(2)}, u32[]{:S(2)}) %collective-permute-start.7) | collective-permute-done | bytes 262176 | tf_op jit(solution)/shard_map/ppermute | solution.py:203
  42.0 1.5 fusion.2
  43.5 3.7 %collective-permute-done.8 = bf16[128,2048]{1,0:T(8,128)(2,1)S(1)} collective-permute-done((bf16[128,2048]{1,0:T(8,128)(2,1)S(1)}, bf16[128,2048]{1,0:T(8,128)(2,1)S(1)}, u32[]{:S(2)}, u32[]{:S(2)}) %collective-permute-start.8) | collective-permute-done | bytes 524320 | tf_op jit(solution)/shard_map/ppermute | solution.py:208
  48.6 4.3 %collective-permute-done.10 = bf16[128,2048]{1,0:T(8,128)(2,1)S(1)} collective-permute-done((bf16[128,2048]{1,0:T(8,128)(2,1)S(1)}, bf16[128,2048]{1,0:T(8,128)(2,1)S(1)}, u32[]{:S(2)}, u32[]{:S(2)}) %collective-permute-start.10) | collective-permute-done | bytes 524320 | tf_op jit(solution)/shard_map/ppermute | solution.py:208
  53.6 1.8 %collective-permute-done.9 = bf16[128,1024]{1,0:T(8,128)(2,1)S(1)} collective-permute-done((bf16[128,1024]{1,0:T(8,128)(2,1)S(1)}, bf16[128,1024]{1,0:T(8,128)(2,1)S(1)}, u32[]{:S(2)}, u32[]{:S(2)}) %collective-permute-start.9) | collective-permute-done | bytes 262176 | tf_op jit(solution)/shard_map/ppermute | solution.py:193
  55.5 2.1 %collective-permute-start.11 = (bf16[32,1024]{1,0:T(8,128)(2,1)S(1)}, bf16[32,1024]{1,0:T(8,128)(2,1)S(1)}, u32[]{:S(2)}, u32[]{:S(2)}) collective-permute-start(bf16[32,1024]{1,0:T(8,128)(2,1)S(1)} %get-tuple-element.50), channel_id=1, source_target_pairs={{0,6},{1,7},{2,4},{3,5},{4,2},{5,3},{6,0},{7,1},{8,14},{9,15},{10,... | collective-permute-start | bytes 196616 | tf_op jit(solution)/shard_map/ppermute | solution.py:161
  58.0 2.0 %collective-permute-start.13 = (bf16[32,1024]{1,0:T(8,128)(2,1)S(1)}, bf16[32,1024]{1,0:T(8,128)(2,1)S(1)}, u32[]{:S(2)}, u32[]{:S(2)}) collective-permute-start(bf16[32,1024]{1,0:T(8,128)(2,1)S(1)} %get-tuple-element.51), channel_id=1, source_target_pairs={{0,2},{1,3},{2,0},{3,1},{4,6},{5,7},{6,4},{7,5},{8,10},{9,11},{10,... | collective-permute-start | bytes 196616 | tf_op jit(solution)/shard_map/ppermute | solution.py:161
  60.0 1.7 %collective-permute-done.11 = bf16[32,1024]{1,0:T(8,128)(2,1)S(1)} collective-permute-done((bf16[32,1024]{1,0:T(8,128)(2,1)S(1)}, bf16[32,1024]{1,0:T(8,128)(2,1)S(1)}, u32[]{:S(2)}, u32[]{:S(2)}) %collective-permute-start.11) | collective-permute-done | bytes 65568 | tf_op jit(solution)/shard_map/ppermute | solution.py:161
  61.7 1.4 collective-permute-done.12
  64.7 2.1 %collective-permute-start.14 = (bf16[32,1024]{1,0:T(8,128)(2,1)S(1)}, bf16[32,1024]{1,0:T(8,128)(2,1)S(1)}, u32[]{:S(2)}, u32[]{:S(2)}) collective-permute-start(bf16[32,1024]{1,0:T(8,128)(2,1)S(1)} %get-tuple-element.59), channel_id=1, source_target_pairs={{0,6},{1,7},{2,4},{3,5},{4,2},{5,3},{6,0},{7,1},{8,14},{9,15},{10,... | collective-permute-start | bytes 196616 | tf_op jit(solution)/shard_map/ppermute | solution.py:173
  67.3 1.8 %collective-permute-start.16 = (bf16[32,1024]{1,0:T(8,128)(2,1)S(1)}, bf16[32,1024]{1,0:T(8,128)(2,1)S(1)}, u32[]{:S(2)}, u32[]{:S(2)}) collective-permute-start(bf16[32,1024]{1,0:T(8,128)(2,1)S(1)} %get-tuple-element.59), channel_id=1, source_target_pairs={{0,2},{1,3},{2,0},{3,1},{4,6},{5,7},{6,4},{7,5},{8,10},{9,11},{10,... | collective-permute-start | bytes 196616 | tf_op jit(solution)/shard_map/ppermute | solution.py:173
  69.2 1.7 %collective-permute-done.14 = bf16[32,1024]{1,0:T(8,128)(2,1)S(1)} collective-permute-done((bf16[32,1024]{1,0:T(8,128)(2,1)S(1)}, bf16[32,1024]{1,0:T(8,128)(2,1)S(1)}, u32[]{:S(2)}, u32[]{:S(2)}) %collective-permute-start.14) | collective-permute-done | bytes 65568 | tf_op jit(solution)/shard_map/ppermute | solution.py:173
  70.9 1.5 collective-permute-done.15
  72.9 1.5 subtract_convert_fusion.5
  74.5 4.3 %collective-permute-done.17.refs_3_ = bf16[128,1024]{1,0:T(8,128)(2,1)S(1)} collective-permute-done((bf16[128,1024]{1,0:T(8,128)(2,1)S(1)}, bf16[128,1024]{1,0:T(8,128)(2,1)S(1)}, u32[]{:S(2)}, u32[]{:S(2)}) %collective-permute-start.17) | collective-permute-done | bytes 262176 | tf_op jit(solution)/shard_map/ppermute | solution.py:203
  78.8 1.5 subtract_convert_fusion.4
  80.6 2.5 %collective-permute-done.18 = bf16[128,2048]{1,0:T(8,128)(2,1)S(1)} collective-permute-done((bf16[128,2048]{1,0:T(8,128)(2,1)S(1)}, bf16[128,2048]{1,0:T(8,128)(2,1)S(1)}, u32[]{:S(2)}, u32[]{:S(2)}) %collective-permute-start.18) | collective-permute-done | bytes 524320 | tf_op jit(solution)/shard_map/ppermute | solution.py:208
  83.8 1.6 collective-permute-start.19
  85.4 3.7 %collective-permute-done.20 = bf16[128,2048]{1,0:T(8,128)(2,1)S(1)} collective-permute-done((bf16[128,2048]{1,0:T(8,128)(2,1)S(1)}, bf16[128,2048]{1,0:T(8,128)(2,1)S(1)}, u32[]{:S(2)}, u32[]{:S(2)}) %collective-permute-start.20) | collective-permute-done | bytes 524320 | tf_op jit(solution)/shard_map/ppermute | solution.py:208
  90.4 2.1 %collective-permute-start.21 = (bf16[32,1024]{1,0:T(8,128)(2,1)S(1)}, bf16[32,1024]{1,0:T(8,128)(2,1)S(1)}, u32[]{:S(2)}, u32[]{:S(2)}) collective-permute-start(bf16[32,1024]{1,0:T(8,128)(2,1)S(1)} %get-tuple-element.47), channel_id=1, source_target_pairs={{0,6},{1,7},{2,4},{3,5},{4,2},{5,3},{6,0},{7,1},{8,14},{9,15},{10,... | collective-permute-start | bytes 196616 | tf_op jit(solution)/shard_map/ppermute | solution.py:161
  93.0 1.8 %collective-permute-start.23 = (bf16[32,1024]{1,0:T(8,128)(2,1)S(1)}, bf16[32,1024]{1,0:T(8,128)(2,1)S(1)}, u32[]{:S(2)}, u32[]{:S(2)}) collective-permute-start(bf16[32,1024]{1,0:T(8,128)(2,1)S(1)} %get-tuple-element.48), channel_id=1, source_target_pairs={{0,2},{1,3},{2,0},{3,1},{4,6},{5,7},{6,4},{7,5},{8,10},{9,11},{10,... | collective-permute-start | bytes 196616 | tf_op jit(solution)/shard_map/ppermute | solution.py:161
  94.8 1.7 %collective-permute-done.21 = bf16[32,1024]{1,0:T(8,128)(2,1)S(1)} collective-permute-done((bf16[32,1024]{1,0:T(8,128)(2,1)S(1)}, bf16[32,1024]{1,0:T(8,128)(2,1)S(1)}, u32[]{:S(2)}, u32[]{:S(2)}) %collective-permute-start.21) | collective-permute-done | bytes 65568 | tf_op jit(solution)/shard_map/ppermute | solution.py:161
  96.5 1.5 collective-permute-done.22
  99.5 2.1 %collective-permute-start.24 = (bf16[32,1024]{1,0:T(8,128)(2,1)S(1)}, bf16[32,1024]{1,0:T(8,128)(2,1)S(1)}, u32[]{:S(2)}, u32[]{:S(2)}) collective-permute-start(bf16[32,1024]{1,0:T(8,128)(2,1)S(1)} %get-tuple-element.61), channel_id=1, source_target_pairs={{0,6},{1,7},{2,4},{3,5},{4,2},{5,3},{6,0},{7,1},{8,14},{9,15},{10,... | collective-permute-start | bytes 196616 | tf_op jit(solution)/shard_map/ppermute | solution.py:173
  102.2 1.8 %collective-permute-start.26 = (bf16[32,1024]{1,0:T(8,128)(2,1)S(1)}, bf16[32,1024]{1,0:T(8,128)(2,1)S(1)}, u32[]{:S(2)}, u32[]{:S(2)}) collective-permute-start(bf16[32,1024]{1,0:T(8,128)(2,1)S(1)} %get-tuple-element.61), channel_id=1, source_target_pairs={{0,2},{1,3},{2,0},{3,1},{4,6},{5,7},{6,4},{7,5},{8,10},{9,11},{10,... | collective-permute-start | bytes 196616 | tf_op jit(solution)/shard_map/ppermute | solution.py:173
  104.0 1.7 %collective-permute-done.24 = bf16[32,1024]{1,0:T(8,128)(2,1)S(1)} collective-permute-done((bf16[32,1024]{1,0:T(8,128)(2,1)S(1)}, bf16[32,1024]{1,0:T(8,128)(2,1)S(1)}, u32[]{:S(2)}, u32[]{:S(2)}) %collective-permute-start.24) | collective-permute-done | bytes 65568 | tf_op jit(solution)/shard_map/ppermute | solution.py:173
  105.7 1.5 collective-permute-done.25
  107.2 1.6 collective-permute-start.27
  108.8 1.5 subtract_convert_fusion.3
  110.4 3.3 %collective-permute-done.27.refs_5_ = bf16[128,1024]{1,0:T(8,128)(2,1)S(1)} collective-permute-done((bf16[128,1024]{1,0:T(8,128)(2,1)S(1)}, bf16[128,1024]{1,0:T(8,128)(2,1)S(1)}, u32[]{:S(2)}, u32[]{:S(2)}) %collective-permute-start.27) | collective-permute-done | bytes 262176 | tf_op jit(solution)/shard_map/ppermute | solution.py:203
  113.6 1.5 subtract_convert_fusion.2
  115.2 3.7 %collective-permute-done.28 = bf16[128,2048]{1,0:T(8,128)(2,1)S(1)} collective-permute-done((bf16[128,2048]{1,0:T(8,128)(2,1)S(1)}, bf16[128,2048]{1,0:T(8,128)(2,1)S(1)}, u32[]{:S(2)}, u32[]{:S(2)}) %collective-permute-start.28) | collective-permute-done | bytes 524320 | tf_op jit(solution)/shard_map/ppermute | solution.py:208
  120.3 4.3 %collective-permute-done.30 = bf16[128,2048]{1,0:T(8,128)(2,1)S(1)} collective-permute-done((bf16[128,2048]{1,0:T(8,128)(2,1)S(1)}, bf16[128,2048]{1,0:T(8,128)(2,1)S(1)}, u32[]{:S(2)}, u32[]{:S(2)}) %collective-permute-start.30) | collective-permute-done | bytes 524320 | tf_op jit(solution)/shard_map/ppermute | solution.py:208
  125.3 1.8 %collective-permute-done.29 = bf16[128,1024]{1,0:T(8,128)(2,1)S(1)} collective-permute-done((bf16[128,1024]{1,0:T(8,128)(2,1)S(1)}, bf16[128,1024]{1,0:T(8,128)(2,1)S(1)}, u32[]{:S(2)}, u32[]{:S(2)}) %collective-permute-start.29) | collective-permute-done | bytes 262176 | tf_op jit(solution)/shard_map/ppermute | solution.py:193
  127.2 2.1 %collective-permute-start.31 = (bf16[32,1024]{1,0:T(8,128)(2,1)S(1)}, bf16[32,1024]{1,0:T(8,128)(2,1)S(1)}, u32[]{:S(2)}, u32[]{:S(2)}) collective-permute-start(bf16[32,1024]{1,0:T(8,128)(2,1)S(1)} %get-tuple-element.44), channel_id=1, source_target_pairs={{0,6},{1,7},{2,4},{3,5},{4,2},{5,3},{6,0},{7,1},{8,14},{9,15},{10,... | collective-permute-start | bytes 196616 | tf_op jit(solution)/shard_map/ppermute | solution.py:161
  129.8 1.9 %collective-permute-start.33 = (bf16[32,1024]{1,0:T(8,128)(2,1)S(1)}, bf16[32,1024]{1,0:T(8,128)(2,1)S(1)}, u32[]{:S(2)}, u32[]{:S(2)}) collective-permute-start(bf16[32,1024]{1,0:T(8,128)(2,1)S(1)} %get-tuple-element.45), channel_id=1, source_target_pairs={{0,2},{1,3},{2,0},{3,1},{4,6},{5,7},{6,4},{7,5},{8,10},{9,11},{10,... | collective-permute-start | bytes 196616 | tf_op jit(solution)/shard_map/ppermute | solution.py:161
  131.7 1.7 %collective-permute-done.31 = bf16[32,1024]{1,0:T(8,128)(2,1)S(1)} collective-permute-done((bf16[32,1024]{1,0:T(8,128)(2,1)S(1)}, bf16[32,1024]{1,0:T(8,128)(2,1)S(1)}, u32[]{:S(2)}, u32[]{:S(2)}) %collective-permute-start.31) | collective-permute-done | bytes 65568 | tf_op jit(solution)/shard_map/ppermute | solution.py:161
  133.4 1.4 collective-permute-done.32
  134.8 0.8 fusion.23
  136.3 2.1 %collective-permute-start.34 = (bf16[32,1024]{1,0:T(8,128)(2,1)S(1)}, bf16[32,1024]{1,0:T(8,128)(2,1)S(1)}, u32[]{:S(2)}, u32[]{:S(2)}) collective-permute-start(bf16[32,1024]{1,0:T(8,128)(2,1)S(1)} %get-tuple-element.63), channel_id=1, source_target_pairs={{0,6},{1,7},{2,4},{3,5},{4,2},{5,3},{6,0},{7,1},{8,14},{9,15},{10,... | collective-permute-start | bytes 196616 | tf_op jit(solution)/shard_map/ppermute | solution.py:173
  139.0 1.8 %collective-permute-start.36 = (bf16[32,1024]{1,0:T(8,128)(2,1)S(1)}, bf16[32,1024]{1,0:T(8,128)(2,1)S(1)}, u32[]{:S(2)}, u32[]{:S(2)}) collective-permute-start(bf16[32,1024]{1,0:T(8,128)(2,1)S(1)} %get-tuple-element.63), channel_id=1, source_target_pairs={{0,2},{1,3},{2,0},{3,1},{4,6},{5,7},{6,4},{7,5},{8,10},{9,11},{10,... | collective-permute-start | bytes 196616 | tf_op jit(solution)/shard_map/ppermute | solution.py:173
  140.8 1.7 %collective-permute-done.34 = bf16[32,1024]{1,0:T(8,128)(2,1)S(1)} collective-permute-done((bf16[32,1024]{1,0:T(8,128)(2,1)S(1)}, bf16[32,1024]{1,0:T(8,128)(2,1)S(1)}, u32[]{:S(2)}, u32[]{:S(2)}) %collective-permute-start.34) | collective-permute-done | bytes 65568 | tf_op jit(solution)/shard_map/ppermute | solution.py:173
  142.5 1.5 collective-permute-done.35
  144.6 2.3 %subtract_convert_fusion.1 = bf16[128,2048]{1,0:T(8,128)(2,1)} fusion(bf16[128,2048]{1,0:T(8,128)(2,1)S(1)} %collective-permute-done.30, bf16[128,1024]{1,0:T(8,128)(2,1)S(1)} %constant_dynamic-update-slice_fusion.refs_6_, bf16[2048,1024]{1,0:T(8,128)(2,1)S(1)} %copy-done), kind=kOutput, calls=%fused_computation.20 | convolution fusion | flops 537657344 | bytes 5505024 | tf_op jit(solution)/shard_map/dot_general | solution.py:147
  146.9 3.6 %collective-permute-done.37.refs_7_ = bf16[128,1024]{1,0:T(8,128)(2,1)S(1)} collective-permute-done((bf16[128,1024]{1,0:T(8,128)(2,1)S(1)}, bf16[128,1024]{1,0:T(8,128)(2,1)S(1)}, u32[]{:S(2)}, u32[]{:S(2)}) %collective-permute-start.37) | collective-permute-done | bytes 262176 | tf_op jit(solution)/shard_map/ppermute | solution.py:203
  150.4 2.3 %subtract_convert_fusion = bf16[128,2048]{1,0:T(8,128)(2,1)} fusion(bf16[128,2048]{1,0:T(8,128)(2,1)S(1)} %collective-permute-done.28, bf16[128,1024]{1,0:T(8,128)(2,1)S(1)} %collective-permute-done.37.refs_7_, bf16[2048,1024]{1,0:T(8,128)(2,1)S(1)} %copy-done), kind=kOutput, calls=%fused_computation.19 | convolution fusion | flops 537657344 | bytes 5505024 | tf_op jit(solution)/shard_map/dot_general | solution.py:147
  152.9 2.0 %shard_map.51 = bf16[1024,1024]{1,0:T(8,128)(2,1)} custom-call(s32[8]{0:T(128)S(1)} %stack.35.start_ref, bf16[128,1024]{1,0:T(8,128)(2,1)S(1)} %constant_dynamic-update-slice_fusion.12.refs_0_, bf16[128,1024]{1,0:T(8,128)(2,1)S(1)} %collective-permute-done.7.refs_1_, bf16[128,1024]{1,0:T(8,128)(2,1)S(1)} %constant_dynamic-update-slice_fusion.8.refs_2_, ...), custom_call_target="tpu_custom_call" | custom-call | bytes 4194304 | tf_op jit(solution)/shard_map/pallas_call | solution.py:97
  154.9 0.8 collective-permute-done.38
  155.7 5.9 %collective-permute-done.39 = bf16[128,2048]{1,0:T(8,128)(2,1)S(1)} collective-permute-done((bf16[128,2048]{1,0:T(8,128)(2,1)}, bf16[128,2048]{1,0:T(8,128)(2,1)S(1)}, u32[]{:S(2)}, u32[]{:S(2)}) %collective-permute-start.39) | collective-permute-done | bytes 524320 | tf_op jit(solution)/shard_map/ppermute | solution.py:208
  161.9 1.8 %copy.5 = f32[2048,256]{1,0:T(8,128)} copy(f32[2048,256]{0,1:T(8,128)S(1)} %convert_bitcast_fusion) | data formatting | bytes 4194304
  (87 shorter events, 16.9 us)
Async XLA Ops:
  5.7 9.5 %collective-permute-start = (bf16[128,1024]{1,0:T(8,128)(2,1)}, bf16[128,1024]{1,0:T(8,128)(2,1)S(1)}, u32[]{:S(2)}, u32[]{:S(2)}) collective-permute-start(bf16[128,1024]{1,0:T(8,128)(2,1)} %get-tuple-element.16), channel_id=1, source_target_pairs={{0,1},{1,0},{2,3},{3,2},{4,5},{5,4},{6,7},{7,6},{8,9},{9,8},{10,11... | collective-permute-start | bytes 786440 | tf_op jit(solution)/shard_map/ppermute | solution.py:193
  8.7 6.5 %copy-start.6 = (f32[128,1024]{1,0:T(8,128)S(1)}, f32[128,1024]{1,0:T(8,128)}, u32[]{:S(2)}) copy-start(f32[128,1024]{1,0:T(8,128)} %get-tuple-element.18) | copy-start | bytes 1572868
  13.2 50.8 %copy-start.1 = (bf16[1024,1024]{1,0:T(8,128)(2,1)}, bf16[1024,1024]{1,0:T(8,128)(2,1)S(1)}, u32[]{:S(2)}) copy-start(bf16[1024,1024]{1,0:T(8,128)(2,1)S(1)} %get-tuple-element.21) | copy-start | bytes 6291460
  15.3 6.6 %collective-permute-start.1 = (bf16[32,1024]{1,0:T(8,128)(2,1)S(1)}, bf16[32,1024]{1,0:T(8,128)(2,1)S(1)}, u32[]{:S(2)}, u32[]{:S(2)}) collective-permute-start(bf16[32,1024]{1,0:T(8,128)(2,1)S(1)} %get-tuple-element.53), channel_id=1, source_target_pairs={{0,6},{1,7},{2,4},{3,5},{4,2},{5,3},{6,0},{7,1},{8,14},{9,15},{10,... | collective-permute-start | bytes 196616 | tf_op jit(solution)/shard_map/ppermute | solution.py:161
  19.2 5.4 %collective-permute-start.2 = (bf16[32,1024]{1,0:T(8,128)(2,1)S(1)}, bf16[32,1024]{1,0:T(8,128)(2,1)S(1)}, u32[]{:S(2)}, u32[]{:S(2)}) collective-permute-start(bf16[32,1024]{1,0:T(8,128)(2,1)S(1)} %get-tuple-element.55), channel_id=1, source_target_pairs={{0,4},{1,5},{2,6},{3,7},{4,0},{5,1},{6,2},{7,3},{8,12},{9,13},{10,... | collective-permute-start | bytes 196616 | tf_op jit(solution)/shard_map/ppermute | solution.py:161
  19.2 5.4 %collective-permute-start.3 = (bf16[32,1024]{1,0:T(8,128)(2,1)S(1)}, bf16[32,1024]{1,0:T(8,128)(2,1)S(1)}, u32[]{:S(2)}, u32[]{:S(2)}) collective-permute-start(bf16[32,1024]{1,0:T(8,128)(2,1)S(1)} %get-tuple-element.54), channel_id=1, source_target_pairs={{0,2},{1,3},{2,0},{3,1},{4,6},{5,7},{6,4},{7,5},{8,10},{9,11},{10,... | collective-permute-start | bytes 196616 | tf_op jit(solution)/shard_map/ppermute | solution.py:161
  19.8 17.3 %copy-start = (bf16[2048,1024]{1,0:T(8,128)(2,1)S(1)}, bf16[2048,1024]{1,0:T(8,128)(2,1)}, u32[]{:S(2)}) copy-start(bf16[2048,1024]{1,0:T(8,128)(2,1)} %x_ref.1) | copy-start | bytes 12582916
  19.8 17.3 %copy-start.5 = (f32[128,2048]{1,0:T(8,128)S(1)}, f32[128,2048]{1,0:T(8,128)}, u32[]{:S(2)}) copy-start(f32[128,2048]{1,0:T(8,128)} %get-tuple-element.22) | copy-start | bytes 3145732
  27.0 15.0 %copy-start.4 = (f32[128,2048]{1,0:T(8,128)S(1)}, f32[128,2048]{1,0:T(8,128)}, u32[]{:S(2)}) copy-start(f32[128,2048]{1,0:T(8,128)} %get-tuple-element.23) | copy-start | bytes 3145732
  27.7 6.1 %collective-permute-start.4 = (bf16[32,1024]{1,0:T(8,128)(2,1)S(1)}, bf16[32,1024]{1,0:T(8,128)(2,1)S(1)}, u32[]{:S(2)}, u32[]{:S(2)}) collective-permute-start(bf16[32,1024]{1,0:T(8,128)(2,1)S(1)} %get-tuple-element.57), channel_id=1, source_target_pairs={{0,6},{1,7},{2,4},{3,5},{4,2},{5,3},{6,0},{7,1},{8,14},{9,15},{10,... | collective-permute-start | bytes 196616 | tf_op jit(solution)/shard_map/ppermute | solution.py:173
  30.0 5.5 %collective-permute-start.5 = (bf16[32,1024]{1,0:T(8,128)(2,1)S(1)}, bf16[32,1024]{1,0:T(8,128)(2,1)S(1)}, u32[]{:S(2)}, u32[]{:S(2)}) collective-permute-start(bf16[32,1024]{1,0:T(8,128)(2,1)S(1)} %get-tuple-element.57), channel_id=1, source_target_pairs={{0,4},{1,5},{2,6},{3,7},{4,0},{5,1},{6,2},{7,3},{8,12},{9,13},{10,... | collective-permute-start | bytes 196616 | tf_op jit(solution)/shard_map/ppermute | solution.py:173
  30.0 5.5 %collective-permute-start.6 = (bf16[32,1024]{1,0:T(8,128)(2,1)S(1)}, bf16[32,1024]{1,0:T(8,128)(2,1)S(1)}, u32[]{:S(2)}, u32[]{:S(2)}) collective-permute-start(bf16[32,1024]{1,0:T(8,128)(2,1)S(1)} %get-tuple-element.57), channel_id=1, source_target_pairs={{0,2},{1,3},{2,0},{3,1},{4,6},{5,7},{6,4},{7,5},{8,10},{9,11},{10,... | collective-permute-start | bytes 196616 | tf_op jit(solution)/shard_map/ppermute | solution.py:173
  35.5 6.4 %collective-permute-start.7 = (bf16[128,1024]{1,0:T(8,128)(2,1)S(1)}, bf16[128,1024]{1,0:T(8,128)(2,1)S(1)}, u32[]{:S(2)}, u32[]{:S(2)}) collective-permute-start(bf16[128,1024]{1,0:T(8,128)(2,1)S(1)} %constant_dynamic-update-slice_fusion.12.refs_0_), channel_id=1, source_target_pairs={{0,1},{1,0},{2,3},{3,2},{4,5},{5,4},{6,7},{7,6},{8,9},{9,8},{10,11... | collective-permute-start | bytes 786440 | tf_op jit(solution)/shard_map/ppermute | solution.py:203
  38.6 8.7 %collective-permute-start.8 = (bf16[128,2048]{1,0:T(8,128)(2,1)S(1)}, bf16[128,2048]{1,0:T(8,128)(2,1)S(1)}, u32[]{:S(2)}, u32[]{:S(2)}) collective-permute-start(bf16[128,2048]{1,0:T(8,128)(2,1)S(1)} %fusion.1), channel_id=1, source_target_pairs={{0,8},{8,16},{16,24},{24,0},{1,9},{9,17},{17,25},{25,1},{2,10},{10... | collective-permute-start | bytes 1572872 | tf_op jit(solution)/shard_map/ppermute | solution.py:208
  43.5 9.4 %collective-permute-start.10 = (bf16[128,2048]{1,0:T(8,128)(2,1)S(1)}, bf16[128,2048]{1,0:T(8,128)(2,1)S(1)}, u32[]{:S(2)}, u32[]{:S(2)}) collective-permute-start(bf16[128,2048]{1,0:T(8,128)(2,1)S(1)} %fusion.2), channel_id=1, source_target_pairs={{0,8},{8,16},{16,24},{24,0},{1,9},{9,17},{17,25},{25,1},{2,10},{10... | collective-permute-start | bytes 1572872 | tf_op jit(solution)/shard_map/ppermute | solution.py:208
  48.0 15.2 %copy-start.3 = (bf16[1024,1024]{1,0:T(8,128)(2,1)S(1)}, bf16[1024,1024]{1,0:T(8,128)(2,1)}, u32[]{:S(2)}) copy-start(bf16[1024,1024]{1,0:T(8,128)(2,1)} %get-tuple-element.20) | copy-start | bytes 6291460
  48.0 7.4 %collective-permute-start.9 = (bf16[128,1024]{1,0:T(8,128)(2,1)S(1)}, bf16[128,1024]{1,0:T(8,128)(2,1)S(1)}, u32[]{:S(2)}, u32[]{:S(2)}) collective-permute-start(bf16[128,1024]{1,0:T(8,128)(2,1)S(1)} %convolution_convert_fusion.2), channel_id=1, source_target_pairs={{0,1},{1,0},{2,3},{3,2},{4,5},{5,4},{6,7},{7,6},{8,9},{9,8},{10,11... | collective-permute-start | bytes 786440 | tf_op jit(solution)/shard_map/ppermute | solution.py:193
  55.5 6.2 %collective-permute-start.11 = (bf16[32,1024]{1,0:T(8,128)(2,1)S(1)}, bf16[32,1024]{1,0:T(8,128)(2,1)S(1)}, u32[]{:S(2)}, u32[]{:S(2)}) collective-permute-start(bf16[32,1024]{1,0:T(8,128)(2,1)S(1)} %get-tuple-element.50), channel_id=1, source_target_pairs={{0,6},{1,7},{2,4},{3,5},{4,2},{5,3},{6,0},{7,1},{8,14},{9,15},{10,... | collective-permute-start | bytes 196616 | tf_op jit(solution)/shard_map/ppermute | solution.py:161
  57.6 5.5 %collective-permute-start.12 = (bf16[32,1024]{1,0:T(8,128)(2,1)S(1)}, bf16[32,1024]{1,0:T(8,128)(2,1)S(1)}, u32[]{:S(2)}, u32[]{:S(2)}) collective-permute-start(bf16[32,1024]{1,0:T(8,128)(2,1)S(1)} %get-tuple-element.52), channel_id=1, source_target_pairs={{0,4},{1,5},{2,6},{3,7},{4,0},{5,1},{6,2},{7,3},{8,12},{9,13},{10,... | collective-permute-start | bytes 196616 | tf_op jit(solution)/shard_map/ppermute | solution.py:161
  58.0 5.2 %collective-permute-start.13 = (bf16[32,1024]{1,0:T(8,128)(2,1)S(1)}, bf16[32,1024]{1,0:T(8,128)(2,1)S(1)}, u32[]{:S(2)}, u32[]{:S(2)}) collective-permute-start(bf16[32,1024]{1,0:T(8,128)(2,1)S(1)} %get-tuple-element.51), channel_id=1, source_target_pairs={{0,2},{1,3},{2,0},{3,1},{4,6},{5,7},{6,4},{7,5},{8,10},{9,11},{10,... | collective-permute-start | bytes 196616 | tf_op jit(solution)/shard_map/ppermute | solution.py:161
  64.7 6.1 %collective-permute-start.14 = (bf16[32,1024]{1,0:T(8,128)(2,1)S(1)}, bf16[32,1024]{1,0:T(8,128)(2,1)S(1)}, u32[]{:S(2)}, u32[]{:S(2)}) collective-permute-start(bf16[32,1024]{1,0:T(8,128)(2,1)S(1)} %get-tuple-element.59), channel_id=1, source_target_pairs={{0,6},{1,7},{2,4},{3,5},{4,2},{5,3},{6,0},{7,1},{8,14},{9,15},{10,... | collective-permute-start | bytes 196616 | tf_op jit(solution)/shard_map/ppermute | solution.py:173
  66.8 5.5 %collective-permute-start.15 = (bf16[32,1024]{1,0:T(8,128)(2,1)S(1)}, bf16[32,1024]{1,0:T(8,128)(2,1)S(1)}, u32[]{:S(2)}, u32[]{:S(2)}) collective-permute-start(bf16[32,1024]{1,0:T(8,128)(2,1)S(1)} %get-tuple-element.59), channel_id=1, source_target_pairs={{0,4},{1,5},{2,6},{3,7},{4,0},{5,1},{6,2},{7,3},{8,12},{9,13},{10,... | collective-permute-start | bytes 196616 | tf_op jit(solution)/shard_map/ppermute | solution.py:173
  67.3 5.0 %collective-permute-start.16 = (bf16[32,1024]{1,0:T(8,128)(2,1)S(1)}, bf16[32,1024]{1,0:T(8,128)(2,1)S(1)}, u32[]{:S(2)}, u32[]{:S(2)}) collective-permute-start(bf16[32,1024]{1,0:T(8,128)(2,1)S(1)} %get-tuple-element.59), channel_id=1, source_target_pairs={{0,2},{1,3},{2,0},{3,1},{4,6},{5,7},{6,4},{7,5},{8,10},{9,11},{10,... | collective-permute-start | bytes 196616 | tf_op jit(solution)/shard_map/ppermute | solution.py:173
  72.4 6.4 %collective-permute-start.17 = (bf16[128,1024]{1,0:T(8,128)(2,1)S(1)}, bf16[128,1024]{1,0:T(8,128)(2,1)S(1)}, u32[]{:S(2)}, u32[]{:S(2)}) collective-permute-start(bf16[128,1024]{1,0:T(8,128)(2,1)S(1)} %constant_dynamic-update-slice_fusion.8.refs_2_), channel_id=1, source_target_pairs={{0,1},{1,0},{2,3},{3,2},{4,5},{5,4},{6,7},{7,6},{8,9},{9,8},{10,11... | collective-permute-start | bytes 786440 | tf_op jit(solution)/shard_map/ppermute | solution.py:203
  74.4 8.7 %collective-permute-start.18 = (bf16[128,2048]{1,0:T(8,128)(2,1)S(1)}, bf16[128,2048]{1,0:T(8,128)(2,1)S(1)}, u32[]{:S(2)}, u32[]{:S(2)}) collective-permute-start(bf16[128,2048]{1,0:T(8,128)(2,1)S(1)} %subtract_convert_fusion.5), channel_id=1, source_target_pairs={{0,8},{8,16},{16,24},{24,0},{1,9},{9,17},{17,25},{25,1},{2,10},{10... | collective-permute-start | bytes 1572872 | tf_op jit(solution)/shard_map/ppermute | solution.py:208
  80.3 8.8 %collective-permute-start.20 = (bf16[128,2048]{1,0:T(8,128)(2,1)S(1)}, bf16[128,2048]{1,0:T(8,128)(2,1)S(1)}, u32[]{:S(2)}, u32[]{:S(2)}) collective-permute-start(bf16[128,2048]{1,0:T(8,128)(2,1)S(1)} %subtract_convert_fusion.4), channel_id=1, source_target_pairs={{0,8},{8,16},{16,24},{24,0},{1,9},{9,17},{17,25},{25,1},{2,10},{10... | collective-permute-start | bytes 1572872 | tf_op jit(solution)/shard_map/ppermute | solution.py:208
  83.8 15.0 %copy-start.2 = (bf16[1024,1024]{1,0:T(8,128)(2,1)S(1)}, bf16[1024,1024]{1,0:T(8,128)(2,1)}, u32[]{:S(2)}) copy-start(bf16[1024,1024]{1,0:T(8,128)(2,1)} %copy-done.1) | copy-start | bytes 6291460
  83.8 6.4 %collective-permute-start.19 = (bf16[128,1024]{1,0:T(8,128)(2,1)S(1)}, bf16[128,1024]{1,0:T(8,128)(2,1)S(1)}, u32[]{:S(2)}, u32[]{:S(2)}) collective-permute-start(bf16[128,1024]{1,0:T(8,128)(2,1)S(1)} %convolution_convert_fusion.1), channel_id=1, source_target_pairs={{0,1},{1,0},{2,3},{3,2},{4,5},{5,4},{6,7},{7,6},{8,9},{9,8},{10,11... | collective-permute-start | bytes 786440 | tf_op jit(solution)/shard_map/ppermute | solution.py:193
  90.4 6.1 %collective-permute-start.21 = (bf16[32,1024]{1,0:T(8,128)(2,1)S(1)}, bf16[32,1024]{1,0:T(8,128)(2,1)S(1)}, u32[]{:S(2)}, u32[]{:S(2)}) collective-permute-start(bf16[32,1024]{1,0:T(8,128)(2,1)S(1)} %get-tuple-element.47), channel_id=1, source_target_pairs={{0,6},{1,7},{2,4},{3,5},{4,2},{5,3},{6,0},{7,1},{8,14},{9,15},{10,... | collective-permute-start | bytes 196616 | tf_op jit(solution)/shard_map/ppermute | solution.py:161
  92.5 5.5 %collective-permute-start.22 = (bf16[32,1024]{1,0:T(8,128)(2,1)S(1)}, bf16[32,1024]{1,0:T(8,128)(2,1)S(1)}, u32[]{:S(2)}, u32[]{:S(2)}) collective-permute-start(bf16[32,1024]{1,0:T(8,128)(2,1)S(1)} %get-tuple-element.49), channel_id=1, source_target_pairs={{0,4},{1,5},{2,6},{3,7},{4,0},{5,1},{6,2},{7,3},{8,12},{9,13},{10,... | collective-permute-start | bytes 196616 | tf_op jit(solution)/shard_map/ppermute | solution.py:161
  93.0 5.0 %collective-permute-start.23 = (bf16[32,1024]{1,0:T(8,128)(2,1)S(1)}, bf16[32,1024]{1,0:T(8,128)(2,1)S(1)}, u32[]{:S(2)}, u32[]{:S(2)}) collective-permute-start(bf16[32,1024]{1,0:T(8,128)(2,1)S(1)} %get-tuple-element.48), channel_id=1, source_target_pairs={{0,2},{1,3},{2,0},{3,1},{4,6},{5,7},{6,4},{7,5},{8,10},{9,11},{10,... | collective-permute-start | bytes 196616 | tf_op jit(solution)/shard_map/ppermute | solution.py:161
  99.5 6.1 %collective-permute-start.24 = (bf16[32,1024]{1,0:T(8,128)(2,1)S(1)}, bf16[32,1024]{1,0:T(8,128)(2,1)S(1)}, u32[]{:S(2)}, u32[]{:S(2)}) collective-permute-start(bf16[32,1024]{1,0:T(8,128)(2,1)S(1)} %get-tuple-element.61), channel_id=1, source_target_pairs={{0,6},{1,7},{2,4},{3,5},{4,2},{5,3},{6,0},{7,1},{8,14},{9,15},{10,... | collective-permute-start | bytes 196616 | tf_op jit(solution)/shard_map/ppermute | solution.py:173
  101.6 5.5 %collective-permute-start.25 = (bf16[32,1024]{1,0:T(8,128)(2,1)S(1)}, bf16[32,1024]{1,0:T(8,128)(2,1)S(1)}, u32[]{:S(2)}, u32[]{:S(2)}) collective-permute-start(bf16[32,1024]{1,0:T(8,128)(2,1)S(1)} %get-tuple-element.61), channel_id=1, source_target_pairs={{0,4},{1,5},{2,6},{3,7},{4,0},{5,1},{6,2},{7,3},{8,12},{9,13},{10,... | collective-permute-start | bytes 196616 | tf_op jit(solution)/shard_map/ppermute | solution.py:173
  102.2 5.0 %collective-permute-start.26 = (bf16[32,1024]{1,0:T(8,128)(2,1)S(1)}, bf16[32,1024]{1,0:T(8,128)(2,1)S(1)}, u32[]{:S(2)}, u32[]{:S(2)}) collective-permute-start(bf16[32,1024]{1,0:T(8,128)(2,1)S(1)} %get-tuple-element.61), channel_id=1, source_target_pairs={{0,2},{1,3},{2,0},{3,1},{4,6},{5,7},{6,4},{7,5},{8,10},{9,11},{10,... | collective-permute-start | bytes 196616 | tf_op jit(solution)/shard_map/ppermute | solution.py:173
  107.2 6.4 %collective-permute-start.27 = (bf16[128,1024]{1,0:T(8,128)(2,1)S(1)}, bf16[128,1024]{1,0:T(8,128)(2,1)S(1)}, u32[]{:S(2)}, u32[]{:S(2)}) collective-permute-start(bf16[128,1024]{1,0:T(8,128)(2,1)S(1)} %constant_dynamic-update-slice_fusion.4.refs_4_), channel_id=1, source_target_pairs={{0,1},{1,0},{2,3},{3,2},{4,5},{5,4},{6,7},{7,6},{8,9},{9,8},{10,11... | collective-permute-start | bytes 786440 | tf_op jit(solution)/shard_map/ppermute | solution.py:203
  110.3 8.7 %collective-permute-start.28 = (bf16[128,2048]{1,0:T(8,128)(2,1)S(1)}, bf16[128,2048]{1,0:T(8,128)(2,1)S(1)}, u32[]{:S(2)}, u32[]{:S(2)}) collective-permute-start(bf16[128,2048]{1,0:T(8,128)(2,1)S(1)} %subtract_convert_fusion.3), channel_id=1, source_target_pairs={{0,8},{8,16},{16,24},{24,0},{1,9},{9,17},{17,25},{25,1},{2,10},{10... | collective-permute-start | bytes 1572872 | tf_op jit(solution)/shard_map/ppermute | solution.py:208
  115.1 9.4 %collective-permute-start.30 = (bf16[128,2048]{1,0:T(8,128)(2,1)S(1)}, bf16[128,2048]{1,0:T(8,128)(2,1)S(1)}, u32[]{:S(2)}, u32[]{:S(2)}) collective-permute-start(bf16[128,2048]{1,0:T(8,128)(2,1)S(1)} %subtract_convert_fusion.2), channel_id=1, source_target_pairs={{0,8},{8,16},{16,24},{24,0},{1,9},{9,17},{17,25},{25,1},{2,10},{10... | collective-permute-start | bytes 1572872 | tf_op jit(solution)/shard_map/ppermute | solution.py:208
  119.7 7.4 %collective-permute-start.29 = (bf16[128,1024]{1,0:T(8,128)(2,1)S(1)}, bf16[128,1024]{1,0:T(8,128)(2,1)S(1)}, u32[]{:S(2)}, u32[]{:S(2)}) collective-permute-start(bf16[128,1024]{1,0:T(8,128)(2,1)S(1)} %convolution_convert_fusion), channel_id=1, source_target_pairs={{0,1},{1,0},{2,3},{3,2},{4,5},{5,4},{6,7},{7,6},{8,9},{9,8},{10,11... | collective-permute-start | bytes 786440 | tf_op jit(solution)/shard_map/ppermute | solution.py:193
  127.2 6.2 %collective-permute-start.31 = (bf16[32,1024]{1,0:T(8,128)(2,1)S(1)}, bf16[32,1024]{1,0:T(8,128)(2,1)S(1)}, u32[]{:S(2)}, u32[]{:S(2)}) collective-permute-start(bf16[32,1024]{1,0:T(8,128)(2,1)S(1)} %get-tuple-element.44), channel_id=1, source_target_pairs={{0,6},{1,7},{2,4},{3,5},{4,2},{5,3},{6,0},{7,1},{8,14},{9,15},{10,... | collective-permute-start | bytes 196616 | tf_op jit(solution)/shard_map/ppermute | solution.py:161
  129.3 5.5 %collective-permute-start.32 = (bf16[32,1024]{1,0:T(8,128)(2,1)S(1)}, bf16[32,1024]{1,0:T(8,128)(2,1)S(1)}, u32[]{:S(2)}, u32[]{:S(2)}) collective-permute-start(bf16[32,1024]{1,0:T(8,128)(2,1)S(1)} %get-tuple-element.46), channel_id=1, source_target_pairs={{0,4},{1,5},{2,6},{3,7},{4,0},{5,1},{6,2},{7,3},{8,12},{9,13},{10,... | collective-permute-start | bytes 196616 | tf_op jit(solution)/shard_map/ppermute | solution.py:161
  129.8 5.0 %collective-permute-start.33 = (bf16[32,1024]{1,0:T(8,128)(2,1)S(1)}, bf16[32,1024]{1,0:T(8,128)(2,1)S(1)}, u32[]{:S(2)}, u32[]{:S(2)}) collective-permute-start(bf16[32,1024]{1,0:T(8,128)(2,1)S(1)} %get-tuple-element.45), channel_id=1, source_target_pairs={{0,2},{1,3},{2,0},{3,1},{4,6},{5,7},{6,4},{7,5},{8,10},{9,11},{10,... | collective-permute-start | bytes 196616 | tf_op jit(solution)/shard_map/ppermute | solution.py:161
  136.3 6.1 %collective-permute-start.34 = (bf16[32,1024]{1,0:T(8,128)(2,1)S(1)}, bf16[32,1024]{1,0:T(8,128)(2,1)S(1)}, u32[]{:S(2)}, u32[]{:S(2)}) collective-permute-start(bf16[32,1024]{1,0:T(8,128)(2,1)S(1)} %get-tuple-element.63), channel_id=1, source_target_pairs={{0,6},{1,7},{2,4},{3,5},{4,2},{5,3},{6,0},{7,1},{8,14},{9,15},{10,... | collective-permute-start | bytes 196616 | tf_op jit(solution)/shard_map/ppermute | solution.py:173
  138.4 5.5 %collective-permute-start.35 = (bf16[32,1024]{1,0:T(8,128)(2,1)S(1)}, bf16[32,1024]{1,0:T(8,128)(2,1)S(1)}, u32[]{:S(2)}, u32[]{:S(2)}) collective-permute-start(bf16[32,1024]{1,0:T(8,128)(2,1)S(1)} %get-tuple-element.63), channel_id=1, source_target_pairs={{0,4},{1,5},{2,6},{3,7},{4,0},{5,1},{6,2},{7,3},{8,12},{9,13},{10,... | collective-permute-start | bytes 196616 | tf_op jit(solution)/shard_map/ppermute | solution.py:173
  139.0 5.0 %collective-permute-start.36 = (bf16[32,1024]{1,0:T(8,128)(2,1)S(1)}, bf16[32,1024]{1,0:T(8,128)(2,1)S(1)}, u32[]{:S(2)}, u32[]{:S(2)}) collective-permute-start(bf16[32,1024]{1,0:T(8,128)(2,1)S(1)} %get-tuple-element.63), channel_id=1, source_target_pairs={{0,2},{1,3},{2,0},{3,1},{4,6},{5,7},{6,4},{7,5},{8,10},{9,11},{10,... | collective-permute-start | bytes 196616 | tf_op jit(solution)/shard_map/ppermute | solution.py:173
  144.0 6.4 %collective-permute-start.37 = (bf16[128,1024]{1,0:T(8,128)(2,1)S(1)}, bf16[128,1024]{1,0:T(8,128)(2,1)S(1)}, u32[]{:S(2)}, u32[]{:S(2)}) collective-permute-start(bf16[128,1024]{1,0:T(8,128)(2,1)S(1)} %constant_dynamic-update-slice_fusion.refs_6_), channel_id=1, source_target_pairs={{0,1},{1,0},{2,3},{3,2},{4,5},{5,4},{6,7},{7,6},{8,9},{9,8},{10,11... | collective-permute-start | bytes 786440 | tf_op jit(solution)/shard_map/ppermute | solution.py:203
  146.9 8.8 %collective-permute-start.38 = (bf16[128,2048]{1,0:T(8,128)(2,1)}, bf16[128,2048]{1,0:T(8,128)(2,1)S(1)}, u32[]{:S(2)}, u32[]{:S(2)}) collective-permute-start(bf16[128,2048]{1,0:T(8,128)(2,1)} %subtract_convert_fusion.1), channel_id=1, source_target_pairs={{0,8},{8,16},{16,24},{24,0},{1,9},{9,17},{17,25},{25,1},{2,10},{10... | collective-permute-start | bytes 1572872 | tf_op jit(solution)/shard_map/ppermute | solution.py:208
  152.8 8.8 %collective-permute-start.39 = (bf16[128,2048]{1,0:T(8,128)(2,1)}, bf16[128,2048]{1,0:T(8,128)(2,1)S(1)}, u32[]{:S(2)}, u32[]{:S(2)}) collective-permute-start(bf16[128,2048]{1,0:T(8,128)(2,1)} %subtract_convert_fusion), channel_id=1, source_target_pairs={{0,8},{8,16},{16,24},{24,0},{1,9},{9,17},{17,25},{25,1},{2,10},{10... | collective-permute-start | bytes 1572872 | tf_op jit(solution)/shard_map/ppermute | solution.py:208

commit v4 on v3

--- a/solution.py
+++ b/solution.py
@@ -18,6 +18,7 @@
 
 CHUNK = 1024
 LANES = 128
+TURN_CHUNK = 512
 FIRST_VMEM = 56 * 1024 * 1024
 SCATTER_VMEM = 12 * 1024 * 1024
 
@@ -82,6 +83,25 @@
     )(lead.reshape(1), residual, residual, features)
 
 
+def turn_kernel(x_ref, out_ref):
+    out_ref[...] = x_ref[...].T
+
+
+def turn(features):
+    rows, feat_width = features.shape
+    return pl.pallas_call(
+        turn_kernel,
+        out_shape=jax.ShapeDtypeStruct((feat_width, rows), features.dtype),
+        grid=(rows // TURN_CHUNK,),
+        in_specs=[pl.BlockSpec((TURN_CHUNK, feat_width), lambda i: (i, 0))],
+        out_specs=pl.BlockSpec((feat_width, TURN_CHUNK), lambda i: (0, i)),
+        compiler_params=pltpu.CompilerParams(vmem_limit_bytes=SCATTER_VMEM),
+        cost_estimate=pl.CostEstimate(
+            flops=0, bytes_accessed=4 * rows * feat_width, transcendentals=0
+        ),
+    )(features)
+
+
 def scatter_kernel(pieces, start_ref, *refs):
     updates, out_ref = refs[:pieces], refs[pieces]
     height = updates[0].shape[0]
@@ -108,6 +128,33 @@
             flops=0, bytes_accessed=4 * pieces * height * feat_width, transcendentals=0
         ),
     )(jnp.stack(starts).astype(jnp.int32), *updates)
+
+
+def place_kernel(place_ref, part_ref, *refs):
+    refs[-1][...] = part_ref[...].astype(F32).T
+
+
+def place_columns(part, place, base):
+    half, rows = part.shape
+    operands = (part,) if base is None else (part, base)
+    in_specs = [pl.BlockSpec((half, CHUNK), lambda i, place: (0, i))]
+    if base is not None:
+        in_specs.append(pl.BlockSpec(memory_space=pl.ANY))
+    return pl.pallas_call(
+        place_kernel,
+        out_shape=jax.ShapeDtypeStruct((rows, 2 * half), F32),
+        grid_spec=pltpu.PrefetchScalarGridSpec(
+            num_scalar_prefetch=1,
+            grid=(rows // CHUNK,),
+            in_specs=in_specs,
+            out_specs=pl.BlockSpec((CHUNK, half), lambda i, place: (i, place[0])),
+        ),
+        input_output_aliases={} if base is None else {2: 0},
+        compiler_params=pltpu.CompilerParams(vmem_limit_bytes=SCATTER_VMEM),
+        cost_estimate=pl.CostEstimate(
+            flops=0, bytes_accessed=6 * rows * half, transcendentals=0
+        ),
+    )(place.reshape(1).astype(jnp.int32), *operands)
 
 
 def on_device(features, residual, inverse_grams):
@@ -145,7 +192,7 @@
 
     def subtract(current, update):
         change = lax.dot_general(
-            update, features, (((1,), (1,)), ((), ())), preferred_element_type=F32
+            update, turned, (((1,), (0,)), ((), ())), preferred_element_type=F32
         )
         return current.astype(F32) - change
 
@@ -193,6 +240,7 @@
         arrived = lax.ppermute(term, "rows", partner)
         if visit == 0:
             inverse_high, inverse_low = split_high_low(inverse_grams)
+            turned = turn(features) if kernels else features.T
             arrived, kept, inverse_high, inverse_low = lax.optimization_barrier(
                 (arrived, kept, inverse_high, inverse_low)
             )
@@ -213,6 +261,9 @@
         increments = jnp.zeros((width * blocks, feat_width), BF16)
         for update, start in zip(updates, starts):
             increments = lax.dynamic_update_slice_in_dim(increments, update, start * half, 0)
+    if kernels:
+        final = place_columns(halves[0], lead, None)
+        return increments, place_columns(halves[1], 1 - lead, final)
     first = jnp.where(lead == 0, halves[0], halves[1])
     second = jnp.where(lead == 0, halves[1], halves[0])
     return increments, jnp.concatenate([first, second], 0).astype(F32).T

time: 164 us -> 162 us (0.988)
  matrix products: 25.4 us -> 19.5 us
  Pallas kernels: 7.08 us -> 11.1 us
  waiting for transfers between devices: 76.4 us -> 78.3 us
  local copies, waits for them, and re-layouts: 2.28 us -> 0.47 us
    dot_general x8, matrix products: 13.6 us -> 7.57 us  [subtract(): lax.dot_general(update, turned, (((1,), (0,)), ((), ())), preferred_eleme...]
    pallas_call x0 -> x3, Pallas kernels: none -> 3.95 us  [the longest x2 2.32 us: place_columns(): pl.pallas_call(place_kernel, out_shape=jax.ShapeDtypeStruct((rows, 2 * ha...]
    ppermute x4, waiting for transfers between devices: 14.4 us -> 17.4 us  [on_device(): update_away = lax.ppermute(update_home, 'rows', partner)]
    unnamed x15 -> x14, local copies, waits for them, and re-layouts: 1.85 us -> 0.04 us
  transfers between devices with their start and end apart: 40 -> 40, of which waited for: 32 -> 32; matrix products, arithmetic and copies ran while one was open for 14% -> 10% of each run, Pallas kernels for 1% -> 3%
where the time goes in v4:
time: 162 us
  waiting for transfers between devices  78.3 us (48%)
  starting transfers between devices  46.2 us (29%)
  matrix products  19.5 us (12%)
  Pallas kernels  11.1 us (7%)
  other arithmetic  4.91 us (3%)
    ppermute x8, waiting for transfers between devices, on_device(): lax.ppermute(part.astype(BF16), 'feat', next_block)  27.9 us
    ppermute x12, starting transfers between devices, reduce_outer(): lax.ppermute(out.astype(BF16), 'rows', outer_step(step)).astype(F32)  17.9 us
    ppermute x12, starting transfers between devices, gather_outer(): got = lax.ppermute(update, 'rows', outer_step(step))  17.8 us
    ppermute x4, waiting for transfers between devices, on_device(): update_away = lax.ppermute(update_home, 'rows', partner)  17.4 us
    ppermute x12, waiting for transfers between devices, reduce_outer(): lax.ppermute(out.astype(BF16), 'rows', outer_step(step)).astype(F32)  14.1 us
    ppermute x12, waiting for transfers between devices, gather_outer(): got = lax.ppermute(update, 'rows', outer_step(step))  12.8 us
    dot_general x8, matrix products, subtract(): lax.dot_general(update, turned, (((1,), (0,)), ((), ())), preferred_eleme...  7.57 us
    dot_general x8, matrix products, apply_inverse(): dot = lambda a, b: lax.dot_general(a, b, dims, preferred_element_type=F32)  7.52 us
  transfers between devices with their start and end apart: 40, of which 32 were waited for; matrix products, arithmetic and copies ran while one was open for 10% of the time, Pallas kernels for 3%

profile of v4, /device:TPU:0, one launch (start us, length us, event | category | flops | bytes accessed | tf_op | source)
XLA Modules:
  0.0 161.5 jit_solution(18007986027047711072)
XLA Ops:
  0.6 5.1 %shard_map.50 = (bf16[128,1024]{1,0:T(8,128)(2,1)}, f32[128,1024]{1,0:T(8,128)}, f32[128,2048]{1,0:T(8,128)}, f32[128,2048]{1,0:T(8,128)}) custom-call(s32[1]{0:T(128)} %bitcast.8.lead_ref.place_ref, f32[2048,256]{1,0:T(8,128)} %home_ref.1, f32[2048,256]{1,0:T(8,128)} %home_ref.1, bf16[2048,1024]{1,0:T(8,128)(2,1)} %x_ref.3), custom_call_target="tpu_custom_call" | custom-call | flops 1073741824 | bytes 9175040 | tf_op jit(solution)/shard_map/pallas_call | solution.py:53
  5.8 3.0 %collective-permute-start = (bf16[128,1024]{1,0:T(8,128)(2,1)}, bf16[128,1024]{1,0:T(8,128)(2,1)S(1)}, u32[]{:S(2)}, u32[]{:S(2)}) collective-permute-start(bf16[128,1024]{1,0:T(8,128)(2,1)} %get-tuple-element.16), channel_id=1, source_target_pairs={{0,1},{1,0},{2,3},{3,2},{4,5},{5,4},{6,7},{7,6},{8,9},{9,8},{10,11... | collective-permute-start | bytes 786440 | tf_op jit(solution)/shard_map/ppermute | solution.py:240
  8.7 4.5 %fusion = (bf16[1024,1024]{1,0:T(8,128)(2,1)S(1)}, bf16[1024,1024]{1,0:T(8,128)(2,1)}) fusion(f32[1024,1024]{1,0:T(8,128)} %param.5), kind=kLoop, calls=%fused_computation.2 | loop fusion | flops 4194304 | bytes 8388608 | tf_op jit(solution)/shard_map/convert_element_type | solution.py:16
  13.2 2.0 %collective-permute-done = bf16[128,1024]{1,0:T(8,128)(2,1)S(1)} collective-permute-done((bf16[128,1024]{1,0:T(8,128)(2,1)}, bf16[128,1024]{1,0:T(8,128)(2,1)S(1)}, u32[]{:S(2)}, u32[]{:S(2)}) %collective-permute-start) | collective-permute-done | bytes 262176 | tf_op jit(solution)/shard_map/ppermute | solution.py:240
  15.4 3.9 %collective-permute-start.1 = (bf16[32,1024]{1,0:T(8,128)(2,1)S(1)}, bf16[32,1024]{1,0:T(8,128)(2,1)S(1)}, u32[]{:S(2)}, u32[]{:S(2)}) collective-permute-start(bf16[32,1024]{1,0:T(8,128)(2,1)S(1)} %get-tuple-element.49), channel_id=1, source_target_pairs={{0,6},{1,7},{2,4},{3,5},{4,2},{5,3},{6,0},{7,1},{8,14},{9,15},{10,... | collective-permute-start | bytes 196616 | tf_op jit(solution)/shard_map/ppermute | solution.py:208
  19.9 2.0 %collective-permute-done.1 = bf16[32,1024]{1,0:T(8,128)(2,1)S(1)} collective-permute-done((bf16[32,1024]{1,0:T(8,128)(2,1)S(1)}, bf16[32,1024]{1,0:T(8,128)(2,1)S(1)}, u32[]{:S(2)}, u32[]{:S(2)}) %collective-permute-start.1) | collective-permute-done | bytes 65568 | tf_op jit(solution)/shard_map/ppermute | solution.py:208
  21.9 2.7 %collective-permute-done.2 = bf16[32,1024]{1,0:T(8,128)(2,1)S(1)} collective-permute-done((bf16[32,1024]{1,0:T(8,128)(2,1)S(1)}, bf16[32,1024]{1,0:T(8,128)(2,1)S(1)}, u32[]{:S(2)}, u32[]{:S(2)}) %collective-permute-start.2) | collective-permute-done | bytes 65568 | tf_op jit(solution)/shard_map/ppermute | solution.py:208
  24.7 2.4 %fusion.11 = f32[64,1024]{1,0:T(8,128)S(1)} fusion(bf16[1024,1024]{1,0:T(8,128)(2,1)} %get-tuple-element.20, bf16[32,1024]{1,0:T(8,128)(2,1)S(1)} %get-tuple-element.38, bf16[32,1024]{1,0:T(8,128)(2,1)S(1)} %get-tuple-element.39), kind=kOutput, calls=%fused_computation.44 | convolution fusion | flops 134479872 | bytes 2490368 | tf_op jit(solution)/shard_map/dot_general | solution.py:189
  27.8 2.3 %collective-permute-start.4 = (bf16[32,1024]{1,0:T(8,128)(2,1)S(1)}, bf16[32,1024]{1,0:T(8,128)(2,1)S(1)}, u32[]{:S(2)}, u32[]{:S(2)}) collective-permute-start(bf16[32,1024]{1,0:T(8,128)(2,1)S(1)} %get-tuple-element.53), channel_id=1, source_target_pairs={{0,6},{1,7},{2,4},{3,5},{4,2},{5,3},{6,0},{7,1},{8,14},{9,15},{10,... | collective-permute-start | bytes 196616 | tf_op jit(solution)/shard_map/ppermute | solution.py:220
  30.1 1.6 %shard_map.51 = bf16[1024,2048]{1,0:T(8,128)(2,1)S(1)} custom-call(bf16[2048,1024]{1,0:T(8,128)(2,1)S(1)} %copy-done), custom_call_target="tpu_custom_call" | custom-call | bytes 8388608 | tf_op jit(solution)/shard_map/pallas_call | solution.py:92
  31.8 2.2 %collective-permute-start.6 = (bf16[32,1024]{1,0:T(8,128)(2,1)S(1)}, bf16[32,1024]{1,0:T(8,128)(2,1)S(1)}, u32[]{:S(2)}, u32[]{:S(2)}) collective-permute-start(bf16[32,1024]{1,0:T(8,128)(2,1)S(1)} %get-tuple-element.53), channel_id=1, source_target_pairs={{0,2},{1,3},{2,0},{3,1},{4,6},{5,7},{6,4},{7,5},{8,10},{9,11},{10,... | collective-permute-start | bytes 196616 | tf_op jit(solution)/shard_map/ppermute | solution.py:220
  34.6 2.7 %collective-permute-done.5 = bf16[32,1024]{1,0:T(8,128)(2,1)S(1)} collective-permute-done((bf16[32,1024]{1,0:T(8,128)(2,1)S(1)}, bf16[32,1024]{1,0:T(8,128)(2,1)S(1)}, u32[]{:S(2)}, u32[]{:S(2)}) %collective-permute-start.5) | collective-permute-done | bytes 65568 | tf_op jit(solution)/shard_map/ppermute | solution.py:220
  37.3 1.6 collective-permute-start.7
  38.9 0.7 fusion.1
  39.7 4.0 %collective-permute-done.7.refs_1_ = bf16[128,1024]{1,0:T(8,128)(2,1)S(1)} collective-permute-done((bf16[128,1024]{1,0:T(8,128)(2,1)S(1)}, bf16[128,1024]{1,0:T(8,128)(2,1)S(1)}, u32[]{:S(2)}, u32[]{:S(2)}) %collective-permute-start.7) | collective-permute-done | bytes 262176 | tf_op jit(solution)/shard_map/ppermute | solution.py:251
  43.8 0.7 fusion.2
  44.6 3.7 %collective-permute-done.8 = bf16[128,2048]{1,0:T(8,128)(2,1)S(1)} collective-permute-done((bf16[128,2048]{1,0:T(8,128)(2,1)S(1)}, bf16[128,2048]{1,0:T(8,128)(2,1)S(1)}, u32[]{:S(2)}, u32[]{:S(2)}) %collective-permute-start.8) | collective-permute-done | bytes 524320 | tf_op jit(solution)/shard_map/ppermute | solution.py:256
  49.6 4.3 %collective-permute-done.10 = bf16[128,2048]{1,0:T(8,128)(2,1)S(1)} collective-permute-done((bf16[128,2048]{1,0:T(8,128)(2,1)S(1)}, bf16[128,2048]{1,0:T(8,128)(2,1)S(1)}, u32[]{:S(2)}, u32[]{:S(2)}) %collective-permute-start.10) | collective-permute-done | bytes 524320 | tf_op jit(solution)/shard_map/ppermute | solution.py:256
  54.7 1.8 %collective-permute-done.9 = bf16[128,1024]{1,0:T(8,128)(2,1)S(1)} collective-permute-done((bf16[128,1024]{1,0:T(8,128)(2,1)S(1)}, bf16[128,1024]{1,0:T(8,128)(2,1)S(1)}, u32[]{:S(2)}, u32[]{:S(2)}) %collective-permute-start.9) | collective-permute-done | bytes 262176 | tf_op jit(solution)/shard_map/ppermute | solution.py:240
  56.6 2.0 %collective-permute-start.11 = (bf16[32,1024]{1,0:T(8,128)(2,1)S(1)}, bf16[32,1024]{1,0:T(8,128)(2,1)S(1)}, u32[]{:S(2)}, u32[]{:S(2)}) collective-permute-start(bf16[32,1024]{1,0:T(8,128)(2,1)S(1)} %get-tuple-element.46), channel_id=1, source_target_pairs={{0,6},{1,7},{2,4},{3,5},{4,2},{5,3},{6,0},{7,1},{8,14},{9,15},{10,... | collective-permute-start | bytes 196616 | tf_op jit(solution)/shard_map/ppermute | solution.py:208
  59.0 2.0 %collective-permute-start.13 = (bf16[32,1024]{1,0:T(8,128)(2,1)S(1)}, bf16[32,1024]{1,0:T(8,128)(2,1)S(1)}, u32[]{:S(2)}, u32[]{:S(2)}) collective-permute-start(bf16[32,1024]{1,0:T(8,128)(2,1)S(1)} %get-tuple-element.47), channel_id=1, source_target_pairs={{0,2},{1,3},{2,0},{3,1},{4,6},{5,7},{6,4},{7,5},{8,10},{9,11},{10,... | collective-permute-start | bytes 196616 | tf_op jit(solution)/shard_map/ppermute | solution.py:208
  61.0 1.7 %collective-permute-done.11 = bf16[32,1024]{1,0:T(8,128)(2,1)S(1)} collective-permute-done((bf16[32,1024]{1,0:T(8,128)(2,1)S(1)}, bf16[32,1024]{1,0:T(8,128)(2,1)S(1)}, u32[]{:S(2)}, u32[]{:S(2)}) %collective-permute-start.11) | collective-permute-done | bytes 65568 | tf_op jit(solution)/shard_map/ppermute | solution.py:208
  62.7 1.4 collective-permute-done.12
  64.2 0.8 fusion.15
  65.8 2.1 %collective-permute-start.14 = (bf16[32,1024]{1,0:T(8,128)(2,1)S(1)}, bf16[32,1024]{1,0:T(8,128)(2,1)S(1)}, u32[]{:S(2)}, u32[]{:S(2)}) collective-permute-start(bf16[32,1024]{1,0:T(8,128)(2,1)S(1)} %get-tuple-element.55), channel_id=1, source_target_pairs={{0,6},{1,7},{2,4},{3,5},{4,2},{5,3},{6,0},{7,1},{8,14},{9,15},{10,... | collective-permute-start | bytes 196616 | tf_op jit(solution)/shard_map/ppermute | solution.py:220
  68.4 1.8 %collective-permute-start.16 = (bf16[32,1024]{1,0:T(8,128)(2,1)S(1)}, bf16[32,1024]{1,0:T(8,128)(2,1)S(1)}, u32[]{:S(2)}, u32[]{:S(2)}) collective-permute-start(bf16[32,1024]{1,0:T(8,128)(2,1)S(1)} %get-tuple-element.55), channel_id=1, source_target_pairs={{0,2},{1,3},{2,0},{3,1},{4,6},{5,7},{6,4},{7,5},{8,10},{9,11},{10,... | collective-permute-start | bytes 196616 | tf_op jit(solution)/shard_map/ppermute | solution.py:220
  70.2 1.7 %collective-permute-done.14 = bf16[32,1024]{1,0:T(8,128)(2,1)S(1)} collective-permute-done((bf16[32,1024]{1,0:T(8,128)(2,1)S(1)}, bf16[32,1024]{1,0:T(8,128)(2,1)S(1)}, u32[]{:S(2)}, u32[]{:S(2)}) %collective-permute-start.14) | collective-permute-done | bytes 65568 | tf_op jit(solution)/shard_map/ppermute | solution.py:220
  71.9 1.5 collective-permute-done.15
  74.8 5.1 %collective-permute-done.17.refs_3_ = bf16[128,1024]{1,0:T(8,128)(2,1)S(1)} collective-permute-done((bf16[128,1024]{1,0:T(8,128)(2,1)S(1)}, bf16[128,1024]{1,0:T(8,128)(2,1)S(1)}, u32[]{:S(2)}, u32[]{:S(2)}) %collective-permute-start.17) | collective-permute-done | bytes 262176 | tf_op jit(solution)/shard_map/ppermute | solution.py:251
  80.8 2.5 %collective-permute-done.18 = bf16[128,2048]{1,0:T(8,128)(2,1)S(1)} collective-permute-done((bf16[128,2048]{1,0:T(8,128)(2,1)S(1)}, bf16[128,2048]{1,0:T(8,128)(2,1)S(1)}, u32[]{:S(2)}, u32[]{:S(2)}) %collective-permute-start.18) | collective-permute-done | bytes 524320 | tf_op jit(solution)/shard_map/ppermute | solution.py:256
  84.1 1.6 collective-permute-start.19
  85.7 3.7 %collective-permute-done.20 = bf16[128,2048]{1,0:T(8,128)(2,1)S(1)} collective-permute-done((bf16[128,2048]{1,0:T(8,128)(2,1)S(1)}, bf16[128,2048]{1,0:T(8,128)(2,1)S(1)}, u32[]{:S(2)}, u32[]{:S(2)}) %collective-permute-start.20) | collective-permute-done | bytes 524320 | tf_op jit(solution)/shard_map/ppermute | solution.py:256
  90.7 2.0 %collective-permute-start.21 = (bf16[32,1024]{1,0:T(8,128)(2,1)S(1)}, bf16[32,1024]{1,0:T(8,128)(2,1)S(1)}, u32[]{:S(2)}, u32[]{:S(2)}) collective-permute-start(bf16[32,1024]{1,0:T(8,128)(2,1)S(1)} %get-tuple-element.43), channel_id=1, source_target_pairs={{0,6},{1,7},{2,4},{3,5},{4,2},{5,3},{6,0},{7,1},{8,14},{9,15},{10,... | collective-permute-start | bytes 196616 | tf_op jit(solution)/shard_map/ppermute | solution.py:208
  93.3 1.8 %collective-permute-start.23 = (bf16[32,1024]{1,0:T(8,128)(2,1)S(1)}, bf16[32,1024]{1,0:T(8,128)(2,1)S(1)}, u32[]{:S(2)}, u32[]{:S(2)}) collective-permute-start(bf16[32,1024]{1,0:T(8,128)(2,1)S(1)} %get-tuple-element.44), channel_id=1, source_target_pairs={{0,2},{1,3},{2,0},{3,1},{4,6},{5,7},{6,4},{7,5},{8,10},{9,11},{10,... | collective-permute-start | bytes 196616 | tf_op jit(solution)/shard_map/ppermute | solution.py:208
  95.1 1.7 %collective-permute-done.21 = bf16[32,1024]{1,0:T(8,128)(2,1)S(1)} collective-permute-done((bf16[32,1024]{1,0:T(8,128)(2,1)S(1)}, bf16[32,1024]{1,0:T(8,128)(2,1)S(1)}, u32[]{:S(2)}, u32[]{:S(2)}) %collective-permute-start.21) | collective-permute-done | bytes 65568 | tf_op jit(solution)/shard_map/ppermute | solution.py:208
  96.8 1.5 collective-permute-done.22
  98.3 0.8 fusion.19
  99.8 2.1 %collective-permute-start.24 = (bf16[32,1024]{1,0:T(8,128)(2,1)S(1)}, bf16[32,1024]{1,0:T(8,128)(2,1)S(1)}, u32[]{:S(2)}, u32[]{:S(2)}) collective-permute-start(bf16[32,1024]{1,0:T(8,128)(2,1)S(1)} %get-tuple-element.57), channel_id=1, source_target_pairs={{0,6},{1,7},{2,4},{3,5},{4,2},{5,3},{6,0},{7,1},{8,14},{9,15},{10,... | collective-permute-start | bytes 196616 | tf_op jit(solution)/shard_map/ppermute | solution.py:220
  102.5 1.8 %collective-permute-start.26 = (bf16[32,1024]{1,0:T(8,128)(2,1)S(1)}, bf16[32,1024]{1,0:T(8,128)(2,1)S(1)}, u32[]{:S(2)}, u32[]{:S(2)}) collective-permute-start(bf16[32,1024]{1,0:T(8,128)(2,1)S(1)} %get-tuple-element.57), channel_id=1, source_target_pairs={{0,2},{1,3},{2,0},{3,1},{4,6},{5,7},{6,4},{7,5},{8,10},{9,11},{10,... | collective-permute-start | bytes 196616 | tf_op jit(solution)/shard_map/ppermute | solution.py:220
  104.3 1.7 %collective-permute-done.24 = bf16[32,1024]{1,0:T(8,128)(2,1)S(1)} collective-permute-done((bf16[32,1024]{1,0:T(8,128)(2,1)S(1)}, bf16[32,1024]{1,0:T(8,128)(2,1)S(1)}, u32[]{:S(2)}, u32[]{:S(2)}) %collective-permute-start.24) | collective-permute-done | bytes 65568 | tf_op jit(solution)/shard_map/ppermute | solution.py:220
  106.0 1.5 collective-permute-done.25
  107.5 1.6 collective-permute-start.27
  109.9 4.0 %collective-permute-done.27.refs_5_ = bf16[128,1024]{1,0:T(8,128)(2,1)S(1)} collective-permute-done((bf16[128,1024]{1,0:T(8,128)(2,1)S(1)}, bf16[128,1024]{1,0:T(8,128)(2,1)S(1)}, u32[]{:S(2)}, u32[]{:S(2)}) %collective-permute-start.27) | collective-permute-done | bytes 262176 | tf_op jit(solution)/shard_map/ppermute | solution.py:251
  114.7 3.7 %collective-permute-done.28 = bf16[128,2048]{1,0:T(8,128)(2,1)S(1)} collective-permute-done((bf16[128,2048]{1,0:T(8,128)(2,1)S(1)}, bf16[128,2048]{1,0:T(8,128)(2,1)S(1)}, u32[]{:S(2)}, u32[]{:S(2)}) %collective-permute-start.28) | collective-permute-done | bytes 524320 | tf_op jit(solution)/shard_map/ppermute | solution.py:256
  118.5 0.7 convolution_convert_fusion
  119.8 4.3 %collective-permute-done.30 = bf16[128,2048]{1,0:T(8,128)(2,1)S(1)} collective-permute-done((bf16[128,2048]{1,0:T(8,128)(2,1)S(1)}, bf16[128,2048]{1,0:T(8,128)(2,1)S(1)}, u32[]{:S(2)}, u32[]{:S(2)}) %collective-permute-start.30) | collective-permute-done | bytes 524320 | tf_op jit(solution)/shard_map/ppermute | solution.py:256
  124.8 1.8 %collective-permute-done.29 = bf16[128,1024]{1,0:T(8,128)(2,1)S(1)} collective-permute-done((bf16[128,1024]{1,0:T(8,128)(2,1)S(1)}, bf16[128,1024]{1,0:T(8,128)(2,1)S(1)}, u32[]{:S(2)}, u32[]{:S(2)}) %collective-permute-start.29) | collective-permute-done | bytes 262176 | tf_op jit(solution)/shard_map/ppermute | solution.py:240
  126.7 2.0 %collective-permute-start.31 = (bf16[32,1024]{1,0:T(8,128)(2,1)S(1)}, bf16[32,1024]{1,0:T(8,128)(2,1)S(1)}, u32[]{:S(2)}, u32[]{:S(2)}) collective-permute-start(bf16[32,1024]{1,0:T(8,128)(2,1)S(1)} %get-tuple-element.40), channel_id=1, source_target_pairs={{0,6},{1,7},{2,4},{3,5},{4,2},{5,3},{6,0},{7,1},{8,14},{9,15},{10,... | collective-permute-start | bytes 196616 | tf_op jit(solution)/shard_map/ppermute | solution.py:208
  129.3 1.9 %collective-permute-start.33 = (bf16[32,1024]{1,0:T(8,128)(2,1)S(1)}, bf16[32,1024]{1,0:T(8,128)(2,1)S(1)}, u32[]{:S(2)}, u32[]{:S(2)}) collective-permute-start(bf16[32,1024]{1,0:T(8,128)(2,1)S(1)} %get-tuple-element.41), channel_id=1, source_target_pairs={{0,2},{1,3},{2,0},{3,1},{4,6},{5,7},{6,4},{7,5},{8,10},{9,11},{10,... | collective-permute-start | bytes 196616 | tf_op jit(solution)/shard_map/ppermute | solution.py:208
  131.2 1.7 %collective-permute-done.31 = bf16[32,1024]{1,0:T(8,128)(2,1)S(1)} collective-permute-done((bf16[32,1024]{1,0:T(8,128)(2,1)S(1)}, bf16[32,1024]{1,0:T(8,128)(2,1)S(1)}, u32[]{:S(2)}, u32[]{:S(2)}) %collective-permute-start.31) | collective-permute-done | bytes 65568 | tf_op jit(solution)/shard_map/ppermute | solution.py:208
  132.9 1.4 collective-permute-done.32
  134.4 0.8 fusion.23
  135.9 2.1 %collective-permute-start.34 = (bf16[32,1024]{1,0:T(8,128)(2,1)S(1)}, bf16[32,1024]{1,0:T(8,128)(2,1)S(1)}, u32[]{:S(2)}, u32[]{:S(2)}) collective-permute-start(bf16[32,1024]{1,0:T(8,128)(2,1)S(1)} %get-tuple-element.59), channel_id=1, source_target_pairs={{0,6},{1,7},{2,4},{3,5},{4,2},{5,3},{6,0},{7,1},{8,14},{9,15},{10,... | collective-permute-start | bytes 196616 | tf_op jit(solution)/shard_map/ppermute | solution.py:220
  138.5 1.8 %collective-permute-start.36 = (bf16[32,1024]{1,0:T(8,128)(2,1)S(1)}, bf16[32,1024]{1,0:T(8,128)(2,1)S(1)}, u32[]{:S(2)}, u32[]{:S(2)}) collective-permute-start(bf16[32,1024]{1,0:T(8,128)(2,1)S(1)} %get-tuple-element.59), channel_id=1, source_target_pairs={{0,2},{1,3},{2,0},{3,1},{4,6},{5,7},{6,4},{7,5},{8,10},{9,11},{10,... | collective-permute-start | bytes 196616 | tf_op jit(solution)/shard_map/ppermute | solution.py:220
  140.3 1.7 %collective-permute-done.34 = bf16[32,1024]{1,0:T(8,128)(2,1)S(1)} collective-permute-done((bf16[32,1024]{1,0:T(8,128)(2,1)S(1)}, bf16[32,1024]{1,0:T(8,128)(2,1)S(1)}, u32[]{:S(2)}, u32[]{:S(2)}) %collective-permute-start.34) | collective-permute-done | bytes 65568 | tf_op jit(solution)/shard_map/ppermute | solution.py:220
  142.0 1.5 collective-permute-done.35
  144.1 1.6 subtract_convert_fusion
  145.7 4.3 %collective-permute-done.37.refs_7_ = bf16[128,1024]{1,0:T(8,128)(2,1)S(1)} collective-permute-done((bf16[128,1024]{1,0:T(8,128)(2,1)S(1)}, bf16[128,1024]{1,0:T(8,128)(2,1)S(1)}, u32[]{:S(2)}, u32[]{:S(2)}) %collective-permute-start.37) | collective-permute-done | bytes 262176 | tf_op jit(solution)/shard_map/ppermute | solution.py:251
  150.0 1.6 subtract_convert_fusion.1
  151.6 2.0 %shard_map.52 = bf16[1024,1024]{1,0:T(8,128)(2,1)} custom-call(s32[8]{0:T(128)S(1)} %stack.35.start_ref, bf16[128,1024]{1,0:T(8,128)(2,1)S(1)} %constant_dynamic-update-slice_fusion.12.refs_0_, bf16[128,1024]{1,0:T(8,128)(2,1)S(1)} %collective-permute-done.7.refs_1_, bf16[128,1024]{1,0:T(8,128)(2,1)S(1)} %constant_dynamic-update-slice_fusion.8.refs_2_, ...), custom_call_target="tpu_custom_call" | custom-call | bytes 4194304 | tf_op jit(solution)/shard_map/pallas_call | solution.py:117
  153.6 0.8 collective-permute-done.39.part_ref
  154.5 1.2 shard_map.53.refs_0_
  155.6 4.7 %collective-permute-done.38.part_ref = bf16[128,2048]{1,0:T(8,128)(2,1)S(1)} collective-permute-done((bf16[128,2048]{1,0:T(8,128)(2,1)}, bf16[128,2048]{1,0:T(8,128)(2,1)S(1)}, u32[]{:S(2)}, u32[]{:S(2)}) %collective-permute-start.38) | collective-permute-done | bytes 524320 | tf_op jit(solution)/shard_map/ppermute | solution.py:256
  160.4 1.2 shard_map.54
  (87 shorter events, 18.2 us)
Async XLA Ops:
  5.8 9.5 %collective-permute-start = (bf16[128,1024]{1,0:T(8,128)(2,1)}, bf16[128,1024]{1,0:T(8,128)(2,1)S(1)}, u32[]{:S(2)}, u32[]{:S(2)}) collective-permute-start(bf16[128,1024]{1,0:T(8,128)(2,1)} %get-tuple-element.16), channel_id=1, source_target_pairs={{0,1},{1,0},{2,3},{3,2},{4,5},{5,4},{6,7},{7,6},{8,9},{9,8},{10,11... | collective-permute-start | bytes 786440 | tf_op jit(solution)/shard_map/ppermute | solution.py:240
  8.7 6.5 %copy-start.6 = (f32[128,1024]{1,0:T(8,128)S(1)}, f32[128,1024]{1,0:T(8,128)}, u32[]{:S(2)}) copy-start(f32[128,1024]{1,0:T(8,128)} %get-tuple-element.18) | copy-start | bytes 1572868
  13.2 51.8 %copy-start.1 = (bf16[1024,1024]{1,0:T(8,128)(2,1)}, bf16[1024,1024]{1,0:T(8,128)(2,1)S(1)}, u32[]{:S(2)}) copy-start(bf16[1024,1024]{1,0:T(8,128)(2,1)S(1)} %get-tuple-element.21) | copy-start | bytes 6291460
  15.4 6.6 %collective-permute-start.1 = (bf16[32,1024]{1,0:T(8,128)(2,1)S(1)}, bf16[32,1024]{1,0:T(8,128)(2,1)S(1)}, u32[]{:S(2)}, u32[]{:S(2)}) collective-permute-start(bf16[32,1024]{1,0:T(8,128)(2,1)S(1)} %get-tuple-element.49), channel_id=1, source_target_pairs={{0,6},{1,7},{2,4},{3,5},{4,2},{5,3},{6,0},{7,1},{8,14},{9,15},{10,... | collective-permute-start | bytes 196616 | tf_op jit(solution)/shard_map/ppermute | solution.py:208
  19.3 5.4 %collective-permute-start.2 = (bf16[32,1024]{1,0:T(8,128)(2,1)S(1)}, bf16[32,1024]{1,0:T(8,128)(2,1)S(1)}, u32[]{:S(2)}, u32[]{:S(2)}) collective-permute-start(bf16[32,1024]{1,0:T(8,128)(2,1)S(1)} %get-tuple-element.51), channel_id=1, source_target_pairs={{0,4},{1,5},{2,6},{3,7},{4,0},{5,1},{6,2},{7,3},{8,12},{9,13},{10,... | collective-permute-start | bytes 196616 | tf_op jit(solution)/shard_map/ppermute | solution.py:208
  19.3 5.4 %collective-permute-start.3 = (bf16[32,1024]{1,0:T(8,128)(2,1)S(1)}, bf16[32,1024]{1,0:T(8,128)(2,1)S(1)}, u32[]{:S(2)}, u32[]{:S(2)}) collective-permute-start(bf16[32,1024]{1,0:T(8,128)(2,1)S(1)} %get-tuple-element.50), channel_id=1, source_target_pairs={{0,2},{1,3},{2,0},{3,1},{4,6},{5,7},{6,4},{7,5},{8,10},{9,11},{10,... | collective-permute-start | bytes 196616 | tf_op jit(solution)/shard_map/ppermute | solution.py:208
  19.9 10.2 %copy-start = (bf16[2048,1024]{1,0:T(8,128)(2,1)S(1)}, bf16[2048,1024]{1,0:T(8,128)(2,1)}, u32[]{:S(2)}) copy-start(bf16[2048,1024]{1,0:T(8,128)(2,1)} %x_ref.3) | copy-start | bytes 12582916
  27.8 11.1 %copy-start.5 = (f32[128,2048]{1,0:T(8,128)S(1)}, f32[128,2048]{1,0:T(8,128)}, u32[]{:S(2)}) copy-start(f32[128,2048]{1,0:T(8,128)} %get-tuple-element.22) | copy-start | bytes 3145732
  27.8 6.8 %collective-permute-start.4 = (bf16[32,1024]{1,0:T(8,128)(2,1)S(1)}, bf16[32,1024]{1,0:T(8,128)(2,1)S(1)}, u32[]{:S(2)}, u32[]{:S(2)}) collective-permute-start(bf16[32,1024]{1,0:T(8,128)(2,1)S(1)} %get-tuple-element.53), channel_id=1, source_target_pairs={{0,6},{1,7},{2,4},{3,5},{4,2},{5,3},{6,0},{7,1},{8,14},{9,15},{10,... | collective-permute-start | bytes 196616 | tf_op jit(solution)/shard_map/ppermute | solution.py:220
  31.7 12.0 %copy-start.4 = (f32[128,2048]{1,0:T(8,128)S(1)}, f32[128,2048]{1,0:T(8,128)}, u32[]{:S(2)}) copy-start(f32[128,2048]{1,0:T(8,128)} %get-tuple-element.23) | copy-start | bytes 3145732
  31.7 5.6 %collective-permute-start.5 = (bf16[32,1024]{1,0:T(8,128)(2,1)S(1)}, bf16[32,1024]{1,0:T(8,128)(2,1)S(1)}, u32[]{:S(2)}, u32[]{:S(2)}) collective-permute-start(bf16[32,1024]{1,0:T(8,128)(2,1)S(1)} %get-tuple-element.53), channel_id=1, source_target_pairs={{0,4},{1,5},{2,6},{3,7},{4,0},{5,1},{6,2},{7,3},{8,12},{9,13},{10,... | collective-permute-start | bytes 196616 | tf_op jit(solution)/shard_map/ppermute | solution.py:220
  31.8 5.5 %collective-permute-start.6 = (bf16[32,1024]{1,0:T(8,128)(2,1)S(1)}, bf16[32,1024]{1,0:T(8,128)(2,1)S(1)}, u32[]{:S(2)}, u32[]{:S(2)}) collective-permute-start(bf16[32,1024]{1,0:T(8,128)(2,1)S(1)} %get-tuple-element.53), channel_id=1, source_target_pairs={{0,2},{1,3},{2,0},{3,1},{4,6},{5,7},{6,4},{7,5},{8,10},{9,11},{10,... | collective-permute-start | bytes 196616 | tf_op jit(solution)/shard_map/ppermute | solution.py:220
  37.3 6.4 %collective-permute-start.7 = (bf16[128,1024]{1,0:T(8,128)(2,1)S(1)}, bf16[128,1024]{1,0:T(8,128)(2,1)S(1)}, u32[]{:S(2)}, u32[]{:S(2)}) collective-permute-start(bf16[128,1024]{1,0:T(8,128)(2,1)S(1)} %constant_dynamic-update-slice_fusion.12.refs_0_), channel_id=1, source_target_pairs={{0,1},{1,0},{2,3},{3,2},{4,5},{5,4},{6,7},{7,6},{8,9},{9,8},{10,11... | collective-permute-start | bytes 786440 | tf_op jit(solution)/shard_map/ppermute | solution.py:251
  39.7 8.7 %collective-permute-start.8 = (bf16[128,2048]{1,0:T(8,128)(2,1)S(1)}, bf16[128,2048]{1,0:T(8,128)(2,1)S(1)}, u32[]{:S(2)}, u32[]{:S(2)}) collective-permute-start(bf16[128,2048]{1,0:T(8,128)(2,1)S(1)} %fusion.1), channel_id=1, source_target_pairs={{0,8},{8,16},{16,24},{24,0},{1,9},{9,17},{17,25},{25,1},{2,10},{10... | collective-permute-start | bytes 1572872 | tf_op jit(solution)/shard_map/ppermute | solution.py:256
  44.5 9.4 %collective-permute-start.10 = (bf16[128,2048]{1,0:T(8,128)(2,1)S(1)}, bf16[128,2048]{1,0:T(8,128)(2,1)S(1)}, u32[]{:S(2)}, u32[]{:S(2)}) collective-permute-start(bf16[128,2048]{1,0:T(8,128)(2,1)S(1)} %fusion.2), channel_id=1, source_target_pairs={{0,8},{8,16},{16,24},{24,0},{1,9},{9,17},{17,25},{25,1},{2,10},{10... | collective-permute-start | bytes 1572872 | tf_op jit(solution)/shard_map/ppermute | solution.py:256
  49.0 15.2 %copy-start.3 = (bf16[1024,1024]{1,0:T(8,128)(2,1)S(1)}, bf16[1024,1024]{1,0:T(8,128)(2,1)}, u32[]{:S(2)}) copy-start(bf16[1024,1024]{1,0:T(8,128)(2,1)} %get-tuple-element.20) | copy-start | bytes 6291460
  49.1 7.4 %collective-permute-start.9 = (bf16[128,1024]{1,0:T(8,128)(2,1)S(1)}, bf16[128,1024]{1,0:T(8,128)(2,1)S(1)}, u32[]{:S(2)}, u32[]{:S(2)}) collective-permute-start(bf16[128,1024]{1,0:T(8,128)(2,1)S(1)} %convolution_convert_fusion.2), channel_id=1, source_target_pairs={{0,1},{1,0},{2,3},{3,2},{4,5},{5,4},{6,7},{7,6},{8,9},{9,8},{10,11... | collective-permute-start | bytes 786440 | tf_op jit(solution)/shard_map/ppermute | solution.py:240
  56.6 6.2 %collective-permute-start.11 = (bf16[32,1024]{1,0:T(8,128)(2,1)S(1)}, bf16[32,1024]{1,0:T(8,128)(2,1)S(1)}, u32[]{:S(2)}, u32[]{:S(2)}) collective-permute-start(bf16[32,1024]{1,0:T(8,128)(2,1)S(1)} %get-tuple-element.46), channel_id=1, source_target_pairs={{0,6},{1,7},{2,4},{3,5},{4,2},{5,3},{6,0},{7,1},{8,14},{9,15},{10,... | collective-permute-start | bytes 196616 | tf_op jit(solution)/shard_map/ppermute | solution.py:208
  58.6 5.6 %collective-permute-start.12 = (bf16[32,1024]{1,0:T(8,128)(2,1)S(1)}, bf16[32,1024]{1,0:T(8,128)(2,1)S(1)}, u32[]{:S(2)}, u32[]{:S(2)}) collective-permute-start(bf16[32,1024]{1,0:T(8,128)(2,1)S(1)} %get-tuple-element.48), channel_id=1, source_target_pairs={{0,4},{1,5},{2,6},{3,7},{4,0},{5,1},{6,2},{7,3},{8,12},{9,13},{10,... | collective-permute-start | bytes 196616 | tf_op jit(solution)/shard_map/ppermute | solution.py:208
  59.0 5.2 %collective-permute-start.13 = (bf16[32,1024]{1,0:T(8,128)(2,1)S(1)}, bf16[32,1024]{1,0:T(8,128)(2,1)S(1)}, u32[]{:S(2)}, u32[]{:S(2)}) collective-permute-start(bf16[32,1024]{1,0:T(8,128)(2,1)S(1)} %get-tuple-element.47), channel_id=1, source_target_pairs={{0,2},{1,3},{2,0},{3,1},{4,6},{5,7},{6,4},{7,5},{8,10},{9,11},{10,... | collective-permute-start | bytes 196616 | tf_op jit(solution)/shard_map/ppermute | solution.py:208
  65.8 6.1 %collective-permute-start.14 = (bf16[32,1024]{1,0:T(8,128)(2,1)S(1)}, bf16[32,1024]{1,0:T(8,128)(2,1)S(1)}, u32[]{:S(2)}, u32[]{:S(2)}) collective-permute-start(bf16[32,1024]{1,0:T(8,128)(2,1)S(1)} %get-tuple-element.55), channel_id=1, source_target_pairs={{0,6},{1,7},{2,4},{3,5},{4,2},{5,3},{6,0},{7,1},{8,14},{9,15},{10,... | collective-permute-start | bytes 196616 | tf_op jit(solution)/shard_map/ppermute | solution.py:220
  67.8 5.5 %collective-permute-start.15 = (bf16[32,1024]{1,0:T(8,128)(2,1)S(1)}, bf16[32,1024]{1,0:T(8,128)(2,1)S(1)}, u32[]{:S(2)}, u32[]{:S(2)}) collective-permute-start(bf16[32,1024]{1,0:T(8,128)(2,1)S(1)} %get-tuple-element.55), channel_id=1, source_target_pairs={{0,4},{1,5},{2,6},{3,7},{4,0},{5,1},{6,2},{7,3},{8,12},{9,13},{10,... | collective-permute-start | bytes 196616 | tf_op jit(solution)/shard_map/ppermute | solution.py:220
  68.4 5.0 %collective-permute-start.16 = (bf16[32,1024]{1,0:T(8,128)(2,1)S(1)}, bf16[32,1024]{1,0:T(8,128)(2,1)S(1)}, u32[]{:S(2)}, u32[]{:S(2)}) collective-permute-start(bf16[32,1024]{1,0:T(8,128)(2,1)S(1)} %get-tuple-element.55), channel_id=1, source_target_pairs={{0,2},{1,3},{2,0},{3,1},{4,6},{5,7},{6,4},{7,5},{8,10},{9,11},{10,... | collective-permute-start | bytes 196616 | tf_op jit(solution)/shard_map/ppermute | solution.py:220
  73.4 6.4 %collective-permute-start.17 = (bf16[128,1024]{1,0:T(8,128)(2,1)S(1)}, bf16[128,1024]{1,0:T(8,128)(2,1)S(1)}, u32[]{:S(2)}, u32[]{:S(2)}) collective-permute-start(bf16[128,1024]{1,0:T(8,128)(2,1)S(1)} %constant_dynamic-update-slice_fusion.8.refs_2_), channel_id=1, source_target_pairs={{0,1},{1,0},{2,3},{3,2},{4,5},{5,4},{6,7},{7,6},{8,9},{9,8},{10,11... | collective-permute-start | bytes 786440 | tf_op jit(solution)/shard_map/ppermute | solution.py:251
  74.7 8.7 %collective-permute-start.18 = (bf16[128,2048]{1,0:T(8,128)(2,1)S(1)}, bf16[128,2048]{1,0:T(8,128)(2,1)S(1)}, u32[]{:S(2)}, u32[]{:S(2)}) collective-permute-start(bf16[128,2048]{1,0:T(8,128)(2,1)S(1)} %subtract_convert_fusion.5), channel_id=1, source_target_pairs={{0,8},{8,16},{16,24},{24,0},{1,9},{9,17},{17,25},{25,1},{2,10},{10... | collective-permute-start | bytes 1572872 | tf_op jit(solution)/shard_map/ppermute | solution.py:256
  80.6 8.8 %collective-permute-start.20 = (bf16[128,2048]{1,0:T(8,128)(2,1)S(1)}, bf16[128,2048]{1,0:T(8,128)(2,1)S(1)}, u32[]{:S(2)}, u32[]{:S(2)}) collective-permute-start(bf16[128,2048]{1,0:T(8,128)(2,1)S(1)} %subtract_convert_fusion.4), channel_id=1, source_target_pairs={{0,8},{8,16},{16,24},{24,0},{1,9},{9,17},{17,25},{25,1},{2,10},{10... | collective-permute-start | bytes 1572872 | tf_op jit(solution)/shard_map/ppermute | solution.py:256
  84.1 15.0 %copy-start.2 = (bf16[1024,1024]{1,0:T(8,128)(2,1)S(1)}, bf16[1024,1024]{1,0:T(8,128)(2,1)}, u32[]{:S(2)}) copy-start(bf16[1024,1024]{1,0:T(8,128)(2,1)} %copy-done.1) | copy-start | bytes 6291460
  84.1 6.4 %collective-permute-start.19 = (bf16[128,1024]{1,0:T(8,128)(2,1)S(1)}, bf16[128,1024]{1,0:T(8,128)(2,1)S(1)}, u32[]{:S(2)}, u32[]{:S(2)}) collective-permute-start(bf16[128,1024]{1,0:T(8,128)(2,1)S(1)} %convolution_convert_fusion.1), channel_id=1, source_target_pairs={{0,1},{1,0},{2,3},{3,2},{4,5},{5,4},{6,7},{7,6},{8,9},{9,8},{10,11... | collective-permute-start | bytes 786440 | tf_op jit(solution)/shard_map/ppermute | solution.py:240
  90.7 6.1 %collective-permute-start.21 = (bf16[32,1024]{1,0:T(8,128)(2,1)S(1)}, bf16[32,1024]{1,0:T(8,128)(2,1)S(1)}, u32[]{:S(2)}, u32[]{:S(2)}) collective-permute-start(bf16[32,1024]{1,0:T(8,128)(2,1)S(1)} %get-tuple-element.43), channel_id=1, source_target_pairs={{0,6},{1,7},{2,4},{3,5},{4,2},{5,3},{6,0},{7,1},{8,14},{9,15},{10,... | collective-permute-start | bytes 196616 | tf_op jit(solution)/shard_map/ppermute | solution.py:208
  92.7 5.6 %collective-permute-start.22 = (bf16[32,1024]{1,0:T(8,128)(2,1)S(1)}, bf16[32,1024]{1,0:T(8,128)(2,1)S(1)}, u32[]{:S(2)}, u32[]{:S(2)}) collective-permute-start(bf16[32,1024]{1,0:T(8,128)(2,1)S(1)} %get-tuple-element.45), channel_id=1, source_target_pairs={{0,4},{1,5},{2,6},{3,7},{4,0},{5,1},{6,2},{7,3},{8,12},{9,13},{10,... | collective-permute-start | bytes 196616 | tf_op jit(solution)/shard_map/ppermute | solution.py:208
  93.3 5.0 %collective-permute-start.23 = (bf16[32,1024]{1,0:T(8,128)(2,1)S(1)}, bf16[32,1024]{1,0:T(8,128)(2,1)S(1)}, u32[]{:S(2)}, u32[]{:S(2)}) collective-permute-start(bf16[32,1024]{1,0:T(8,128)(2,1)S(1)} %get-tuple-element.44), channel_id=1, source_target_pairs={{0,2},{1,3},{2,0},{3,1},{4,6},{5,7},{6,4},{7,5},{8,10},{9,11},{10,... | collective-permute-start | bytes 196616 | tf_op jit(solution)/shard_map/ppermute | solution.py:208
  99.8 6.1 %collective-permute-start.24 = (bf16[32,1024]{1,0:T(8,128)(2,1)S(1)}, bf16[32,1024]{1,0:T(8,128)(2,1)S(1)}, u32[]{:S(2)}, u32[]{:S(2)}) collective-permute-start(bf16[32,1024]{1,0:T(8,128)(2,1)S(1)} %get-tuple-element.57), channel_id=1, source_target_pairs={{0,6},{1,7},{2,4},{3,5},{4,2},{5,3},{6,0},{7,1},{8,14},{9,15},{10,... | collective-permute-start | bytes 196616 | tf_op jit(solution)/shard_map/ppermute | solution.py:220
  101.9 5.5 %collective-permute-start.25 = (bf16[32,1024]{1,0:T(8,128)(2,1)S(1)}, bf16[32,1024]{1,0:T(8,128)(2,1)S(1)}, u32[]{:S(2)}, u32[]{:S(2)}) collective-permute-start(bf16[32,1024]{1,0:T(8,128)(2,1)S(1)} %get-tuple-element.57), channel_id=1, source_target_pairs={{0,4},{1,5},{2,6},{3,7},{4,0},{5,1},{6,2},{7,3},{8,12},{9,13},{10,... | collective-permute-start | bytes 196616 | tf_op jit(solution)/shard_map/ppermute | solution.py:220
  102.5 5.0 %collective-permute-start.26 = (bf16[32,1024]{1,0:T(8,128)(2,1)S(1)}, bf16[32,1024]{1,0:T(8,128)(2,1)S(1)}, u32[]{:S(2)}, u32[]{:S(2)}) collective-permute-start(bf16[32,1024]{1,0:T(8,128)(2,1)S(1)} %get-tuple-element.57), channel_id=1, source_target_pairs={{0,2},{1,3},{2,0},{3,1},{4,6},{5,7},{6,4},{7,5},{8,10},{9,11},{10,... | collective-permute-start | bytes 196616 | tf_op jit(solution)/shard_map/ppermute | solution.py:220
  107.5 6.4 %collective-permute-start.27 = (bf16[128,1024]{1,0:T(8,128)(2,1)S(1)}, bf16[128,1024]{1,0:T(8,128)(2,1)S(1)}, u32[]{:S(2)}, u32[]{:S(2)}) collective-permute-start(bf16[128,1024]{1,0:T(8,128)(2,1)S(1)} %constant_dynamic-update-slice_fusion.4.refs_4_), channel_id=1, source_target_pairs={{0,1},{1,0},{2,3},{3,2},{4,5},{5,4},{6,7},{7,6},{8,9},{9,8},{10,11... | collective-permute-start | bytes 786440 | tf_op jit(solution)/shard_map/ppermute | solution.py:251
  109.8 8.7 %collective-permute-start.28 = (bf16[128,2048]{1,0:T(8,128)(2,1)S(1)}, bf16[128,2048]{1,0:T(8,128)(2,1)S(1)}, u32[]{:S(2)}, u32[]{:S(2)}) collective-permute-start(bf16[128,2048]{1,0:T(8,128)(2,1)S(1)} %subtract_convert_fusion.3), channel_id=1, source_target_pairs={{0,8},{8,16},{16,24},{24,0},{1,9},{9,17},{17,25},{25,1},{2,10},{10... | collective-permute-start | bytes 1572872 | tf_op jit(solution)/shard_map/ppermute | solution.py:256
  114.7 9.4 %collective-permute-start.30 = (bf16[128,2048]{1,0:T(8,128)(2,1)S(1)}, bf16[128,2048]{1,0:T(8,128)(2,1)S(1)}, u32[]{:S(2)}, u32[]{:S(2)}) collective-permute-start(bf16[128,2048]{1,0:T(8,128)(2,1)S(1)} %subtract_convert_fusion.2), channel_id=1, source_target_pairs={{0,8},{8,16},{16,24},{24,0},{1,9},{9,17},{17,25},{25,1},{2,10},{10... | collective-permute-start | bytes 1572872 | tf_op jit(solution)/shard_map/ppermute | solution.py:256
  119.2 7.4 %collective-permute-start.29 = (bf16[128,1024]{1,0:T(8,128)(2,1)S(1)}, bf16[128,1024]{1,0:T(8,128)(2,1)S(1)}, u32[]{:S(2)}, u32[]{:S(2)}) collective-permute-start(bf16[128,1024]{1,0:T(8,128)(2,1)S(1)} %convolution_convert_fusion), channel_id=1, source_target_pairs={{0,1},{1,0},{2,3},{3,2},{4,5},{5,4},{6,7},{7,6},{8,9},{9,8},{10,11... | collective-permute-start | bytes 786440 | tf_op jit(solution)/shard_map/ppermute | solution.py:240
  126.7 6.2 %collective-permute-start.31 = (bf16[32,1024]{1,0:T(8,128)(2,1)S(1)}, bf16[32,1024]{1,0:T(8,128)(2,1)S(1)}, u32[]{:S(2)}, u32[]{:S(2)}) collective-permute-start(bf16[32,1024]{1,0:T(8,128)(2,1)S(1)} %get-tuple-element.40), channel_id=1, source_target_pairs={{0,6},{1,7},{2,4},{3,5},{4,2},{5,3},{6,0},{7,1},{8,14},{9,15},{10,... | collective-permute-start | bytes 196616 | tf_op jit(solution)/shard_map/ppermute | solution.py:208
  128.8 5.5 %collective-permute-start.32 = (bf16[32,1024]{1,0:T(8,128)(2,1)S(1)}, bf16[32,1024]{1,0:T(8,128)(2,1)S(1)}, u32[]{:S(2)}, u32[]{:S(2)}) collective-permute-start(bf16[32,1024]{1,0:T(8,128)(2,1)S(1)} %get-tuple-element.42), channel_id=1, source_target_pairs={{0,4},{1,5},{2,6},{3,7},{4,0},{5,1},{6,2},{7,3},{8,12},{9,13},{10,... | collective-permute-start | bytes 196616 | tf_op jit(solution)/shard_map/ppermute | solution.py:208
  129.3 5.0 %collective-permute-start.33 = (bf16[32,1024]{1,0:T(8,128)(2,1)S(1)}, bf16[32,1024]{1,0:T(8,128)(2,1)S(1)}, u32[]{:S(2)}, u32[]{:S(2)}) collective-permute-start(bf16[32,1024]{1,0:T(8,128)(2,1)S(1)} %get-tuple-element.41), channel_id=1, source_target_pairs={{0,2},{1,3},{2,0},{3,1},{4,6},{5,7},{6,4},{7,5},{8,10},{9,11},{10,... | collective-permute-start | bytes 196616 | tf_op jit(solution)/shard_map/ppermute | solution.py:208
  135.9 6.1 %collective-permute-start.34 = (bf16[32,1024]{1,0:T(8,128)(2,1)S(1)}, bf16[32,1024]{1,0:T(8,128)(2,1)S(1)}, u32[]{:S(2)}, u32[]{:S(2)}) collective-permute-start(bf16[32,1024]{1,0:T(8,128)(2,1)S(1)} %get-tuple-element.59), channel_id=1, source_target_pairs={{0,6},{1,7},{2,4},{3,5},{4,2},{5,3},{6,0},{7,1},{8,14},{9,15},{10,... | collective-permute-start | bytes 196616 | tf_op jit(solution)/shard_map/ppermute | solution.py:220
  137.9 5.6 %collective-permute-start.35 = (bf16[32,1024]{1,0:T(8,128)(2,1)S(1)}, bf16[32,1024]{1,0:T(8,128)(2,1)S(1)}, u32[]{:S(2)}, u32[]{:S(2)}) collective-permute-start(bf16[32,1024]{1,0:T(8,128)(2,1)S(1)} %get-tuple-element.59), channel_id=1, source_target_pairs={{0,4},{1,5},{2,6},{3,7},{4,0},{5,1},{6,2},{7,3},{8,12},{9,13},{10,... | collective-permute-start | bytes 196616 | tf_op jit(solution)/shard_map/ppermute | solution.py:220
  138.5 5.0 %collective-permute-start.36 = (bf16[32,1024]{1,0:T(8,128)(2,1)S(1)}, bf16[32,1024]{1,0:T(8,128)(2,1)S(1)}, u32[]{:S(2)}, u32[]{:S(2)}) collective-permute-start(bf16[32,1024]{1,0:T(8,128)(2,1)S(1)} %get-tuple-element.59), channel_id=1, source_target_pairs={{0,2},{1,3},{2,0},{3,1},{4,6},{5,7},{6,4},{7,5},{8,10},{9,11},{10,... | collective-permute-start | bytes 196616 | tf_op jit(solution)/shard_map/ppermute | solution.py:220
  143.5 6.4 %collective-permute-start.37 = (bf16[128,1024]{1,0:T(8,128)(2,1)S(1)}, bf16[128,1024]{1,0:T(8,128)(2,1)S(1)}, u32[]{:S(2)}, u32[]{:S(2)}) collective-permute-start(bf16[128,1024]{1,0:T(8,128)(2,1)S(1)} %constant_dynamic-update-slice_fusion.refs_6_), channel_id=1, source_target_pairs={{0,1},{1,0},{2,3},{3,2},{4,5},{5,4},{6,7},{7,6},{8,9},{9,8},{10,11... | collective-permute-start | bytes 786440 | tf_op jit(solution)/shard_map/ppermute | solution.py:251
  145.7 8.8 %collective-permute-start.39 = (bf16[128,2048]{1,0:T(8,128)(2,1)}, bf16[128,2048]{1,0:T(8,128)(2,1)S(1)}, u32[]{:S(2)}, u32[]{:S(2)}) collective-permute-start(bf16[128,2048]{1,0:T(8,128)(2,1)} %subtract_convert_fusion), channel_id=1, source_target_pairs={{0,8},{8,16},{16,24},{24,0},{1,9},{9,17},{17,25},{25,1},{2,10},{10... | collective-permute-start | bytes 1572872 | tf_op jit(solution)/shard_map/ppermute | solution.py:256
  151.6 8.8 %collective-permute-start.38 = (bf16[128,2048]{1,0:T(8,128)(2,1)}, bf16[128,2048]{1,0:T(8,128)(2,1)S(1)}, u32[]{:S(2)}, u32[]{:S(2)}) collective-permute-start(bf16[128,2048]{1,0:T(8,128)(2,1)} %subtract_convert_fusion.1), channel_id=1, source_target_pairs={{0,8},{8,16},{16,24},{24,0},{1,9},{9,17},{17,25},{25,1},{2,10},{10... | collective-permute-start | bytes 1572872 | tf_op jit(solution)/shard_map/ppermute | solution.py:256

commit v5 on v4

--- a/solution.py
+++ b/solution.py
@@ -123,7 +123,7 @@
             in_specs=[pl.BlockSpec((height, feat_width), whole)] * pieces,
             out_specs=pl.BlockSpec((pieces * height, feat_width), whole),
         ),
-        compiler_params=pltpu.CompilerParams(vmem_limit_bytes=SCATTER_VMEM),
+        compiler_params=pltpu.CompilerParams(vmem_limit_bytes=FIRST_VMEM),
         cost_estimate=pl.CostEstimate(
             flops=0, bytes_accessed=4 * pieces * height * feat_width, transcendentals=0
         ),

time: 162 us -> 161 us (level)
  waiting for transfers between devices: 78.3 us -> 76.5 us
  matrix products: 19.5 us -> 17.8 us
    ppermute x8, waiting for transfers between devices: 27.9 us -> 25.4 us  [on_device(): lax.ppermute(part.astype(BF16), 'feat', next_block)]
    dot_general x8, matrix products: 7.57 us -> 5.92 us  [subtract(): lax.dot_general(update, turned, (((1,), (0,)), ((), ())), preferred_eleme...]
    pallas_call x1, Pallas kernels: 2 us -> 3.62 us  [scatter_rows(): pl.pallas_call(functools.partial(scatter_kernel, pieces), out_shape=jax.S...]
  transfers between devices with their start and end apart: 40 -> 40, of which waited for: 32 -> 31; matrix products, arithmetic and copies ran while one was open for 10% -> 10% of each run, Pallas kernels for 3% -> 4%
where the time goes in v5:
time: 161 us
  waiting for transfers between devices  76.5 us (48%)
  starting transfers between devices  46.3 us (29%)
  matrix products  17.8 us (11%)
  Pallas kernels  12.7 us (8%)
  other arithmetic  4.92 us (3%)
    ppermute x8, waiting for transfers between devices, on_device(): lax.ppermute(part.astype(BF16), 'feat', next_block)  25.4 us
    ppermute x4, waiting for transfers between devices, on_device(): update_away = lax.ppermute(update_home, 'rows', partner)  18.2 us
    ppermute x12, starting transfers between devices, reduce_outer(): lax.ppermute(out.astype(BF16), 'rows', outer_step(step)).astype(F32)  17.9 us
    ppermute x12, starting transfers between devices, gather_outer(): got = lax.ppermute(update, 'rows', outer_step(step))  17.8 us
    ppermute x12, waiting for transfers between devices, reduce_outer(): lax.ppermute(out.astype(BF16), 'rows', outer_step(step)).astype(F32)  14.1 us
    ppermute x12, waiting for transfers between devices, gather_outer(): got = lax.ppermute(update, 'rows', outer_step(step))  12.8 us
    dot_general x8, matrix products, apply_inverse(): dot = lambda a, b: lax.dot_general(a, b, dims, preferred_element_type=F32)  7.52 us
    ppermute x4, waiting for transfers between devices, on_device(): arrived = lax.ppermute(term, 'rows', partner)  6.03 us
  transfers between devices with their start and end apart: 40, of which 31 were waited for; matrix products, arithmetic and copies ran while one was open for 10% of the time, Pallas kernels for 4%

profile of v5, /device:TPU:0, one launch (start us, length us, event | category | flops | bytes accessed | tf_op | source)
XLA Modules:
  0.0 160.5 jit_solution(8838525371024281095)
XLA Ops:
  0.6 5.1 %shard_map.50 = (bf16[128,1024]{1,0:T(8,128)(2,1)}, f32[128,1024]{1,0:T(8,128)}, f32[128,2048]{1,0:T(8,128)}, f32[128,2048]{1,0:T(8,128)}) custom-call(s32[1]{0:T(128)} %bitcast.8.lead_ref.place_ref, f32[2048,256]{1,0:T(8,128)} %home_ref.1, f32[2048,256]{1,0:T(8,128)} %home_ref.1, bf16[2048,1024]{1,0:T(8,128)(2,1)} %x_ref.3), custom_call_target="tpu_custom_call" | custom-call | flops 1073741824 | bytes 9175040 | tf_op jit(solution)/shard_map/pallas_call | solution.py:53
  5.7 3.0 %collective-permute-start = (bf16[128,1024]{1,0:T(8,128)(2,1)}, bf16[128,1024]{1,0:T(8,128)(2,1)S(1)}, u32[]{:S(2)}, u32[]{:S(2)}) collective-permute-start(bf16[128,1024]{1,0:T(8,128)(2,1)} %get-tuple-element.16), channel_id=1, source_target_pairs={{0,1},{1,0},{2,3},{3,2},{4,5},{5,4},{6,7},{7,6},{8,9},{9,8},{10,11... | collective-permute-start | bytes 786440 | tf_op jit(solution)/shard_map/ppermute | solution.py:240
  8.7 4.5 %fusion = (bf16[1024,1024]{1,0:T(8,128)(2,1)S(1)}, bf16[1024,1024]{1,0:T(8,128)(2,1)}) fusion(f32[1024,1024]{1,0:T(8,128)} %param.5), kind=kLoop, calls=%fused_computation.2 | loop fusion | flops 4194304 | bytes 8388608 | tf_op jit(solution)/shard_map/convert_element_type | solution.py:16
  13.2 2.0 %collective-permute-done = bf16[128,1024]{1,0:T(8,128)(2,1)S(1)} collective-permute-done((bf16[128,1024]{1,0:T(8,128)(2,1)}, bf16[128,1024]{1,0:T(8,128)(2,1)S(1)}, u32[]{:S(2)}, u32[]{:S(2)}) %collective-permute-start) | collective-permute-done | bytes 262176 | tf_op jit(solution)/shard_map/ppermute | solution.py:240
  15.3 3.9 %collective-permute-start.1 = (bf16[32,1024]{1,0:T(8,128)(2,1)S(1)}, bf16[32,1024]{1,0:T(8,128)(2,1)S(1)}, u32[]{:S(2)}, u32[]{:S(2)}) collective-permute-start(bf16[32,1024]{1,0:T(8,128)(2,1)S(1)} %get-tuple-element.49), channel_id=1, source_target_pairs={{0,6},{1,7},{2,4},{3,5},{4,2},{5,3},{6,0},{7,1},{8,14},{9,15},{10,... | collective-permute-start | bytes 196616 | tf_op jit(solution)/shard_map/ppermute | solution.py:208
  19.9 2.0 %collective-permute-done.1 = bf16[32,1024]{1,0:T(8,128)(2,1)S(1)} collective-permute-done((bf16[32,1024]{1,0:T(8,128)(2,1)S(1)}, bf16[32,1024]{1,0:T(8,128)(2,1)S(1)}, u32[]{:S(2)}, u32[]{:S(2)}) %collective-permute-start.1) | collective-permute-done | bytes 65568 | tf_op jit(solution)/shard_map/ppermute | solution.py:208
  21.9 2.7 %collective-permute-done.2 = bf16[32,1024]{1,0:T(8,128)(2,1)S(1)} collective-permute-done((bf16[32,1024]{1,0:T(8,128)(2,1)S(1)}, bf16[32,1024]{1,0:T(8,128)(2,1)S(1)}, u32[]{:S(2)}, u32[]{:S(2)}) %collective-permute-start.2) | collective-permute-done | bytes 65568 | tf_op jit(solution)/shard_map/ppermute | solution.py:208
  24.6 2.3 %fusion.11 = f32[64,1024]{1,0:T(8,128)S(1)} fusion(bf16[1024,1024]{1,0:T(8,128)(2,1)} %get-tuple-element.20, bf16[32,1024]{1,0:T(8,128)(2,1)S(1)} %get-tuple-element.38, bf16[32,1024]{1,0:T(8,128)(2,1)S(1)} %get-tuple-element.39), kind=kOutput, calls=%fused_computation.44 | convolution fusion | flops 134479872 | bytes 2490368 | tf_op jit(solution)/shard_map/dot_general | solution.py:189
  27.8 2.3 %collective-permute-start.4 = (bf16[32,1024]{1,0:T(8,128)(2,1)S(1)}, bf16[32,1024]{1,0:T(8,128)(2,1)S(1)}, u32[]{:S(2)}, u32[]{:S(2)}) collective-permute-start(bf16[32,1024]{1,0:T(8,128)(2,1)S(1)} %get-tuple-element.53), channel_id=1, source_target_pairs={{0,6},{1,7},{2,4},{3,5},{4,2},{5,3},{6,0},{7,1},{8,14},{9,15},{10,... | collective-permute-start | bytes 196616 | tf_op jit(solution)/shard_map/ppermute | solution.py:220
  30.0 1.6 %shard_map.51 = bf16[1024,2048]{1,0:T(8,128)(2,1)S(1)} custom-call(bf16[2048,1024]{1,0:T(8,128)(2,1)S(1)} %copy-done), custom_call_target="tpu_custom_call" | custom-call | bytes 8388608 | tf_op jit(solution)/shard_map/pallas_call | solution.py:92
  31.8 2.2 %collective-permute-start.6 = (bf16[32,1024]{1,0:T(8,128)(2,1)S(1)}, bf16[32,1024]{1,0:T(8,128)(2,1)S(1)}, u32[]{:S(2)}, u32[]{:S(2)}) collective-permute-start(bf16[32,1024]{1,0:T(8,128)(2,1)S(1)} %get-tuple-element.53), channel_id=1, source_target_pairs={{0,2},{1,3},{2,0},{3,1},{4,6},{5,7},{6,4},{7,5},{8,10},{9,11},{10,... | collective-permute-start | bytes 196616 | tf_op jit(solution)/shard_map/ppermute | solution.py:220
  34.5 2.7 %collective-permute-done.5 = bf16[32,1024]{1,0:T(8,128)(2,1)S(1)} collective-permute-done((bf16[32,1024]{1,0:T(8,128)(2,1)S(1)}, bf16[32,1024]{1,0:T(8,128)(2,1)S(1)}, u32[]{:S(2)}, u32[]{:S(2)}) %collective-permute-start.5) | collective-permute-done | bytes 65568 | tf_op jit(solution)/shard_map/ppermute | solution.py:220
  37.3 1.6 collective-permute-start.7
  38.9 0.7 fusion.1
  39.7 4.0 %collective-permute-done.7.refs_1_ = bf16[128,1024]{1,0:T(8,128)(2,1)S(1)} collective-permute-done((bf16[128,1024]{1,0:T(8,128)(2,1)S(1)}, bf16[128,1024]{1,0:T(8,128)(2,1)S(1)}, u32[]{:S(2)}, u32[]{:S(2)}) %collective-permute-start.7) | collective-permute-done | bytes 262176 | tf_op jit(solution)/shard_map/ppermute | solution.py:251
  43.7 0.7 fusion.2
  44.6 3.7 %collective-permute-done.8 = bf16[128,2048]{1,0:T(8,128)(2,1)S(1)} collective-permute-done((bf16[128,2048]{1,0:T(8,128)(2,1)S(1)}, bf16[128,2048]{1,0:T(8,128)(2,1)S(1)}, u32[]{:S(2)}, u32[]{:S(2)}) %collective-permute-start.8) | collective-permute-done | bytes 524320 | tf_op jit(solution)/shard_map/ppermute | solution.py:256
  49.6 4.3 %collective-permute-done.10 = bf16[128,2048]{1,0:T(8,128)(2,1)S(1)} collective-permute-done((bf16[128,2048]{1,0:T(8,128)(2,1)S(1)}, bf16[128,2048]{1,0:T(8,128)(2,1)S(1)}, u32[]{:S(2)}, u32[]{:S(2)}) %collective-permute-start.10) | collective-permute-done | bytes 524320 | tf_op jit(solution)/shard_map/ppermute | solution.py:256
  54.6 1.8 %collective-permute-done.9 = bf16[128,1024]{1,0:T(8,128)(2,1)S(1)} collective-permute-done((bf16[128,1024]{1,0:T(8,128)(2,1)S(1)}, bf16[128,1024]{1,0:T(8,128)(2,1)S(1)}, u32[]{:S(2)}, u32[]{:S(2)}) %collective-permute-start.9) | collective-permute-done | bytes 262176 | tf_op jit(solution)/shard_map/ppermute | solution.py:240
  56.5 2.0 %collective-permute-start.11 = (bf16[32,1024]{1,0:T(8,128)(2,1)S(1)}, bf16[32,1024]{1,0:T(8,128)(2,1)S(1)}, u32[]{:S(2)}, u32[]{:S(2)}) collective-permute-start(bf16[32,1024]{1,0:T(8,128)(2,1)S(1)} %get-tuple-element.46), channel_id=1, source_target_pairs={{0,6},{1,7},{2,4},{3,5},{4,2},{5,3},{6,0},{7,1},{8,14},{9,15},{10,... | collective-permute-start | bytes 196616 | tf_op jit(solution)/shard_map/ppermute | solution.py:208
  59.0 2.0 %collective-permute-start.13 = (bf16[32,1024]{1,0:T(8,128)(2,1)S(1)}, bf16[32,1024]{1,0:T(8,128)(2,1)S(1)}, u32[]{:S(2)}, u32[]{:S(2)}) collective-permute-start(bf16[32,1024]{1,0:T(8,128)(2,1)S(1)} %get-tuple-element.47), channel_id=1, source_target_pairs={{0,2},{1,3},{2,0},{3,1},{4,6},{5,7},{6,4},{7,5},{8,10},{9,11},{10,... | collective-permute-start | bytes 196616 | tf_op jit(solution)/shard_map/ppermute | solution.py:208
  61.0 1.7 %collective-permute-done.11 = bf16[32,1024]{1,0:T(8,128)(2,1)S(1)} collective-permute-done((bf16[32,1024]{1,0:T(8,128)(2,1)S(1)}, bf16[32,1024]{1,0:T(8,128)(2,1)S(1)}, u32[]{:S(2)}, u32[]{:S(2)}) %collective-permute-start.11) | collective-permute-done | bytes 65568 | tf_op jit(solution)/shard_map/ppermute | solution.py:208
  62.7 1.4 collective-permute-done.12
  64.2 0.8 fusion.15
  65.7 2.1 %collective-permute-start.14 = (bf16[32,1024]{1,0:T(8,128)(2,1)S(1)}, bf16[32,1024]{1,0:T(8,128)(2,1)S(1)}, u32[]{:S(2)}, u32[]{:S(2)}) collective-permute-start(bf16[32,1024]{1,0:T(8,128)(2,1)S(1)} %get-tuple-element.55), channel_id=1, source_target_pairs={{0,6},{1,7},{2,4},{3,5},{4,2},{5,3},{6,0},{7,1},{8,14},{9,15},{10,... | collective-permute-start | bytes 196616 | tf_op jit(solution)/shard_map/ppermute | solution.py:220
  68.4 1.8 %collective-permute-start.16 = (bf16[32,1024]{1,0:T(8,128)(2,1)S(1)}, bf16[32,1024]{1,0:T(8,128)(2,1)S(1)}, u32[]{:S(2)}, u32[]{:S(2)}) collective-permute-start(bf16[32,1024]{1,0:T(8,128)(2,1)S(1)} %get-tuple-element.55), channel_id=1, source_target_pairs={{0,2},{1,3},{2,0},{3,1},{4,6},{5,7},{6,4},{7,5},{8,10},{9,11},{10,... | collective-permute-start | bytes 196616 | tf_op jit(solution)/shard_map/ppermute | solution.py:220
  70.2 1.7 %collective-permute-done.14 = bf16[32,1024]{1,0:T(8,128)(2,1)S(1)} collective-permute-done((bf16[32,1024]{1,0:T(8,128)(2,1)S(1)}, bf16[32,1024]{1,0:T(8,128)(2,1)S(1)}, u32[]{:S(2)}, u32[]{:S(2)}) %collective-permute-start.14) | collective-permute-done | bytes 65568 | tf_op jit(solution)/shard_map/ppermute | solution.py:220
  71.9 1.5 collective-permute-done.15
  74.0 0.7 subtract_convert_fusion.5
  74.8 5.1 %collective-permute-done.17.refs_3_ = bf16[128,1024]{1,0:T(8,128)(2,1)S(1)} collective-permute-done((bf16[128,1024]{1,0:T(8,128)(2,1)S(1)}, bf16[128,1024]{1,0:T(8,128)(2,1)S(1)}, u32[]{:S(2)}, u32[]{:S(2)}) %collective-permute-start.17) | collective-permute-done | bytes 262176 | tf_op jit(solution)/shard_map/ppermute | solution.py:251
  79.8 0.7 subtract_convert_fusion.4
  80.8 2.5 %collective-permute-done.18 = bf16[128,2048]{1,0:T(8,128)(2,1)S(1)} collective-permute-done((bf16[128,2048]{1,0:T(8,128)(2,1)S(1)}, bf16[128,2048]{1,0:T(8,128)(2,1)S(1)}, u32[]{:S(2)}, u32[]{:S(2)}) %collective-permute-start.18) | collective-permute-done | bytes 524320 | tf_op jit(solution)/shard_map/ppermute | solution.py:256
  84.1 1.6 collective-permute-start.19
  85.7 3.7 %collective-permute-done.20 = bf16[128,2048]{1,0:T(8,128)(2,1)S(1)} collective-permute-done((bf16[128,2048]{1,0:T(8,128)(2,1)S(1)}, bf16[128,2048]{1,0:T(8,128)(2,1)S(1)}, u32[]{:S(2)}, u32[]{:S(2)}) %collective-permute-start.20) | collective-permute-done | bytes 524320 | tf_op jit(solution)/shard_map/ppermute | solution.py:256
  90.6 2.0 %collective-permute-start.21 = (bf16[32,1024]{1,0:T(8,128)(2,1)S(1)}, bf16[32,1024]{1,0:T(8,128)(2,1)S(1)}, u32[]{:S(2)}, u32[]{:S(2)}) collective-permute-start(bf16[32,1024]{1,0:T(8,128)(2,1)S(1)} %get-tuple-element.43), channel_id=1, source_target_pairs={{0,6},{1,7},{2,4},{3,5},{4,2},{5,3},{6,0},{7,1},{8,14},{9,15},{10,... | collective-permute-start | bytes 196616 | tf_op jit(solution)/shard_map/ppermute | solution.py:208
  93.3 1.8 %collective-permute-start.23 = (bf16[32,1024]{1,0:T(8,128)(2,1)S(1)}, bf16[32,1024]{1,0:T(8,128)(2,1)S(1)}, u32[]{:S(2)}, u32[]{:S(2)}) collective-permute-start(bf16[32,1024]{1,0:T(8,128)(2,1)S(1)} %get-tuple-element.44), channel_id=1, source_target_pairs={{0,2},{1,3},{2,0},{3,1},{4,6},{5,7},{6,4},{7,5},{8,10},{9,11},{10,... | collective-permute-start | bytes 196616 | tf_op jit(solution)/shard_map/ppermute | solution.py:208
  95.1 1.7 %collective-permute-done.21 = bf16[32,1024]{1,0:T(8,128)(2,1)S(1)} collective-permute-done((bf16[32,1024]{1,0:T(8,128)(2,1)S(1)}, bf16[32,1024]{1,0:T(8,128)(2,1)S(1)}, u32[]{:S(2)}, u32[]{:S(2)}) %collective-permute-start.21) | collective-permute-done | bytes 65568 | tf_op jit(solution)/shard_map/ppermute | solution.py:208
  96.8 1.5 collective-permute-done.22
  98.3 0.8 fusion.19
  99.8 2.1 %collective-permute-start.24 = (bf16[32,1024]{1,0:T(8,128)(2,1)S(1)}, bf16[32,1024]{1,0:T(8,128)(2,1)S(1)}, u32[]{:S(2)}, u32[]{:S(2)}) collective-permute-start(bf16[32,1024]{1,0:T(8,128)(2,1)S(1)} %get-tuple-element.57), channel_id=1, source_target_pairs={{0,6},{1,7},{2,4},{3,5},{4,2},{5,3},{6,0},{7,1},{8,14},{9,15},{10,... | collective-permute-start | bytes 196616 | tf_op jit(solution)/shard_map/ppermute | solution.py:220
  102.4 1.8 %collective-permute-start.26 = (bf16[32,1024]{1,0:T(8,128)(2,1)S(1)}, bf16[32,1024]{1,0:T(8,128)(2,1)S(1)}, u32[]{:S(2)}, u32[]{:S(2)}) collective-permute-start(bf16[32,1024]{1,0:T(8,128)(2,1)S(1)} %get-tuple-element.57), channel_id=1, source_target_pairs={{0,2},{1,3},{2,0},{3,1},{4,6},{5,7},{6,4},{7,5},{8,10},{9,11},{10,... | collective-permute-start | bytes 196616 | tf_op jit(solution)/shard_map/ppermute | solution.py:220
  104.2 1.7 %collective-permute-done.24 = bf16[32,1024]{1,0:T(8,128)(2,1)S(1)} collective-permute-done((bf16[32,1024]{1,0:T(8,128)(2,1)S(1)}, bf16[32,1024]{1,0:T(8,128)(2,1)S(1)}, u32[]{:S(2)}, u32[]{:S(2)}) %collective-permute-start.24) | collective-permute-done | bytes 65568 | tf_op jit(solution)/shard_map/ppermute | solution.py:220
  105.9 1.5 collective-permute-done.25
  107.5 1.6 collective-permute-start.27
  109.9 4.0 %collective-permute-done.27.refs_5_ = bf16[128,1024]{1,0:T(8,128)(2,1)S(1)} collective-permute-done((bf16[128,1024]{1,0:T(8,128)(2,1)S(1)}, bf16[128,1024]{1,0:T(8,128)(2,1)S(1)}, u32[]{:S(2)}, u32[]{:S(2)}) %collective-permute-start.27) | collective-permute-done | bytes 262176 | tf_op jit(solution)/shard_map/ppermute | solution.py:251
  113.9 0.7 subtract_convert_fusion.2
  114.7 3.7 %collective-permute-done.28 = bf16[128,2048]{1,0:T(8,128)(2,1)S(1)} collective-permute-done((bf16[128,2048]{1,0:T(8,128)(2,1)S(1)}, bf16[128,2048]{1,0:T(8,128)(2,1)S(1)}, u32[]{:S(2)}, u32[]{:S(2)}) %collective-permute-start.28) | collective-permute-done | bytes 524320 | tf_op jit(solution)/shard_map/ppermute | solution.py:256
  119.8 4.3 %collective-permute-done.30 = bf16[128,2048]{1,0:T(8,128)(2,1)S(1)} collective-permute-done((bf16[128,2048]{1,0:T(8,128)(2,1)S(1)}, bf16[128,2048]{1,0:T(8,128)(2,1)S(1)}, u32[]{:S(2)}, u32[]{:S(2)}) %collective-permute-start.30) | collective-permute-done | bytes 524320 | tf_op jit(solution)/shard_map/ppermute | solution.py:256
  124.8 1.8 %collective-permute-done.29 = bf16[128,1024]{1,0:T(8,128)(2,1)S(1)} collective-permute-done((bf16[128,1024]{1,0:T(8,128)(2,1)S(1)}, bf16[128,1024]{1,0:T(8,128)(2,1)S(1)}, u32[]{:S(2)}, u32[]{:S(2)}) %collective-permute-start.29) | collective-permute-done | bytes 262176 | tf_op jit(solution)/shard_map/ppermute | solution.py:240
  126.7 2.0 %collective-permute-start.31 = (bf16[32,1024]{1,0:T(8,128)(2,1)S(1)}, bf16[32,1024]{1,0:T(8,128)(2,1)S(1)}, u32[]{:S(2)}, u32[]{:S(2)}) collective-permute-start(bf16[32,1024]{1,0:T(8,128)(2,1)S(1)} %get-tuple-element.40), channel_id=1, source_target_pairs={{0,6},{1,7},{2,4},{3,5},{4,2},{5,3},{6,0},{7,1},{8,14},{9,15},{10,... | collective-permute-start | bytes 196616 | tf_op jit(solution)/shard_map/ppermute | solution.py:208
  129.3 1.9 %collective-permute-start.33 = (bf16[32,1024]{1,0:T(8,128)(2,1)S(1)}, bf16[32,1024]{1,0:T(8,128)(2,1)S(1)}, u32[]{:S(2)}, u32[]{:S(2)}) collective-permute-start(bf16[32,1024]{1,0:T(8,128)(2,1)S(1)} %get-tuple-element.41), channel_id=1, source_target_pairs={{0,2},{1,3},{2,0},{3,1},{4,6},{5,7},{6,4},{7,5},{8,10},{9,11},{10,... | collective-permute-start | bytes 196616 | tf_op jit(solution)/shard_map/ppermute | solution.py:208
  131.2 1.7 %collective-permute-done.31 = bf16[32,1024]{1,0:T(8,128)(2,1)S(1)} collective-permute-done((bf16[32,1024]{1,0:T(8,128)(2,1)S(1)}, bf16[32,1024]{1,0:T(8,128)(2,1)S(1)}, u32[]{:S(2)}, u32[]{:S(2)}) %collective-permute-start.31) | collective-permute-done | bytes 65568 | tf_op jit(solution)/shard_map/ppermute | solution.py:208
  132.9 1.4 collective-permute-done.32
  134.3 0.8 fusion.23
  135.9 2.1 %collective-permute-start.34 = (bf16[32,1024]{1,0:T(8,128)(2,1)S(1)}, bf16[32,1024]{1,0:T(8,128)(2,1)S(1)}, u32[]{:S(2)}, u32[]{:S(2)}) collective-permute-start(bf16[32,1024]{1,0:T(8,128)(2,1)S(1)} %get-tuple-element.59), channel_id=1, source_target_pairs={{0,6},{1,7},{2,4},{3,5},{4,2},{5,3},{6,0},{7,1},{8,14},{9,15},{10,... | collective-permute-start | bytes 196616 | tf_op jit(solution)/shard_map/ppermute | solution.py:220
  138.5 1.8 %collective-permute-start.36 = (bf16[32,1024]{1,0:T(8,128)(2,1)S(1)}, bf16[32,1024]{1,0:T(8,128)(2,1)S(1)}, u32[]{:S(2)}, u32[]{:S(2)}) collective-permute-start(bf16[32,1024]{1,0:T(8,128)(2,1)S(1)} %get-tuple-element.59), channel_id=1, source_target_pairs={{0,2},{1,3},{2,0},{3,1},{4,6},{5,7},{6,4},{7,5},{8,10},{9,11},{10,... | collective-permute-start | bytes 196616 | tf_op jit(solution)/shard_map/ppermute | solution.py:220
  140.3 1.7 %collective-permute-done.34 = bf16[32,1024]{1,0:T(8,128)(2,1)S(1)} collective-permute-done((bf16[32,1024]{1,0:T(8,128)(2,1)S(1)}, bf16[32,1024]{1,0:T(8,128)(2,1)S(1)}, u32[]{:S(2)}, u32[]{:S(2)}) %collective-permute-start.34) | collective-permute-done | bytes 65568 | tf_op jit(solution)/shard_map/ppermute | solution.py:220
  142.0 1.5 collective-permute-done.35
  144.9 5.1 %collective-permute-done.37.refs_7_ = bf16[128,1024]{1,0:T(8,128)(2,1)S(1)} collective-permute-done((bf16[128,1024]{1,0:T(8,128)(2,1)S(1)}, bf16[128,1024]{1,0:T(8,128)(2,1)S(1)}, u32[]{:S(2)}, u32[]{:S(2)}) %collective-permute-start.37) | collective-permute-done | bytes 262176 | tf_op jit(solution)/shard_map/ppermute | solution.py:251
  150.0 0.7 subtract_convert_fusion.1
  151.5 3.6 %shard_map.52 = bf16[1024,1024]{1,0:T(8,128)(2,1)} custom-call(s32[8]{0:T(128)} %stack.35.start_ref, bf16[128,1024]{1,0:T(8,128)(2,1)} %copy-done.2, bf16[128,1024]{1,0:T(8,128)(2,1)} %copy-done.6, bf16[128,1024]{1,0:T(8,128)(2,1)} %copy-done.4, bf16[128,1024]{1,0:T(8,128)(2,1)} %copy-done.9, bf16[128,1024]{1,0:T(8,128)(2,1)} %copy-done.5, ...), custom_call_target="tpu_custom_call" | custom-call | bytes 4194304 | tf_op jit(solution)/shard_map/pallas_call | solution.py:117
  155.1 1.2 shard_map.53.refs_0_
  156.3 3.1 %collective-permute-done.38.part_ref = bf16[128,2048]{1,0:T(8,128)(2,1)S(1)} collective-permute-done((bf16[128,2048]{1,0:T(8,128)(2,1)S(1)}, bf16[128,2048]{1,0:T(8,128)(2,1)S(1)}, u32[]{:S(2)}, u32[]{:S(2)}) %collective-permute-start.38) | collective-permute-done | bytes 524320 | tf_op jit(solution)/shard_map/ppermute | solution.py:256
  159.4 1.2 shard_map.54
  (99 shorter events, 18.1 us)
Async XLA Ops:
  5.7 9.5 %collective-permute-start = (bf16[128,1024]{1,0:T(8,128)(2,1)}, bf16[128,1024]{1,0:T(8,128)(2,1)S(1)}, u32[]{:S(2)}, u32[]{:S(2)}) collective-permute-start(bf16[128,1024]{1,0:T(8,128)(2,1)} %get-tuple-element.16), channel_id=1, source_target_pairs={{0,1},{1,0},{2,3},{3,2},{4,5},{5,4},{6,7},{7,6},{8,9},{9,8},{10,11... | collective-permute-start | bytes 786440 | tf_op jit(solution)/shard_map/ppermute | solution.py:240
  8.7 6.5 %copy-start.12 = (f32[128,1024]{1,0:T(8,128)S(1)}, f32[128,1024]{1,0:T(8,128)}, u32[]{:S(2)}) copy-start(f32[128,1024]{1,0:T(8,128)} %get-tuple-element.18) | copy-start | bytes 1572868
  15.3 6.6 %collective-permute-start.1 = (bf16[32,1024]{1,0:T(8,128)(2,1)S(1)}, bf16[32,1024]{1,0:T(8,128)(2,1)S(1)}, u32[]{:S(2)}, u32[]{:S(2)}) collective-permute-start(bf16[32,1024]{1,0:T(8,128)(2,1)S(1)} %get-tuple-element.49), channel_id=1, source_target_pairs={{0,6},{1,7},{2,4},{3,5},{4,2},{5,3},{6,0},{7,1},{8,14},{9,15},{10,... | collective-permute-start | bytes 196616 | tf_op jit(solution)/shard_map/ppermute | solution.py:208
  19.2 5.4 %collective-permute-start.2 = (bf16[32,1024]{1,0:T(8,128)(2,1)S(1)}, bf16[32,1024]{1,0:T(8,128)(2,1)S(1)}, u32[]{:S(2)}, u32[]{:S(2)}) collective-permute-start(bf16[32,1024]{1,0:T(8,128)(2,1)S(1)} %get-tuple-element.51), channel_id=1, source_target_pairs={{0,4},{1,5},{2,6},{3,7},{4,0},{5,1},{6,2},{7,3},{8,12},{9,13},{10,... | collective-permute-start | bytes 196616 | tf_op jit(solution)/shard_map/ppermute | solution.py:208
  19.2 5.4 %collective-permute-start.3 = (bf16[32,1024]{1,0:T(8,128)(2,1)S(1)}, bf16[32,1024]{1,0:T(8,128)(2,1)S(1)}, u32[]{:S(2)}, u32[]{:S(2)}) collective-permute-start(bf16[32,1024]{1,0:T(8,128)(2,1)S(1)} %get-tuple-element.50), channel_id=1, source_target_pairs={{0,2},{1,3},{2,0},{3,1},{4,6},{5,7},{6,4},{7,5},{8,10},{9,11},{10,... | collective-permute-start | bytes 196616 | tf_op jit(solution)/shard_map/ppermute | solution.py:208
  19.9 10.2 %copy-start = (bf16[2048,1024]{1,0:T(8,128)(2,1)S(1)}, bf16[2048,1024]{1,0:T(8,128)(2,1)}, u32[]{:S(2)}) copy-start(bf16[2048,1024]{1,0:T(8,128)(2,1)} %x_ref.3) | copy-start | bytes 12582916
  27.7 11.1 %copy-start.8 = (f32[128,2048]{1,0:T(8,128)S(1)}, f32[128,2048]{1,0:T(8,128)}, u32[]{:S(2)}) copy-start(f32[128,2048]{1,0:T(8,128)} %get-tuple-element.22) | copy-start | bytes 3145732
  27.8 6.8 %collective-permute-start.4 = (bf16[32,1024]{1,0:T(8,128)(2,1)S(1)}, bf16[32,1024]{1,0:T(8,128)(2,1)S(1)}, u32[]{:S(2)}, u32[]{:S(2)}) collective-permute-start(bf16[32,1024]{1,0:T(8,128)(2,1)S(1)} %get-tuple-element.53), channel_id=1, source_target_pairs={{0,6},{1,7},{2,4},{3,5},{4,2},{5,3},{6,0},{7,1},{8,14},{9,15},{10,... | collective-permute-start | bytes 196616 | tf_op jit(solution)/shard_map/ppermute | solution.py:220
  31.7 12.1 %copy-start.7 = (f32[128,2048]{1,0:T(8,128)S(1)}, f32[128,2048]{1,0:T(8,128)}, u32[]{:S(2)}) copy-start(f32[128,2048]{1,0:T(8,128)} %get-tuple-element.23) | copy-start | bytes 3145732
  31.7 5.6 %collective-permute-start.5 = (bf16[32,1024]{1,0:T(8,128)(2,1)S(1)}, bf16[32,1024]{1,0:T(8,128)(2,1)S(1)}, u32[]{:S(2)}, u32[]{:S(2)}) collective-permute-start(bf16[32,1024]{1,0:T(8,128)(2,1)S(1)} %get-tuple-element.53), channel_id=1, source_target_pairs={{0,4},{1,5},{2,6},{3,7},{4,0},{5,1},{6,2},{7,3},{8,12},{9,13},{10,... | collective-permute-start | bytes 196616 | tf_op jit(solution)/shard_map/ppermute | solution.py:220
  31.8 5.5 %collective-permute-start.6 = (bf16[32,1024]{1,0:T(8,128)(2,1)S(1)}, bf16[32,1024]{1,0:T(8,128)(2,1)S(1)}, u32[]{:S(2)}, u32[]{:S(2)}) collective-permute-start(bf16[32,1024]{1,0:T(8,128)(2,1)S(1)} %get-tuple-element.53), channel_id=1, source_target_pairs={{0,2},{1,3},{2,0},{3,1},{4,6},{5,7},{6,4},{7,5},{8,10},{9,11},{10,... | collective-permute-start | bytes 196616 | tf_op jit(solution)/shard_map/ppermute | solution.py:220
  37.3 7.2 %copy-start.2 = (bf16[128,1024]{1,0:T(8,128)(2,1)}, bf16[128,1024]{1,0:T(8,128)(2,1)S(1)}, u32[]{:S(2)}) copy-start(bf16[128,1024]{1,0:T(8,128)(2,1)S(1)} %constant_dynamic-update-slice_fusion.12.refs_0_) | copy-start | bytes 786436
  37.3 6.4 %collective-permute-start.7 = (bf16[128,1024]{1,0:T(8,128)(2,1)S(1)}, bf16[128,1024]{1,0:T(8,128)(2,1)S(1)}, u32[]{:S(2)}, u32[]{:S(2)}) collective-permute-start(bf16[128,1024]{1,0:T(8,128)(2,1)S(1)} %constant_dynamic-update-slice_fusion.12.refs_0_), channel_id=1, source_target_pairs={{0,1},{1,0},{2,3},{3,2},{4,5},{5,4},{6,7},{7,6},{8,9},{9,8},{10,11... | collective-permute-start | bytes 786440 | tf_op jit(solution)/shard_map/ppermute | solution.py:251
  39.6 8.7 %collective-permute-start.8 = (bf16[128,2048]{1,0:T(8,128)(2,1)S(1)}, bf16[128,2048]{1,0:T(8,128)(2,1)S(1)}, u32[]{:S(2)}, u32[]{:S(2)}) collective-permute-start(bf16[128,2048]{1,0:T(8,128)(2,1)S(1)} %fusion.1), channel_id=1, source_target_pairs={{0,8},{8,16},{16,24},{24,0},{1,9},{9,17},{17,25},{25,1},{2,10},{10... | collective-permute-start | bytes 1572872 | tf_op jit(solution)/shard_map/ppermute | solution.py:256
  43.7 5.3 %copy-start.6 = (bf16[128,1024]{1,0:T(8,128)(2,1)}, bf16[128,1024]{1,0:T(8,128)(2,1)S(1)}, u32[]{:S(2)}) copy-start(bf16[128,1024]{1,0:T(8,128)(2,1)S(1)} %collective-permute-done.7.refs_1_) | copy-start | bytes 786436
  44.5 9.4 %collective-permute-start.10 = (bf16[128,2048]{1,0:T(8,128)(2,1)S(1)}, bf16[128,2048]{1,0:T(8,128)(2,1)S(1)}, u32[]{:S(2)}, u32[]{:S(2)}) collective-permute-start(bf16[128,2048]{1,0:T(8,128)(2,1)S(1)} %fusion.2), channel_id=1, source_target_pairs={{0,8},{8,16},{16,24},{24,0},{1,9},{9,17},{17,25},{25,1},{2,10},{10... | collective-permute-start | bytes 1572872 | tf_op jit(solution)/shard_map/ppermute | solution.py:256
  49.0 15.2 %copy-start.1 = (bf16[1024,1024]{1,0:T(8,128)(2,1)S(1)}, bf16[1024,1024]{1,0:T(8,128)(2,1)}, u32[]{:S(2)}) copy-start(bf16[1024,1024]{1,0:T(8,128)(2,1)} %get-tuple-element.20) | copy-start | bytes 6291460
  49.0 7.4 %collective-permute-start.9 = (bf16[128,1024]{1,0:T(8,128)(2,1)S(1)}, bf16[128,1024]{1,0:T(8,128)(2,1)S(1)}, u32[]{:S(2)}, u32[]{:S(2)}) collective-permute-start(bf16[128,1024]{1,0:T(8,128)(2,1)S(1)} %convolution_convert_fusion.2), channel_id=1, source_target_pairs={{0,1},{1,0},{2,3},{3,2},{4,5},{5,4},{6,7},{7,6},{8,9},{9,8},{10,11... | collective-permute-start | bytes 786440 | tf_op jit(solution)/shard_map/ppermute | solution.py:240
  56.5 6.2 %collective-permute-start.11 = (bf16[32,1024]{1,0:T(8,128)(2,1)S(1)}, bf16[32,1024]{1,0:T(8,128)(2,1)S(1)}, u32[]{:S(2)}, u32[]{:S(2)}) collective-permute-start(bf16[32,1024]{1,0:T(8,128)(2,1)S(1)} %get-tuple-element.46), channel_id=1, source_target_pairs={{0,6},{1,7},{2,4},{3,5},{4,2},{5,3},{6,0},{7,1},{8,14},{9,15},{10,... | collective-permute-start | bytes 196616 | tf_op jit(solution)/shard_map/ppermute | solution.py:208
  58.6 5.6 %collective-permute-start.12 = (bf16[32,1024]{1,0:T(8,128)(2,1)S(1)}, bf16[32,1024]{1,0:T(8,128)(2,1)S(1)}, u32[]{:S(2)}, u32[]{:S(2)}) collective-permute-start(bf16[32,1024]{1,0:T(8,128)(2,1)S(1)} %get-tuple-element.48), channel_id=1, source_target_pairs={{0,4},{1,5},{2,6},{3,7},{4,0},{5,1},{6,2},{7,3},{8,12},{9,13},{10,... | collective-permute-start | bytes 196616 | tf_op jit(solution)/shard_map/ppermute | solution.py:208
  59.0 5.2 %collective-permute-start.13 = (bf16[32,1024]{1,0:T(8,128)(2,1)S(1)}, bf16[32,1024]{1,0:T(8,128)(2,1)S(1)}, u32[]{:S(2)}, u32[]{:S(2)}) collective-permute-start(bf16[32,1024]{1,0:T(8,128)(2,1)S(1)} %get-tuple-element.47), channel_id=1, source_target_pairs={{0,2},{1,3},{2,0},{3,1},{4,6},{5,7},{6,4},{7,5},{8,10},{9,11},{10,... | collective-permute-start | bytes 196616 | tf_op jit(solution)/shard_map/ppermute | solution.py:208
  65.7 6.1 %collective-permute-start.14 = (bf16[32,1024]{1,0:T(8,128)(2,1)S(1)}, bf16[32,1024]{1,0:T(8,128)(2,1)S(1)}, u32[]{:S(2)}, u32[]{:S(2)}) collective-permute-start(bf16[32,1024]{1,0:T(8,128)(2,1)S(1)} %get-tuple-element.55), channel_id=1, source_target_pairs={{0,6},{1,7},{2,4},{3,5},{4,2},{5,3},{6,0},{7,1},{8,14},{9,15},{10,... | collective-permute-start | bytes 196616 | tf_op jit(solution)/shard_map/ppermute | solution.py:220
  67.8 5.5 %collective-permute-start.15 = (bf16[32,1024]{1,0:T(8,128)(2,1)S(1)}, bf16[32,1024]{1,0:T(8,128)(2,1)S(1)}, u32[]{:S(2)}, u32[]{:S(2)}) collective-permute-start(bf16[32,1024]{1,0:T(8,128)(2,1)S(1)} %get-tuple-element.55), channel_id=1, source_target_pairs={{0,4},{1,5},{2,6},{3,7},{4,0},{5,1},{6,2},{7,3},{8,12},{9,13},{10,... | collective-permute-start | bytes 196616 | tf_op jit(solution)/shard_map/ppermute | solution.py:220
  68.4 5.0 %collective-permute-start.16 = (bf16[32,1024]{1,0:T(8,128)(2,1)S(1)}, bf16[32,1024]{1,0:T(8,128)(2,1)S(1)}, u32[]{:S(2)}, u32[]{:S(2)}) collective-permute-start(bf16[32,1024]{1,0:T(8,128)(2,1)S(1)} %get-tuple-element.55), channel_id=1, source_target_pairs={{0,2},{1,3},{2,0},{3,1},{4,6},{5,7},{6,4},{7,5},{8,10},{9,11},{10,... | collective-permute-start | bytes 196616 | tf_op jit(solution)/shard_map/ppermute | solution.py:220
  73.4 7.2 %copy-start.4 = (bf16[128,1024]{1,0:T(8,128)(2,1)}, bf16[128,1024]{1,0:T(8,128)(2,1)S(1)}, u32[]{:S(2)}) copy-start(bf16[128,1024]{1,0:T(8,128)(2,1)S(1)} %constant_dynamic-update-slice_fusion.8.refs_2_) | copy-start | bytes 786436
  73.4 6.4 %collective-permute-start.17 = (bf16[128,1024]{1,0:T(8,128)(2,1)S(1)}, bf16[128,1024]{1,0:T(8,128)(2,1)S(1)}, u32[]{:S(2)}, u32[]{:S(2)}) collective-permute-start(bf16[128,1024]{1,0:T(8,128)(2,1)S(1)} %constant_dynamic-update-slice_fusion.8.refs_2_), channel_id=1, source_target_pairs={{0,1},{1,0},{2,3},{3,2},{4,5},{5,4},{6,7},{7,6},{8,9},{9,8},{10,11... | collective-permute-start | bytes 786440 | tf_op jit(solution)/shard_map/ppermute | solution.py:251
  74.7 8.7 %collective-permute-start.18 = (bf16[128,2048]{1,0:T(8,128)(2,1)S(1)}, bf16[128,2048]{1,0:T(8,128)(2,1)S(1)}, u32[]{:S(2)}, u32[]{:S(2)}) collective-permute-start(bf16[128,2048]{1,0:T(8,128)(2,1)S(1)} %subtract_convert_fusion.5), channel_id=1, source_target_pairs={{0,8},{8,16},{16,24},{24,0},{1,9},{9,17},{17,25},{25,1},{2,10},{10... | collective-permute-start | bytes 1572872 | tf_op jit(solution)/shard_map/ppermute | solution.py:256
  79.8 4.3 %copy-start.9 = (bf16[128,1024]{1,0:T(8,128)(2,1)}, bf16[128,1024]{1,0:T(8,128)(2,1)S(1)}, u32[]{:S(2)}) copy-start(bf16[128,1024]{1,0:T(8,128)(2,1)S(1)} %collective-permute-done.17.refs_3_) | copy-start | bytes 786436
  80.6 8.8 %collective-permute-start.20 = (bf16[128,2048]{1,0:T(8,128)(2,1)S(1)}, bf16[128,2048]{1,0:T(8,128)(2,1)S(1)}, u32[]{:S(2)}, u32[]{:S(2)}) collective-permute-start(bf16[128,2048]{1,0:T(8,128)(2,1)S(1)} %subtract_convert_fusion.4), channel_id=1, source_target_pairs={{0,8},{8,16},{16,24},{24,0},{1,9},{9,17},{17,25},{25,1},{2,10},{10... | collective-permute-start | bytes 1572872 | tf_op jit(solution)/shard_map/ppermute | solution.py:256
  84.1 6.4 %collective-permute-start.19 = (bf16[128,1024]{1,0:T(8,128)(2,1)S(1)}, bf16[128,1024]{1,0:T(8,128)(2,1)S(1)}, u32[]{:S(2)}, u32[]{:S(2)}) collective-permute-start(bf16[128,1024]{1,0:T(8,128)(2,1)S(1)} %convolution_convert_fusion.1), channel_id=1, source_target_pairs={{0,1},{1,0},{2,3},{3,2},{4,5},{5,4},{6,7},{7,6},{8,9},{9,8},{10,11... | collective-permute-start | bytes 786440 | tf_op jit(solution)/shard_map/ppermute | solution.py:240
  90.6 6.1 %collective-permute-start.21 = (bf16[32,1024]{1,0:T(8,128)(2,1)S(1)}, bf16[32,1024]{1,0:T(8,128)(2,1)S(1)}, u32[]{:S(2)}, u32[]{:S(2)}) collective-permute-start(bf16[32,1024]{1,0:T(8,128)(2,1)S(1)} %get-tuple-element.43), channel_id=1, source_target_pairs={{0,6},{1,7},{2,4},{3,5},{4,2},{5,3},{6,0},{7,1},{8,14},{9,15},{10,... | collective-permute-start | bytes 196616 | tf_op jit(solution)/shard_map/ppermute | solution.py:208
  92.7 5.5 %collective-permute-start.22 = (bf16[32,1024]{1,0:T(8,128)(2,1)S(1)}, bf16[32,1024]{1,0:T(8,128)(2,1)S(1)}, u32[]{:S(2)}, u32[]{:S(2)}) collective-permute-start(bf16[32,1024]{1,0:T(8,128)(2,1)S(1)} %get-tuple-element.45), channel_id=1, source_target_pairs={{0,4},{1,5},{2,6},{3,7},{4,0},{5,1},{6,2},{7,3},{8,12},{9,13},{10,... | collective-permute-start | bytes 196616 | tf_op jit(solution)/shard_map/ppermute | solution.py:208
  93.3 5.0 %collective-permute-start.23 = (bf16[32,1024]{1,0:T(8,128)(2,1)S(1)}, bf16[32,1024]{1,0:T(8,128)(2,1)S(1)}, u32[]{:S(2)}, u32[]{:S(2)}) collective-permute-start(bf16[32,1024]{1,0:T(8,128)(2,1)S(1)} %get-tuple-element.44), channel_id=1, source_target_pairs={{0,2},{1,3},{2,0},{3,1},{4,6},{5,7},{6,4},{7,5},{8,10},{9,11},{10,... | collective-permute-start | bytes 196616 | tf_op jit(solution)/shard_map/ppermute | solution.py:208
  99.8 6.1 %collective-permute-start.24 = (bf16[32,1024]{1,0:T(8,128)(2,1)S(1)}, bf16[32,1024]{1,0:T(8,128)(2,1)S(1)}, u32[]{:S(2)}, u32[]{:S(2)}) collective-permute-start(bf16[32,1024]{1,0:T(8,128)(2,1)S(1)} %get-tuple-element.57), channel_id=1, source_target_pairs={{0,6},{1,7},{2,4},{3,5},{4,2},{5,3},{6,0},{7,1},{8,14},{9,15},{10,... | collective-permute-start | bytes 196616 | tf_op jit(solution)/shard_map/ppermute | solution.py:220
  101.9 5.5 %collective-permute-start.25 = (bf16[32,1024]{1,0:T(8,128)(2,1)S(1)}, bf16[32,1024]{1,0:T(8,128)(2,1)S(1)}, u32[]{:S(2)}, u32[]{:S(2)}) collective-permute-start(bf16[32,1024]{1,0:T(8,128)(2,1)S(1)} %get-tuple-element.57), channel_id=1, source_target_pairs={{0,4},{1,5},{2,6},{3,7},{4,0},{5,1},{6,2},{7,3},{8,12},{9,13},{10,... | collective-permute-start | bytes 196616 | tf_op jit(solution)/shard_map/ppermute | solution.py:220
  102.4 5.0 %collective-permute-start.26 = (bf16[32,1024]{1,0:T(8,128)(2,1)S(1)}, bf16[32,1024]{1,0:T(8,128)(2,1)S(1)}, u32[]{:S(2)}, u32[]{:S(2)}) collective-permute-start(bf16[32,1024]{1,0:T(8,128)(2,1)S(1)} %get-tuple-element.57), channel_id=1, source_target_pairs={{0,2},{1,3},{2,0},{3,1},{4,6},{5,7},{6,4},{7,5},{8,10},{9,11},{10,... | collective-permute-start | bytes 196616 | tf_op jit(solution)/shard_map/ppermute | solution.py:220
  107.5 7.2 %copy-start.5 = (bf16[128,1024]{1,0:T(8,128)(2,1)}, bf16[128,1024]{1,0:T(8,128)(2,1)S(1)}, u32[]{:S(2)}) copy-start(bf16[128,1024]{1,0:T(8,128)(2,1)S(1)} %constant_dynamic-update-slice_fusion.4.refs_4_) | copy-start | bytes 786436
  107.5 6.4 %collective-permute-start.27 = (bf16[128,1024]{1,0:T(8,128)(2,1)S(1)}, bf16[128,1024]{1,0:T(8,128)(2,1)S(1)}, u32[]{:S(2)}, u32[]{:S(2)}) collective-permute-start(bf16[128,1024]{1,0:T(8,128)(2,1)S(1)} %constant_dynamic-update-slice_fusion.4.refs_4_), channel_id=1, source_target_pairs={{0,1},{1,0},{2,3},{3,2},{4,5},{5,4},{6,7},{7,6},{8,9},{9,8},{10,11... | collective-permute-start | bytes 786440 | tf_op jit(solution)/shard_map/ppermute | solution.py:251
  109.8 8.7 %collective-permute-start.28 = (bf16[128,2048]{1,0:T(8,128)(2,1)S(1)}, bf16[128,2048]{1,0:T(8,128)(2,1)S(1)}, u32[]{:S(2)}, u32[]{:S(2)}) collective-permute-start(bf16[128,2048]{1,0:T(8,128)(2,1)S(1)} %subtract_convert_fusion.3), channel_id=1, source_target_pairs={{0,8},{8,16},{16,24},{24,0},{1,9},{9,17},{17,25},{25,1},{2,10},{10... | collective-permute-start | bytes 1572872 | tf_op jit(solution)/shard_map/ppermute | solution.py:256
  113.9 5.3 %copy-start.10 = (bf16[128,1024]{1,0:T(8,128)(2,1)}, bf16[128,1024]{1,0:T(8,128)(2,1)S(1)}, u32[]{:S(2)}) copy-start(bf16[128,1024]{1,0:T(8,128)(2,1)S(1)} %collective-permute-done.27.refs_5_) | copy-start | bytes 786436
  114.7 9.4 %collective-permute-start.30 = (bf16[128,2048]{1,0:T(8,128)(2,1)S(1)}, bf16[128,2048]{1,0:T(8,128)(2,1)S(1)}, u32[]{:S(2)}, u32[]{:S(2)}) collective-permute-start(bf16[128,2048]{1,0:T(8,128)(2,1)S(1)} %subtract_convert_fusion.2), channel_id=1, source_target_pairs={{0,8},{8,16},{16,24},{24,0},{1,9},{9,17},{17,25},{25,1},{2,10},{10... | collective-permute-start | bytes 1572872 | tf_op jit(solution)/shard_map/ppermute | solution.py:256
  119.2 7.4 %collective-permute-start.29 = (bf16[128,1024]{1,0:T(8,128)(2,1)S(1)}, bf16[128,1024]{1,0:T(8,128)(2,1)S(1)}, u32[]{:S(2)}, u32[]{:S(2)}) collective-permute-start(bf16[128,1024]{1,0:T(8,128)(2,1)S(1)} %convolution_convert_fusion), channel_id=1, source_target_pairs={{0,1},{1,0},{2,3},{3,2},{4,5},{5,4},{6,7},{7,6},{8,9},{9,8},{10,11... | collective-permute-start | bytes 786440 | tf_op jit(solution)/shard_map/ppermute | solution.py:240
  126.7 6.2 %collective-permute-start.31 = (bf16[32,1024]{1,0:T(8,128)(2,1)S(1)}, bf16[32,1024]{1,0:T(8,128)(2,1)S(1)}, u32[]{:S(2)}, u32[]{:S(2)}) collective-permute-start(bf16[32,1024]{1,0:T(8,128)(2,1)S(1)} %get-tuple-element.40), channel_id=1, source_target_pairs={{0,6},{1,7},{2,4},{3,5},{4,2},{5,3},{6,0},{7,1},{8,14},{9,15},{10,... | collective-permute-start | bytes 196616 | tf_op jit(solution)/shard_map/ppermute | solution.py:208
  128.8 5.5 %collective-permute-start.32 = (bf16[32,1024]{1,0:T(8,128)(2,1)S(1)}, bf16[32,1024]{1,0:T(8,128)(2,1)S(1)}, u32[]{:S(2)}, u32[]{:S(2)}) collective-permute-start(bf16[32,1024]{1,0:T(8,128)(2,1)S(1)} %get-tuple-element.42), channel_id=1, source_target_pairs={{0,4},{1,5},{2,6},{3,7},{4,0},{5,1},{6,2},{7,3},{8,12},{9,13},{10,... | collective-permute-start | bytes 196616 | tf_op jit(solution)/shard_map/ppermute | solution.py:208
  129.3 5.0 %collective-permute-start.33 = (bf16[32,1024]{1,0:T(8,128)(2,1)S(1)}, bf16[32,1024]{1,0:T(8,128)(2,1)S(1)}, u32[]{:S(2)}, u32[]{:S(2)}) collective-permute-start(bf16[32,1024]{1,0:T(8,128)(2,1)S(1)} %get-tuple-element.41), channel_id=1, source_target_pairs={{0,2},{1,3},{2,0},{3,1},{4,6},{5,7},{6,4},{7,5},{8,10},{9,11},{10,... | collective-permute-start | bytes 196616 | tf_op jit(solution)/shard_map/ppermute | solution.py:208
  135.9 6.1 %collective-permute-start.34 = (bf16[32,1024]{1,0:T(8,128)(2,1)S(1)}, bf16[32,1024]{1,0:T(8,128)(2,1)S(1)}, u32[]{:S(2)}, u32[]{:S(2)}) collective-permute-start(bf16[32,1024]{1,0:T(8,128)(2,1)S(1)} %get-tuple-element.59), channel_id=1, source_target_pairs={{0,6},{1,7},{2,4},{3,5},{4,2},{5,3},{6,0},{7,1},{8,14},{9,15},{10,... | collective-permute-start | bytes 196616 | tf_op jit(solution)/shard_map/ppermute | solution.py:220
  137.9 5.6 %collective-permute-start.35 = (bf16[32,1024]{1,0:T(8,128)(2,1)S(1)}, bf16[32,1024]{1,0:T(8,128)(2,1)S(1)}, u32[]{:S(2)}, u32[]{:S(2)}) collective-permute-start(bf16[32,1024]{1,0:T(8,128)(2,1)S(1)} %get-tuple-element.59), channel_id=1, source_target_pairs={{0,4},{1,5},{2,6},{3,7},{4,0},{5,1},{6,2},{7,3},{8,12},{9,13},{10,... | collective-permute-start | bytes 196616 | tf_op jit(solution)/shard_map/ppermute | solution.py:220
  138.5 5.0 %collective-permute-start.36 = (bf16[32,1024]{1,0:T(8,128)(2,1)S(1)}, bf16[32,1024]{1,0:T(8,128)(2,1)S(1)}, u32[]{:S(2)}, u32[]{:S(2)}) collective-permute-start(bf16[32,1024]{1,0:T(8,128)(2,1)S(1)} %get-tuple-element.59), channel_id=1, source_target_pairs={{0,2},{1,3},{2,0},{3,1},{4,6},{5,7},{6,4},{7,5},{8,10},{9,11},{10,... | collective-permute-start | bytes 196616 | tf_op jit(solution)/shard_map/ppermute | solution.py:220
  143.5 7.2 %copy-start.3 = (bf16[128,1024]{1,0:T(8,128)(2,1)}, bf16[128,1024]{1,0:T(8,128)(2,1)S(1)}, u32[]{:S(2)}) copy-start(bf16[128,1024]{1,0:T(8,128)(2,1)S(1)} %constant_dynamic-update-slice_fusion.refs_6_) | copy-start | bytes 786436
  143.5 6.4 %collective-permute-start.37 = (bf16[128,1024]{1,0:T(8,128)(2,1)S(1)}, bf16[128,1024]{1,0:T(8,128)(2,1)S(1)}, u32[]{:S(2)}, u32[]{:S(2)}) collective-permute-start(bf16[128,1024]{1,0:T(8,128)(2,1)S(1)} %constant_dynamic-update-slice_fusion.refs_6_), channel_id=1, source_target_pairs={{0,1},{1,0},{2,3},{3,2},{4,5},{5,4},{6,7},{7,6},{8,9},{9,8},{10,11... | collective-permute-start | bytes 786440 | tf_op jit(solution)/shard_map/ppermute | solution.py:251
  144.8 10.3 %collective-permute-start.39 = (bf16[128,2048]{1,0:T(8,128)(2,1)S(1)}, bf16[128,2048]{1,0:T(8,128)(2,1)S(1)}, u32[]{:S(2)}, u32[]{:S(2)}) collective-permute-start(bf16[128,2048]{1,0:T(8,128)(2,1)S(1)} %subtract_convert_fusion), channel_id=1, source_target_pairs={{0,8},{8,16},{16,24},{24,0},{1,9},{9,17},{17,25},{25,1},{2,10},{10... | collective-permute-start | bytes 1572872 | tf_op jit(solution)/shard_map/ppermute | solution.py:256
  150.0 1.5 copy-start.11
  150.7 8.7 %collective-permute-start.38 = (bf16[128,2048]{1,0:T(8,128)(2,1)S(1)}, bf16[128,2048]{1,0:T(8,128)(2,1)S(1)}, u32[]{:S(2)}, u32[]{:S(2)}) collective-permute-start(bf16[128,2048]{1,0:T(8,128)(2,1)S(1)} %subtract_convert_fusion.1), channel_id=1, source_target_pairs={{0,8},{8,16},{16,24},{24,0},{1,9},{9,17},{17,25},{25,1},{2,10},{10... | collective-permute-start | bytes 1572872 | tf_op jit(solution)/shard_map/ppermute | solution.py:256

commit v6 on v5

--- a/solution.py
+++ b/solution.py
@@ -18,33 +18,27 @@
 
 CHUNK = 1024
 LANES = 128
+COLUMNS = 512
 TURN_CHUNK = 512
 FIRST_VMEM = 56 * 1024 * 1024
 SCATTER_VMEM = 12 * 1024 * 1024
 
 
-def first_kernel(lead_ref, away_ref, home_ref, x_ref, term_ref, kept_ref, away_out, home_out, acc):
-    step = pl.program_id(0)
+def first_kernel(lead_ref, away_ref, home_ref, x_ref, term_ref, kept_ref, away_out, home_out, both):
     half = away_ref.shape[1]
-    away = away_ref[...].T
-    home = home_ref[...].T
-    away_out[...] = away
-    home_out[...] = home
-    both = jnp.concatenate([away, home], 0).astype(BF16)
-    product = jnp.dot(both, x_ref[...], preferred_element_type=F32)
-
-    @pl.when(step == 0)
+
+    @pl.when(pl.program_id(0) == 0)
     def _():
-        acc[...] = product
-
-    @pl.when(step > 0)
-    def _():
-        acc[...] += product
-
-    @pl.when(step == pl.num_programs(0) - 1)
-    def _():
-        term_ref[...] = acc[:half, :].astype(BF16)
-        kept_ref[...] = acc[half:, :]
+        away = away_ref[...].T
+        home = home_ref[...].T
+        away_out[...] = away
+        home_out[...] = home
+        both[:half, :] = away.astype(BF16)
+        both[half:, :] = home.astype(BF16)
+
+    product = jnp.dot(both[...], x_ref[...], preferred_element_type=F32)
+    term_ref[...] = product[:half, :].astype(BF16)
+    kept_ref[...] = product[half:, :]
 
 
 def first_projection(features, residual, lead):
@@ -60,19 +54,19 @@
         ),
         grid_spec=pltpu.PrefetchScalarGridSpec(
             num_scalar_prefetch=1,
-            grid=(rows // CHUNK,),
+            grid=(feat_width // COLUMNS,),
             in_specs=[
-                pl.BlockSpec((CHUNK, half), lambda i, lead: (i, lead[0])),
-                pl.BlockSpec((CHUNK, half), lambda i, lead: (i, 1 - lead[0])),
-                pl.BlockSpec((CHUNK, feat_width), lambda i, lead: (i, 0)),
+                pl.BlockSpec((rows, half), lambda i, lead: (0, lead[0])),
+                pl.BlockSpec((rows, half), lambda i, lead: (0, 1 - lead[0])),
+                pl.BlockSpec((rows, COLUMNS), lambda i, lead: (0, i)),
             ],
             out_specs=[
-                pl.BlockSpec((half, feat_width), lambda i, lead: (0, 0)),
-                pl.BlockSpec((half, feat_width), lambda i, lead: (0, 0)),
-                pl.BlockSpec((half, CHUNK), lambda i, lead: (0, i)),
-                pl.BlockSpec((half, CHUNK), lambda i, lead: (0, i)),
+                pl.BlockSpec((half, COLUMNS), lambda i, lead: (0, i)),
+                pl.BlockSpec((half, COLUMNS), lambda i, lead: (0, i)),
+                pl.BlockSpec((half, rows), lambda i, lead: (0, 0)),
+                pl.BlockSpec((half, rows), lambda i, lead: (0, 0)),
             ],
-            scratch_shapes=[pltpu.VMEM((2 * half, feat_width), F32)],
+            scratch_shapes=[pltpu.VMEM((2 * half, rows), BF16)],
         ),
         compiler_params=pltpu.CompilerParams(vmem_limit_bytes=FIRST_VMEM),
         cost_estimate=pl.CostEstimate(
@@ -222,7 +216,7 @@
         return full
 
     updates, starts = [], []
-    kernels = half % LANES == 0 and features.shape[0] % CHUNK == 0 and feat_width % LANES == 0
+    kernels = half % LANES == 0 and features.shape[0] % CHUNK == 0 and feat_width % COLUMNS == 0
     if kernels:
         term, kept, *halves = first_projection(features, residual, 1 - inner_id)
     else:

time: 161 us -> 161 us (level)
  no operation moved by 1% of the time
where the time goes in v6:
time: 161 us
  waiting for transfers between devices  76.5 us (48%)
  starting transfers between devices  46.3 us (29%)
  matrix products  17.8 us (11%)
  Pallas kernels  12.6 us (8%)
  other arithmetic  4.92 us (3%)
    ppermute x8, waiting for transfers between devices, on_device(): lax.ppermute(part.astype(BF16), 'feat', next_block)  25.4 us
    ppermute x4, waiting for transfers between devices, on_device(): update_away = lax.ppermute(update_home, 'rows', partner)  18.2 us
    ppermute x12, starting transfers between devices, reduce_outer(): lax.ppermute(out.astype(BF16), 'rows', outer_step(step)).astype(F32)  17.9 us
    ppermute x12, starting transfers between devices, gather_outer(): got = lax.ppermute(update, 'rows', outer_step(step))  17.8 us
    ppermute x12, waiting for transfers between devices, reduce_outer(): lax.ppermute(out.astype(BF16), 'rows', outer_step(step)).astype(F32)  14.1 us
    ppermute x12, waiting for transfers between devices, gather_outer(): got = lax.ppermute(update, 'rows', outer_step(step))  12.8 us
    dot_general x8, matrix products, apply_inverse(): dot = lambda a, b: lax.dot_general(a, b, dims, preferred_element_type=F32)  7.52 us
    ppermute x4, waiting for transfers between devices, on_device(): arrived = lax.ppermute(term, 'rows', partner)  6.04 us
  transfers between devices with their start and end apart: 40, of which 31 were waited for; matrix products, arithmetic and copies ran while one was open for 10% of the time, Pallas kernels for 4%

profile of v6, /device:TPU:0, one launch (start us, length us, event | category | flops | bytes accessed | tf_op | source)
XLA Modules:
  0.0 160.5 jit_solution(611951181678177945)
XLA Ops:
  0.6 5.1 %shard_map.50 = (bf16[128,1024]{1,0:T(8,128)(2,1)}, f32[128,1024]{1,0:T(8,128)}, f32[128,2048]{1,0:T(8,128)}, f32[128,2048]{1,0:T(8,128)}) custom-call(s32[1]{0:T(128)} %bitcast.8.lead_ref.place_ref, f32[2048,256]{1,0:T(8,128)} %home_ref.1, f32[2048,256]{1,0:T(8,128)} %home_ref.1, bf16[2048,1024]{1,0:T(8,128)(2,1)} %x_ref.3), custom_call_target="tpu_custom_call" | custom-call | flops 1073741824 | bytes 9175040 | tf_op jit(solution)/shard_map/pallas_call | solution.py:47
  5.7 3.0 %collective-permute-start = (bf16[128,1024]{1,0:T(8,128)(2,1)}, bf16[128,1024]{1,0:T(8,128)(2,1)S(1)}, u32[]{:S(2)}, u32[]{:S(2)}) collective-permute-start(bf16[128,1024]{1,0:T(8,128)(2,1)} %get-tuple-element.16), channel_id=1, source_target_pairs={{0,1},{1,0},{2,3},{3,2},{4,5},{5,4},{6,7},{7,6},{8,9},{9,8},{10,11... | collective-permute-start | bytes 786440 | tf_op jit(solution)/shard_map/ppermute | solution.py:234
  8.7 4.5 %fusion = (bf16[1024,1024]{1,0:T(8,128)(2,1)S(1)}, bf16[1024,1024]{1,0:T(8,128)(2,1)}) fusion(f32[1024,1024]{1,0:T(8,128)} %param.5), kind=kLoop, calls=%fused_computation.2 | loop fusion | flops 4194304 | bytes 8388608 | tf_op jit(solution)/shard_map/convert_element_type | solution.py:16
  13.2 2.0 %collective-permute-done = bf16[128,1024]{1,0:T(8,128)(2,1)S(1)} collective-permute-done((bf16[128,1024]{1,0:T(8,128)(2,1)}, bf16[128,1024]{1,0:T(8,128)(2,1)S(1)}, u32[]{:S(2)}, u32[]{:S(2)}) %collective-permute-start) | collective-permute-done | bytes 262176 | tf_op jit(solution)/shard_map/ppermute | solution.py:234
  15.3 3.9 %collective-permute-start.1 = (bf16[32,1024]{1,0:T(8,128)(2,1)S(1)}, bf16[32,1024]{1,0:T(8,128)(2,1)S(1)}, u32[]{:S(2)}, u32[]{:S(2)}) collective-permute-start(bf16[32,1024]{1,0:T(8,128)(2,1)S(1)} %get-tuple-element.49), channel_id=1, source_target_pairs={{0,6},{1,7},{2,4},{3,5},{4,2},{5,3},{6,0},{7,1},{8,14},{9,15},{10,... | collective-permute-start | bytes 196616 | tf_op jit(solution)/shard_map/ppermute | solution.py:202
  19.8 2.0 %collective-permute-done.1 = bf16[32,1024]{1,0:T(8,128)(2,1)S(1)} collective-permute-done((bf16[32,1024]{1,0:T(8,128)(2,1)S(1)}, bf16[32,1024]{1,0:T(8,128)(2,1)S(1)}, u32[]{:S(2)}, u32[]{:S(2)}) %collective-permute-start.1) | collective-permute-done | bytes 65568 | tf_op jit(solution)/shard_map/ppermute | solution.py:202
  21.9 2.7 %collective-permute-done.2 = bf16[32,1024]{1,0:T(8,128)(2,1)S(1)} collective-permute-done((bf16[32,1024]{1,0:T(8,128)(2,1)S(1)}, bf16[32,1024]{1,0:T(8,128)(2,1)S(1)}, u32[]{:S(2)}, u32[]{:S(2)}) %collective-permute-start.2) | collective-permute-done | bytes 65568 | tf_op jit(solution)/shard_map/ppermute | solution.py:202
  24.6 2.3 %fusion.11 = f32[64,1024]{1,0:T(8,128)S(1)} fusion(bf16[1024,1024]{1,0:T(8,128)(2,1)} %get-tuple-element.20, bf16[32,1024]{1,0:T(8,128)(2,1)S(1)} %get-tuple-element.38, bf16[32,1024]{1,0:T(8,128)(2,1)S(1)} %get-tuple-element.39), kind=kOutput, calls=%fused_computation.44 | convolution fusion | flops 134479872 | bytes 2490368 | tf_op jit(solution)/shard_map/dot_general | solution.py:183
  27.7 2.3 %collective-permute-start.4 = (bf16[32,1024]{1,0:T(8,128)(2,1)S(1)}, bf16[32,1024]{1,0:T(8,128)(2,1)S(1)}, u32[]{:S(2)}, u32[]{:S(2)}) collective-permute-start(bf16[32,1024]{1,0:T(8,128)(2,1)S(1)} %get-tuple-element.53), channel_id=1, source_target_pairs={{0,6},{1,7},{2,4},{3,5},{4,2},{5,3},{6,0},{7,1},{8,14},{9,15},{10,... | collective-permute-start | bytes 196616 | tf_op jit(solution)/shard_map/ppermute | solution.py:214
  30.0 1.6 %shard_map.51 = bf16[1024,2048]{1,0:T(8,128)(2,1)S(1)} custom-call(bf16[2048,1024]{1,0:T(8,128)(2,1)S(1)} %copy-done), custom_call_target="tpu_custom_call" | custom-call | bytes 8388608 | tf_op jit(solution)/shard_map/pallas_call | solution.py:86
  31.7 2.2 %collective-permute-start.6 = (bf16[32,1024]{1,0:T(8,128)(2,1)S(1)}, bf16[32,1024]{1,0:T(8,128)(2,1)S(1)}, u32[]{:S(2)}, u32[]{:S(2)}) collective-permute-start(bf16[32,1024]{1,0:T(8,128)(2,1)S(1)} %get-tuple-element.53), channel_id=1, source_target_pairs={{0,2},{1,3},{2,0},{3,1},{4,6},{5,7},{6,4},{7,5},{8,10},{9,11},{10,... | collective-permute-start | bytes 196616 | tf_op jit(solution)/shard_map/ppermute | solution.py:214
  34.5 2.7 %collective-permute-done.5 = bf16[32,1024]{1,0:T(8,128)(2,1)S(1)} collective-permute-done((bf16[32,1024]{1,0:T(8,128)(2,1)S(1)}, bf16[32,1024]{1,0:T(8,128)(2,1)S(1)}, u32[]{:S(2)}, u32[]{:S(2)}) %collective-permute-start.5) | collective-permute-done | bytes 65568 | tf_op jit(solution)/shard_map/ppermute | solution.py:214
  37.3 1.6 collective-permute-start.7
  38.9 0.7 fusion.1
  39.7 4.0 %collective-permute-done.7.refs_1_ = bf16[128,1024]{1,0:T(8,128)(2,1)S(1)} collective-permute-done((bf16[128,1024]{1,0:T(8,128)(2,1)S(1)}, bf16[128,1024]{1,0:T(8,128)(2,1)S(1)}, u32[]{:S(2)}, u32[]{:S(2)}) %collective-permute-start.7) | collective-permute-done | bytes 262176 | tf_op jit(solution)/shard_map/ppermute | solution.py:245
  43.7 0.7 fusion.2
  44.5 3.7 %collective-permute-done.8 = bf16[128,2048]{1,0:T(8,128)(2,1)S(1)} collective-permute-done((bf16[128,2048]{1,0:T(8,128)(2,1)S(1)}, bf16[128,2048]{1,0:T(8,128)(2,1)S(1)}, u32[]{:S(2)}, u32[]{:S(2)}) %collective-permute-start.8) | collective-permute-done | bytes 524320 | tf_op jit(solution)/shard_map/ppermute | solution.py:250
  49.6 4.3 %collective-permute-done.10 = bf16[128,2048]{1,0:T(8,128)(2,1)S(1)} collective-permute-done((bf16[128,2048]{1,0:T(8,128)(2,1)S(1)}, bf16[128,2048]{1,0:T(8,128)(2,1)S(1)}, u32[]{:S(2)}, u32[]{:S(2)}) %collective-permute-start.10) | collective-permute-done | bytes 524320 | tf_op jit(solution)/shard_map/ppermute | solution.py:250
  54.6 1.8 %collective-permute-done.9 = bf16[128,1024]{1,0:T(8,128)(2,1)S(1)} collective-permute-done((bf16[128,1024]{1,0:T(8,128)(2,1)S(1)}, bf16[128,1024]{1,0:T(8,128)(2,1)S(1)}, u32[]{:S(2)}, u32[]{:S(2)}) %collective-permute-start.9) | collective-permute-done | bytes 262176 | tf_op jit(solution)/shard_map/ppermute | solution.py:234
  56.5 2.0 %collective-permute-start.11 = (bf16[32,1024]{1,0:T(8,128)(2,1)S(1)}, bf16[32,1024]{1,0:T(8,128)(2,1)S(1)}, u32[]{:S(2)}, u32[]{:S(2)}) collective-permute-start(bf16[32,1024]{1,0:T(8,128)(2,1)S(1)} %get-tuple-element.46), channel_id=1, source_target_pairs={{0,6},{1,7},{2,4},{3,5},{4,2},{5,3},{6,0},{7,1},{8,14},{9,15},{10,... | collective-permute-start | bytes 196616 | tf_op jit(solution)/shard_map/ppermute | solution.py:202
  59.0 2.0 %collective-permute-start.13 = (bf16[32,1024]{1,0:T(8,128)(2,1)S(1)}, bf16[32,1024]{1,0:T(8,128)(2,1)S(1)}, u32[]{:S(2)}, u32[]{:S(2)}) collective-permute-start(bf16[32,1024]{1,0:T(8,128)(2,1)S(1)} %get-tuple-element.47), channel_id=1, source_target_pairs={{0,2},{1,3},{2,0},{3,1},{4,6},{5,7},{6,4},{7,5},{8,10},{9,11},{10,... | collective-permute-start | bytes 196616 | tf_op jit(solution)/shard_map/ppermute | solution.py:202
  61.0 1.7 %collective-permute-done.11 = bf16[32,1024]{1,0:T(8,128)(2,1)S(1)} collective-permute-done((bf16[32,1024]{1,0:T(8,128)(2,1)S(1)}, bf16[32,1024]{1,0:T(8,128)(2,1)S(1)}, u32[]{:S(2)}, u32[]{:S(2)}) %collective-permute-start.11) | collective-permute-done | bytes 65568 | tf_op jit(solution)/shard_map/ppermute | solution.py:202
  62.7 1.4 collective-permute-done.12
  64.2 0.8 fusion.15
  65.7 2.1 %collective-permute-start.14 = (bf16[32,1024]{1,0:T(8,128)(2,1)S(1)}, bf16[32,1024]{1,0:T(8,128)(2,1)S(1)}, u32[]{:S(2)}, u32[]{:S(2)}) collective-permute-start(bf16[32,1024]{1,0:T(8,128)(2,1)S(1)} %get-tuple-element.55), channel_id=1, source_target_pairs={{0,6},{1,7},{2,4},{3,5},{4,2},{5,3},{6,0},{7,1},{8,14},{9,15},{10,... | collective-permute-start | bytes 196616 | tf_op jit(solution)/shard_map/ppermute | solution.py:214
  68.3 1.8 %collective-permute-start.16 = (bf16[32,1024]{1,0:T(8,128)(2,1)S(1)}, bf16[32,1024]{1,0:T(8,128)(2,1)S(1)}, u32[]{:S(2)}, u32[]{:S(2)}) collective-permute-start(bf16[32,1024]{1,0:T(8,128)(2,1)S(1)} %get-tuple-element.55), channel_id=1, source_target_pairs={{0,2},{1,3},{2,0},{3,1},{4,6},{5,7},{6,4},{7,5},{8,10},{9,11},{10,... | collective-permute-start | bytes 196616 | tf_op jit(solution)/shard_map/ppermute | solution.py:214
  70.1 1.7 %collective-permute-done.14 = bf16[32,1024]{1,0:T(8,128)(2,1)S(1)} collective-permute-done((bf16[32,1024]{1,0:T(8,128)(2,1)S(1)}, bf16[32,1024]{1,0:T(8,128)(2,1)S(1)}, u32[]{:S(2)}, u32[]{:S(2)}) %collective-permute-start.14) | collective-permute-done | bytes 65568 | tf_op jit(solution)/shard_map/ppermute | solution.py:214
  71.8 1.5 collective-permute-done.15
  73.9 0.7 subtract_convert_fusion.5
  74.7 5.1 %collective-permute-done.17.refs_3_ = bf16[128,1024]{1,0:T(8,128)(2,1)S(1)} collective-permute-done((bf16[128,1024]{1,0:T(8,128)(2,1)S(1)}, bf16[128,1024]{1,0:T(8,128)(2,1)S(1)}, u32[]{:S(2)}, u32[]{:S(2)}) %collective-permute-start.17) | collective-permute-done | bytes 262176 | tf_op jit(solution)/shard_map/ppermute | solution.py:245
  79.8 0.7 subtract_convert_fusion.4
  80.8 2.5 %collective-permute-done.18 = bf16[128,2048]{1,0:T(8,128)(2,1)S(1)} collective-permute-done((bf16[128,2048]{1,0:T(8,128)(2,1)S(1)}, bf16[128,2048]{1,0:T(8,128)(2,1)S(1)}, u32[]{:S(2)}, u32[]{:S(2)}) %collective-permute-start.18) | collective-permute-done | bytes 524320 | tf_op jit(solution)/shard_map/ppermute | solution.py:250
  84.1 1.6 collective-permute-start.19
  85.7 3.7 %collective-permute-done.20 = bf16[128,2048]{1,0:T(8,128)(2,1)S(1)} collective-permute-done((bf16[128,2048]{1,0:T(8,128)(2,1)S(1)}, bf16[128,2048]{1,0:T(8,128)(2,1)S(1)}, u32[]{:S(2)}, u32[]{:S(2)}) %collective-permute-start.20) | collective-permute-done | bytes 524320 | tf_op jit(solution)/shard_map/ppermute | solution.py:250
  90.6 2.0 %collective-permute-start.21 = (bf16[32,1024]{1,0:T(8,128)(2,1)S(1)}, bf16[32,1024]{1,0:T(8,128)(2,1)S(1)}, u32[]{:S(2)}, u32[]{:S(2)}) collective-permute-start(bf16[32,1024]{1,0:T(8,128)(2,1)S(1)} %get-tuple-element.43), channel_id=1, source_target_pairs={{0,6},{1,7},{2,4},{3,5},{4,2},{5,3},{6,0},{7,1},{8,14},{9,15},{10,... | collective-permute-start | bytes 196616 | tf_op jit(solution)/shard_map/ppermute | solution.py:202
  93.2 1.8 %collective-permute-start.23 = (bf16[32,1024]{1,0:T(8,128)(2,1)S(1)}, bf16[32,1024]{1,0:T(8,128)(2,1)S(1)}, u32[]{:S(2)}, u32[]{:S(2)}) collective-permute-start(bf16[32,1024]{1,0:T(8,128)(2,1)S(1)} %get-tuple-element.44), channel_id=1, source_target_pairs={{0,2},{1,3},{2,0},{3,1},{4,6},{5,7},{6,4},{7,5},{8,10},{9,11},{10,... | collective-permute-start | bytes 196616 | tf_op jit(solution)/shard_map/ppermute | solution.py:202
  95.1 1.7 %collective-permute-done.21 = bf16[32,1024]{1,0:T(8,128)(2,1)S(1)} collective-permute-done((bf16[32,1024]{1,0:T(8,128)(2,1)S(1)}, bf16[32,1024]{1,0:T(8,128)(2,1)S(1)}, u32[]{:S(2)}, u32[]{:S(2)}) %collective-permute-start.21) | collective-permute-done | bytes 65568 | tf_op jit(solution)/shard_map/ppermute | solution.py:202
  96.8 1.5 collective-permute-done.22
  98.3 0.8 fusion.19
  99.8 2.1 %collective-permute-start.24 = (bf16[32,1024]{1,0:T(8,128)(2,1)S(1)}, bf16[32,1024]{1,0:T(8,128)(2,1)S(1)}, u32[]{:S(2)}, u32[]{:S(2)}) collective-permute-start(bf16[32,1024]{1,0:T(8,128)(2,1)S(1)} %get-tuple-element.57), channel_id=1, source_target_pairs={{0,6},{1,7},{2,4},{3,5},{4,2},{5,3},{6,0},{7,1},{8,14},{9,15},{10,... | collective-permute-start | bytes 196616 | tf_op jit(solution)/shard_map/ppermute | solution.py:214
  102.4 1.8 %collective-permute-start.26 = (bf16[32,1024]{1,0:T(8,128)(2,1)S(1)}, bf16[32,1024]{1,0:T(8,128)(2,1)S(1)}, u32[]{:S(2)}, u32[]{:S(2)}) collective-permute-start(bf16[32,1024]{1,0:T(8,128)(2,1)S(1)} %get-tuple-element.57), channel_id=1, source_target_pairs={{0,2},{1,3},{2,0},{3,1},{4,6},{5,7},{6,4},{7,5},{8,10},{9,11},{10,... | collective-permute-start | bytes 196616 | tf_op jit(solution)/shard_map/ppermute | solution.py:214
  104.2 1.7 %collective-permute-done.24 = bf16[32,1024]{1,0:T(8,128)(2,1)S(1)} collective-permute-done((bf16[32,1024]{1,0:T(8,128)(2,1)S(1)}, bf16[32,1024]{1,0:T(8,128)(2,1)S(1)}, u32[]{:S(2)}, u32[]{:S(2)}) %collective-permute-start.24) | collective-permute-done | bytes 65568 | tf_op jit(solution)/shard_map/ppermute | solution.py:214
  105.9 1.5 collective-permute-done.25
  107.4 1.6 collective-permute-start.27
  109.8 4.0 %collective-permute-done.27.refs_5_ = bf16[128,1024]{1,0:T(8,128)(2,1)S(1)} collective-permute-done((bf16[128,1024]{1,0:T(8,128)(2,1)S(1)}, bf16[128,1024]{1,0:T(8,128)(2,1)S(1)}, u32[]{:S(2)}, u32[]{:S(2)}) %collective-permute-start.27) | collective-permute-done | bytes 262176 | tf_op jit(solution)/shard_map/ppermute | solution.py:245
  113.9 0.7 subtract_convert_fusion.2
  114.7 3.7 %collective-permute-done.28 = bf16[128,2048]{1,0:T(8,128)(2,1)S(1)} collective-permute-done((bf16[128,2048]{1,0:T(8,128)(2,1)S(1)}, bf16[128,2048]{1,0:T(8,128)(2,1)S(1)}, u32[]{:S(2)}, u32[]{:S(2)}) %collective-permute-start.28) | collective-permute-done | bytes 524320 | tf_op jit(solution)/shard_map/ppermute | solution.py:250
  119.7 4.3 %collective-permute-done.30 = bf16[128,2048]{1,0:T(8,128)(2,1)S(1)} collective-permute-done((bf16[128,2048]{1,0:T(8,128)(2,1)S(1)}, bf16[128,2048]{1,0:T(8,128)(2,1)S(1)}, u32[]{:S(2)}, u32[]{:S(2)}) %collective-permute-start.30) | collective-permute-done | bytes 524320 | tf_op jit(solution)/shard_map/ppermute | solution.py:250
  124.8 1.8 %collective-permute-done.29 = bf16[128,1024]{1,0:T(8,128)(2,1)S(1)} collective-permute-done((bf16[128,1024]{1,0:T(8,128)(2,1)S(1)}, bf16[128,1024]{1,0:T(8,128)(2,1)S(1)}, u32[]{:S(2)}, u32[]{:S(2)}) %collective-permute-start.29) | collective-permute-done | bytes 262176 | tf_op jit(solution)/shard_map/ppermute | solution.py:234
  126.7 2.0 %collective-permute-start.31 = (bf16[32,1024]{1,0:T(8,128)(2,1)S(1)}, bf16[32,1024]{1,0:T(8,128)(2,1)S(1)}, u32[]{:S(2)}, u32[]{:S(2)}) collective-permute-start(bf16[32,1024]{1,0:T(8,128)(2,1)S(1)} %get-tuple-element.40), channel_id=1, source_target_pairs={{0,6},{1,7},{2,4},{3,5},{4,2},{5,3},{6,0},{7,1},{8,14},{9,15},{10,... | collective-permute-start | bytes 196616 | tf_op jit(solution)/shard_map/ppermute | solution.py:202
  129.3 1.9 %collective-permute-start.33 = (bf16[32,1024]{1,0:T(8,128)(2,1)S(1)}, bf16[32,1024]{1,0:T(8,128)(2,1)S(1)}, u32[]{:S(2)}, u32[]{:S(2)}) collective-permute-start(bf16[32,1024]{1,0:T(8,128)(2,1)S(1)} %get-tuple-element.41), channel_id=1, source_target_pairs={{0,2},{1,3},{2,0},{3,1},{4,6},{5,7},{6,4},{7,5},{8,10},{9,11},{10,... | collective-permute-start | bytes 196616 | tf_op jit(solution)/shard_map/ppermute | solution.py:202
  131.1 1.7 %collective-permute-done.31 = bf16[32,1024]{1,0:T(8,128)(2,1)S(1)} collective-permute-done((bf16[32,1024]{1,0:T(8,128)(2,1)S(1)}, bf16[32,1024]{1,0:T(8,128)(2,1)S(1)}, u32[]{:S(2)}, u32[]{:S(2)}) %collective-permute-start.31) | collective-permute-done | bytes 65568 | tf_op jit(solution)/shard_map/ppermute | solution.py:202
  132.9 1.4 collective-permute-done.32
  134.3 0.8 fusion.23
  135.8 2.0 %collective-permute-start.34 = (bf16[32,1024]{1,0:T(8,128)(2,1)S(1)}, bf16[32,1024]{1,0:T(8,128)(2,1)S(1)}, u32[]{:S(2)}, u32[]{:S(2)}) collective-permute-start(bf16[32,1024]{1,0:T(8,128)(2,1)S(1)} %get-tuple-element.59), channel_id=1, source_target_pairs={{0,6},{1,7},{2,4},{3,5},{4,2},{5,3},{6,0},{7,1},{8,14},{9,15},{10,... | collective-permute-start | bytes 196616 | tf_op jit(solution)/shard_map/ppermute | solution.py:214
  138.5 1.8 %collective-permute-start.36 = (bf16[32,1024]{1,0:T(8,128)(2,1)S(1)}, bf16[32,1024]{1,0:T(8,128)(2,1)S(1)}, u32[]{:S(2)}, u32[]{:S(2)}) collective-permute-start(bf16[32,1024]{1,0:T(8,128)(2,1)S(1)} %get-tuple-element.59), channel_id=1, source_target_pairs={{0,2},{1,3},{2,0},{3,1},{4,6},{5,7},{6,4},{7,5},{8,10},{9,11},{10,... | collective-permute-start | bytes 196616 | tf_op jit(solution)/shard_map/ppermute | solution.py:214
  140.3 1.7 %collective-permute-done.34 = bf16[32,1024]{1,0:T(8,128)(2,1)S(1)} collective-permute-done((bf16[32,1024]{1,0:T(8,128)(2,1)S(1)}, bf16[32,1024]{1,0:T(8,128)(2,1)S(1)}, u32[]{:S(2)}, u32[]{:S(2)}) %collective-permute-start.34) | collective-permute-done | bytes 65568 | tf_op jit(solution)/shard_map/ppermute | solution.py:214
  142.0 1.5 collective-permute-done.35
  144.9 5.1 %collective-permute-done.37.refs_7_ = bf16[128,1024]{1,0:T(8,128)(2,1)S(1)} collective-permute-done((bf16[128,1024]{1,0:T(8,128)(2,1)S(1)}, bf16[128,1024]{1,0:T(8,128)(2,1)S(1)}, u32[]{:S(2)}, u32[]{:S(2)}) %collective-permute-start.37) | collective-permute-done | bytes 262176 | tf_op jit(solution)/shard_map/ppermute | solution.py:245
  149.9 0.7 subtract_convert_fusion.1
  151.5 3.6 %shard_map.52 = bf16[1024,1024]{1,0:T(8,128)(2,1)} custom-call(s32[8]{0:T(128)} %stack.35.start_ref, bf16[128,1024]{1,0:T(8,128)(2,1)} %copy-done.2, bf16[128,1024]{1,0:T(8,128)(2,1)} %copy-done.6, bf16[128,1024]{1,0:T(8,128)(2,1)} %copy-done.4, bf16[128,1024]{1,0:T(8,128)(2,1)} %copy-done.9, bf16[128,1024]{1,0:T(8,128)(2,1)} %copy-done.5, ...), custom_call_target="tpu_custom_call" | custom-call | bytes 4194304 | tf_op jit(solution)/shard_map/pallas_call | solution.py:111
  155.1 1.2 shard_map.53.refs_0_
  156.3 3.1 %collective-permute-done.38.part_ref = bf16[128,2048]{1,0:T(8,128)(2,1)S(1)} collective-permute-done((bf16[128,2048]{1,0:T(8,128)(2,1)S(1)}, bf16[128,2048]{1,0:T(8,128)(2,1)S(1)}, u32[]{:S(2)}, u32[]{:S(2)}) %collective-permute-start.38) | collective-permute-done | bytes 524320 | tf_op jit(solution)/shard_map/ppermute | solution.py:250
  159.4 1.2 shard_map.54
  (99 shorter events, 18.1 us)
Async XLA Ops:
  5.7 9.5 %collective-permute-start = (bf16[128,1024]{1,0:T(8,128)(2,1)}, bf16[128,1024]{1,0:T(8,128)(2,1)S(1)}, u32[]{:S(2)}, u32[]{:S(2)}) collective-permute-start(bf16[128,1024]{1,0:T(8,128)(2,1)} %get-tuple-element.16), channel_id=1, source_target_pairs={{0,1},{1,0},{2,3},{3,2},{4,5},{5,4},{6,7},{7,6},{8,9},{9,8},{10,11... | collective-permute-start | bytes 786440 | tf_op jit(solution)/shard_map/ppermute | solution.py:234
  8.7 6.5 %copy-start.12 = (f32[128,1024]{1,0:T(8,128)S(1)}, f32[128,1024]{1,0:T(8,128)}, u32[]{:S(2)}) copy-start(f32[128,1024]{1,0:T(8,128)} %get-tuple-element.18) | copy-start | bytes 1572868
  15.3 6.6 %collective-permute-start.1 = (bf16[32,1024]{1,0:T(8,128)(2,1)S(1)}, bf16[32,1024]{1,0:T(8,128)(2,1)S(1)}, u32[]{:S(2)}, u32[]{:S(2)}) collective-permute-start(bf16[32,1024]{1,0:T(8,128)(2,1)S(1)} %get-tuple-element.49), channel_id=1, source_target_pairs={{0,6},{1,7},{2,4},{3,5},{4,2},{5,3},{6,0},{7,1},{8,14},{9,15},{10,... | collective-permute-start | bytes 196616 | tf_op jit(solution)/shard_map/ppermute | solution.py:202
  19.2 5.4 %collective-permute-start.2 = (bf16[32,1024]{1,0:T(8,128)(2,1)S(1)}, bf16[32,1024]{1,0:T(8,128)(2,1)S(1)}, u32[]{:S(2)}, u32[]{:S(2)}) collective-permute-start(bf16[32,1024]{1,0:T(8,128)(2,1)S(1)} %get-tuple-element.51), channel_id=1, source_target_pairs={{0,4},{1,5},{2,6},{3,7},{4,0},{5,1},{6,2},{7,3},{8,12},{9,13},{10,... | collective-permute-start | bytes 196616 | tf_op jit(solution)/shard_map/ppermute | solution.py:202
  19.2 5.4 %collective-permute-start.3 = (bf16[32,1024]{1,0:T(8,128)(2,1)S(1)}, bf16[32,1024]{1,0:T(8,128)(2,1)S(1)}, u32[]{:S(2)}, u32[]{:S(2)}) collective-permute-start(bf16[32,1024]{1,0:T(8,128)(2,1)S(1)} %get-tuple-element.50), channel_id=1, source_target_pairs={{0,2},{1,3},{2,0},{3,1},{4,6},{5,7},{6,4},{7,5},{8,10},{9,11},{10,... | collective-permute-start | bytes 196616 | tf_op jit(solution)/shard_map/ppermute | solution.py:202
  19.8 10.2 %copy-start = (bf16[2048,1024]{1,0:T(8,128)(2,1)S(1)}, bf16[2048,1024]{1,0:T(8,128)(2,1)}, u32[]{:S(2)}) copy-start(bf16[2048,1024]{1,0:T(8,128)(2,1)} %x_ref.3) | copy-start | bytes 12582916
  27.7 11.1 %copy-start.8 = (f32[128,2048]{1,0:T(8,128)S(1)}, f32[128,2048]{1,0:T(8,128)}, u32[]{:S(2)}) copy-start(f32[128,2048]{1,0:T(8,128)} %get-tuple-element.22) | copy-start | bytes 3145732
  27.7 6.8 %collective-permute-start.4 = (bf16[32,1024]{1,0:T(8,128)(2,1)S(1)}, bf16[32,1024]{1,0:T(8,128)(2,1)S(1)}, u32[]{:S(2)}, u32[]{:S(2)}) collective-permute-start(bf16[32,1024]{1,0:T(8,128)(2,1)S(1)} %get-tuple-element.53), channel_id=1, source_target_pairs={{0,6},{1,7},{2,4},{3,5},{4,2},{5,3},{6,0},{7,1},{8,14},{9,15},{10,... | collective-permute-start | bytes 196616 | tf_op jit(solution)/shard_map/ppermute | solution.py:214
  31.7 12.1 %copy-start.7 = (f32[128,2048]{1,0:T(8,128)S(1)}, f32[128,2048]{1,0:T(8,128)}, u32[]{:S(2)}) copy-start(f32[128,2048]{1,0:T(8,128)} %get-tuple-element.23) | copy-start | bytes 3145732
  31.7 5.6 %collective-permute-start.5 = (bf16[32,1024]{1,0:T(8,128)(2,1)S(1)}, bf16[32,1024]{1,0:T(8,128)(2,1)S(1)}, u32[]{:S(2)}, u32[]{:S(2)}) collective-permute-start(bf16[32,1024]{1,0:T(8,128)(2,1)S(1)} %get-tuple-element.53), channel_id=1, source_target_pairs={{0,4},{1,5},{2,6},{3,7},{4,0},{5,1},{6,2},{7,3},{8,12},{9,13},{10,... | collective-permute-start | bytes 196616 | tf_op jit(solution)/shard_map/ppermute | solution.py:214
  31.7 5.5 %collective-permute-start.6 = (bf16[32,1024]{1,0:T(8,128)(2,1)S(1)}, bf16[32,1024]{1,0:T(8,128)(2,1)S(1)}, u32[]{:S(2)}, u32[]{:S(2)}) collective-permute-start(bf16[32,1024]{1,0:T(8,128)(2,1)S(1)} %get-tuple-element.53), channel_id=1, source_target_pairs={{0,2},{1,3},{2,0},{3,1},{4,6},{5,7},{6,4},{7,5},{8,10},{9,11},{10,... | collective-permute-start | bytes 196616 | tf_op jit(solution)/shard_map/ppermute | solution.py:214
  37.3 7.2 %copy-start.2 = (bf16[128,1024]{1,0:T(8,128)(2,1)}, bf16[128,1024]{1,0:T(8,128)(2,1)S(1)}, u32[]{:S(2)}) copy-start(bf16[128,1024]{1,0:T(8,128)(2,1)S(1)} %constant_dynamic-update-slice_fusion.12.refs_0_) | copy-start | bytes 786436
  37.3 6.4 %collective-permute-start.7 = (bf16[128,1024]{1,0:T(8,128)(2,1)S(1)}, bf16[128,1024]{1,0:T(8,128)(2,1)S(1)}, u32[]{:S(2)}, u32[]{:S(2)}) collective-permute-start(bf16[128,1024]{1,0:T(8,128)(2,1)S(1)} %constant_dynamic-update-slice_fusion.12.refs_0_), channel_id=1, source_target_pairs={{0,1},{1,0},{2,3},{3,2},{4,5},{5,4},{6,7},{7,6},{8,9},{9,8},{10,11... | collective-permute-start | bytes 786440 | tf_op jit(solution)/shard_map/ppermute | solution.py:245
  39.6 8.7 %collective-permute-start.8 = (bf16[128,2048]{1,0:T(8,128)(2,1)S(1)}, bf16[128,2048]{1,0:T(8,128)(2,1)S(1)}, u32[]{:S(2)}, u32[]{:S(2)}) collective-permute-start(bf16[128,2048]{1,0:T(8,128)(2,1)S(1)} %fusion.1), channel_id=1, source_target_pairs={{0,8},{8,16},{16,24},{24,0},{1,9},{9,17},{17,25},{25,1},{2,10},{10... | collective-permute-start | bytes 1572872 | tf_op jit(solution)/shard_map/ppermute | solution.py:250
  43.7 5.3 %copy-start.6 = (bf16[128,1024]{1,0:T(8,128)(2,1)}, bf16[128,1024]{1,0:T(8,128)(2,1)S(1)}, u32[]{:S(2)}) copy-start(bf16[128,1024]{1,0:T(8,128)(2,1)S(1)} %collective-permute-done.7.refs_1_) | copy-start | bytes 786436
  44.5 9.4 %collective-permute-start.10 = (bf16[128,2048]{1,0:T(8,128)(2,1)S(1)}, bf16[128,2048]{1,0:T(8,128)(2,1)S(1)}, u32[]{:S(2)}, u32[]{:S(2)}) collective-permute-start(bf16[128,2048]{1,0:T(8,128)(2,1)S(1)} %fusion.2), channel_id=1, source_target_pairs={{0,8},{8,16},{16,24},{24,0},{1,9},{9,17},{17,25},{25,1},{2,10},{10... | collective-permute-start | bytes 1572872 | tf_op jit(solution)/shard_map/ppermute | solution.py:250
  49.0 15.2 %copy-start.1 = (bf16[1024,1024]{1,0:T(8,128)(2,1)S(1)}, bf16[1024,1024]{1,0:T(8,128)(2,1)}, u32[]{:S(2)}) copy-start(bf16[1024,1024]{1,0:T(8,128)(2,1)} %get-tuple-element.20) | copy-start | bytes 6291460
  49.0 7.4 %collective-permute-start.9 = (bf16[128,1024]{1,0:T(8,128)(2,1)S(1)}, bf16[128,1024]{1,0:T(8,128)(2,1)S(1)}, u32[]{:S(2)}, u32[]{:S(2)}) collective-permute-start(bf16[128,1024]{1,0:T(8,128)(2,1)S(1)} %convolution_convert_fusion.2), channel_id=1, source_target_pairs={{0,1},{1,0},{2,3},{3,2},{4,5},{5,4},{6,7},{7,6},{8,9},{9,8},{10,11... | collective-permute-start | bytes 786440 | tf_op jit(solution)/shard_map/ppermute | solution.py:234
  56.5 6.2 %collective-permute-start.11 = (bf16[32,1024]{1,0:T(8,128)(2,1)S(1)}, bf16[32,1024]{1,0:T(8,128)(2,1)S(1)}, u32[]{:S(2)}, u32[]{:S(2)}) collective-permute-start(bf16[32,1024]{1,0:T(8,128)(2,1)S(1)} %get-tuple-element.46), channel_id=1, source_target_pairs={{0,6},{1,7},{2,4},{3,5},{4,2},{5,3},{6,0},{7,1},{8,14},{9,15},{10,... | collective-permute-start | bytes 196616 | tf_op jit(solution)/shard_map/ppermute | solution.py:202
  58.6 5.6 %collective-permute-start.12 = (bf16[32,1024]{1,0:T(8,128)(2,1)S(1)}, bf16[32,1024]{1,0:T(8,128)(2,1)S(1)}, u32[]{:S(2)}, u32[]{:S(2)}) collective-permute-start(bf16[32,1024]{1,0:T(8,128)(2,1)S(1)} %get-tuple-element.48), channel_id=1, source_target_pairs={{0,4},{1,5},{2,6},{3,7},{4,0},{5,1},{6,2},{7,3},{8,12},{9,13},{10,... | collective-permute-start | bytes 196616 | tf_op jit(solution)/shard_map/ppermute | solution.py:202
  59.0 5.2 %collective-permute-start.13 = (bf16[32,1024]{1,0:T(8,128)(2,1)S(1)}, bf16[32,1024]{1,0:T(8,128)(2,1)S(1)}, u32[]{:S(2)}, u32[]{:S(2)}) collective-permute-start(bf16[32,1024]{1,0:T(8,128)(2,1)S(1)} %get-tuple-element.47), channel_id=1, source_target_pairs={{0,2},{1,3},{2,0},{3,1},{4,6},{5,7},{6,4},{7,5},{8,10},{9,11},{10,... | collective-permute-start | bytes 196616 | tf_op jit(solution)/shard_map/ppermute | solution.py:202
  65.7 6.1 %collective-permute-start.14 = (bf16[32,1024]{1,0:T(8,128)(2,1)S(1)}, bf16[32,1024]{1,0:T(8,128)(2,1)S(1)}, u32[]{:S(2)}, u32[]{:S(2)}) collective-permute-start(bf16[32,1024]{1,0:T(8,128)(2,1)S(1)} %get-tuple-element.55), channel_id=1, source_target_pairs={{0,6},{1,7},{2,4},{3,5},{4,2},{5,3},{6,0},{7,1},{8,14},{9,15},{10,... | collective-permute-start | bytes 196616 | tf_op jit(solution)/shard_map/ppermute | solution.py:214
  67.8 5.5 %collective-permute-start.15 = (bf16[32,1024]{1,0:T(8,128)(2,1)S(1)}, bf16[32,1024]{1,0:T(8,128)(2,1)S(1)}, u32[]{:S(2)}, u32[]{:S(2)}) collective-permute-start(bf16[32,1024]{1,0:T(8,128)(2,1)S(1)} %get-tuple-element.55), channel_id=1, source_target_pairs={{0,4},{1,5},{2,6},{3,7},{4,0},{5,1},{6,2},{7,3},{8,12},{9,13},{10,... | collective-permute-start | bytes 196616 | tf_op jit(solution)/shard_map/ppermute | solution.py:214
  68.3 5.0 %collective-permute-start.16 = (bf16[32,1024]{1,0:T(8,128)(2,1)S(1)}, bf16[32,1024]{1,0:T(8,128)(2,1)S(1)}, u32[]{:S(2)}, u32[]{:S(2)}) collective-permute-start(bf16[32,1024]{1,0:T(8,128)(2,1)S(1)} %get-tuple-element.55), channel_id=1, source_target_pairs={{0,2},{1,3},{2,0},{3,1},{4,6},{5,7},{6,4},{7,5},{8,10},{9,11},{10,... | collective-permute-start | bytes 196616 | tf_op jit(solution)/shard_map/ppermute | solution.py:214
  73.3 7.2 %copy-start.4 = (bf16[128,1024]{1,0:T(8,128)(2,1)}, bf16[128,1024]{1,0:T(8,128)(2,1)S(1)}, u32[]{:S(2)}) copy-start(bf16[128,1024]{1,0:T(8,128)(2,1)S(1)} %constant_dynamic-update-slice_fusion.8.refs_2_) | copy-start | bytes 786436
  73.4 6.4 %collective-permute-start.17 = (bf16[128,1024]{1,0:T(8,128)(2,1)S(1)}, bf16[128,1024]{1,0:T(8,128)(2,1)S(1)}, u32[]{:S(2)}, u32[]{:S(2)}) collective-permute-start(bf16[128,1024]{1,0:T(8,128)(2,1)S(1)} %constant_dynamic-update-slice_fusion.8.refs_2_), channel_id=1, source_target_pairs={{0,1},{1,0},{2,3},{3,2},{4,5},{5,4},{6,7},{7,6},{8,9},{9,8},{10,11... | collective-permute-start | bytes 786440 | tf_op jit(solution)/shard_map/ppermute | solution.py:245
  74.7 8.7 %collective-permute-start.18 = (bf16[128,2048]{1,0:T(8,128)(2,1)S(1)}, bf16[128,2048]{1,0:T(8,128)(2,1)S(1)}, u32[]{:S(2)}, u32[]{:S(2)}) collective-permute-start(bf16[128,2048]{1,0:T(8,128)(2,1)S(1)} %subtract_convert_fusion.5), channel_id=1, source_target_pairs={{0,8},{8,16},{16,24},{24,0},{1,9},{9,17},{17,25},{25,1},{2,10},{10... | collective-permute-start | bytes 1572872 | tf_op jit(solution)/shard_map/ppermute | solution.py:250
  79.8 4.3 %copy-start.9 = (bf16[128,1024]{1,0:T(8,128)(2,1)}, bf16[128,1024]{1,0:T(8,128)(2,1)S(1)}, u32[]{:S(2)}) copy-start(bf16[128,1024]{1,0:T(8,128)(2,1)S(1)} %collective-permute-done.17.refs_3_) | copy-start | bytes 786436
  80.5 8.8 %collective-permute-start.20 = (bf16[128,2048]{1,0:T(8,128)(2,1)S(1)}, bf16[128,2048]{1,0:T(8,128)(2,1)S(1)}, u32[]{:S(2)}, u32[]{:S(2)}) collective-permute-start(bf16[128,2048]{1,0:T(8,128)(2,1)S(1)} %subtract_convert_fusion.4), channel_id=1, source_target_pairs={{0,8},{8,16},{16,24},{24,0},{1,9},{9,17},{17,25},{25,1},{2,10},{10... | collective-permute-start | bytes 1572872 | tf_op jit(solution)/shard_map/ppermute | solution.py:250
  84.1 6.4 %collective-permute-start.19 = (bf16[128,1024]{1,0:T(8,128)(2,1)S(1)}, bf16[128,1024]{1,0:T(8,128)(2,1)S(1)}, u32[]{:S(2)}, u32[]{:S(2)}) collective-permute-start(bf16[128,1024]{1,0:T(8,128)(2,1)S(1)} %convolution_convert_fusion.1), channel_id=1, source_target_pairs={{0,1},{1,0},{2,3},{3,2},{4,5},{5,4},{6,7},{7,6},{8,9},{9,8},{10,11... | collective-permute-start | bytes 786440 | tf_op jit(solution)/shard_map/ppermute | solution.py:234
  90.6 6.1 %collective-permute-start.21 = (bf16[32,1024]{1,0:T(8,128)(2,1)S(1)}, bf16[32,1024]{1,0:T(8,128)(2,1)S(1)}, u32[]{:S(2)}, u32[]{:S(2)}) collective-permute-start(bf16[32,1024]{1,0:T(8,128)(2,1)S(1)} %get-tuple-element.43), channel_id=1, source_target_pairs={{0,6},{1,7},{2,4},{3,5},{4,2},{5,3},{6,0},{7,1},{8,14},{9,15},{10,... | collective-permute-start | bytes 196616 | tf_op jit(solution)/shard_map/ppermute | solution.py:202
  92.7 5.5 %collective-permute-start.22 = (bf16[32,1024]{1,0:T(8,128)(2,1)S(1)}, bf16[32,1024]{1,0:T(8,128)(2,1)S(1)}, u32[]{:S(2)}, u32[]{:S(2)}) collective-permute-start(bf16[32,1024]{1,0:T(8,128)(2,1)S(1)} %get-tuple-element.45), channel_id=1, source_target_pairs={{0,4},{1,5},{2,6},{3,7},{4,0},{5,1},{6,2},{7,3},{8,12},{9,13},{10,... | collective-permute-start | bytes 196616 | tf_op jit(solution)/shard_map/ppermute | solution.py:202
  93.2 5.0 %collective-permute-start.23 = (bf16[32,1024]{1,0:T(8,128)(2,1)S(1)}, bf16[32,1024]{1,0:T(8,128)(2,1)S(1)}, u32[]{:S(2)}, u32[]{:S(2)}) collective-permute-start(bf16[32,1024]{1,0:T(8,128)(2,1)S(1)} %get-tuple-element.44), channel_id=1, source_target_pairs={{0,2},{1,3},{2,0},{3,1},{4,6},{5,7},{6,4},{7,5},{8,10},{9,11},{10,... | collective-permute-start | bytes 196616 | tf_op jit(solution)/shard_map/ppermute | solution.py:202
  99.8 6.1 %collective-permute-start.24 = (bf16[32,1024]{1,0:T(8,128)(2,1)S(1)}, bf16[32,1024]{1,0:T(8,128)(2,1)S(1)}, u32[]{:S(2)}, u32[]{:S(2)}) collective-permute-start(bf16[32,1024]{1,0:T(8,128)(2,1)S(1)} %get-tuple-element.57), channel_id=1, source_target_pairs={{0,6},{1,7},{2,4},{3,5},{4,2},{5,3},{6,0},{7,1},{8,14},{9,15},{10,... | collective-permute-start | bytes 196616 | tf_op jit(solution)/shard_map/ppermute | solution.py:214
  101.8 5.5 %collective-permute-start.25 = (bf16[32,1024]{1,0:T(8,128)(2,1)S(1)}, bf16[32,1024]{1,0:T(8,128)(2,1)S(1)}, u32[]{:S(2)}, u32[]{:S(2)}) collective-permute-start(bf16[32,1024]{1,0:T(8,128)(2,1)S(1)} %get-tuple-element.57), channel_id=1, source_target_pairs={{0,4},{1,5},{2,6},{3,7},{4,0},{5,1},{6,2},{7,3},{8,12},{9,13},{10,... | collective-permute-start | bytes 196616 | tf_op jit(solution)/shard_map/ppermute | solution.py:214
  102.4 5.0 %collective-permute-start.26 = (bf16[32,1024]{1,0:T(8,128)(2,1)S(1)}, bf16[32,1024]{1,0:T(8,128)(2,1)S(1)}, u32[]{:S(2)}, u32[]{:S(2)}) collective-permute-start(bf16[32,1024]{1,0:T(8,128)(2,1)S(1)} %get-tuple-element.57), channel_id=1, source_target_pairs={{0,2},{1,3},{2,0},{3,1},{4,6},{5,7},{6,4},{7,5},{8,10},{9,11},{10,... | collective-permute-start | bytes 196616 | tf_op jit(solution)/shard_map/ppermute | solution.py:214
  107.4 7.2 %copy-start.5 = (bf16[128,1024]{1,0:T(8,128)(2,1)}, bf16[128,1024]{1,0:T(8,128)(2,1)S(1)}, u32[]{:S(2)}) copy-start(bf16[128,1024]{1,0:T(8,128)(2,1)S(1)} %constant_dynamic-update-slice_fusion.4.refs_4_) | copy-start | bytes 786436
  107.4 6.4 %collective-permute-start.27 = (bf16[128,1024]{1,0:T(8,128)(2,1)S(1)}, bf16[128,1024]{1,0:T(8,128)(2,1)S(1)}, u32[]{:S(2)}, u32[]{:S(2)}) collective-permute-start(bf16[128,1024]{1,0:T(8,128)(2,1)S(1)} %constant_dynamic-update-slice_fusion.4.refs_4_), channel_id=1, source_target_pairs={{0,1},{1,0},{2,3},{3,2},{4,5},{5,4},{6,7},{7,6},{8,9},{9,8},{10,11... | collective-permute-start | bytes 786440 | tf_op jit(solution)/shard_map/ppermute | solution.py:245
  109.8 8.7 %collective-permute-start.28 = (bf16[128,2048]{1,0:T(8,128)(2,1)S(1)}, bf16[128,2048]{1,0:T(8,128)(2,1)S(1)}, u32[]{:S(2)}, u32[]{:S(2)}) collective-permute-start(bf16[128,2048]{1,0:T(8,128)(2,1)S(1)} %subtract_convert_fusion.3), channel_id=1, source_target_pairs={{0,8},{8,16},{16,24},{24,0},{1,9},{9,17},{17,25},{25,1},{2,10},{10... | collective-permute-start | bytes 1572872 | tf_op jit(solution)/shard_map/ppermute | solution.py:250
  113.9 5.3 %copy-start.10 = (bf16[128,1024]{1,0:T(8,128)(2,1)}, bf16[128,1024]{1,0:T(8,128)(2,1)S(1)}, u32[]{:S(2)}) copy-start(bf16[128,1024]{1,0:T(8,128)(2,1)S(1)} %collective-permute-done.27.refs_5_) | copy-start | bytes 786436
  114.6 9.4 %collective-permute-start.30 = (bf16[128,2048]{1,0:T(8,128)(2,1)S(1)}, bf16[128,2048]{1,0:T(8,128)(2,1)S(1)}, u32[]{:S(2)}, u32[]{:S(2)}) collective-permute-start(bf16[128,2048]{1,0:T(8,128)(2,1)S(1)} %subtract_convert_fusion.2), channel_id=1, source_target_pairs={{0,8},{8,16},{16,24},{24,0},{1,9},{9,17},{17,25},{25,1},{2,10},{10... | collective-permute-start | bytes 1572872 | tf_op jit(solution)/shard_map/ppermute | solution.py:250
  119.2 7.4 %collective-permute-start.29 = (bf16[128,1024]{1,0:T(8,128)(2,1)S(1)}, bf16[128,1024]{1,0:T(8,128)(2,1)S(1)}, u32[]{:S(2)}, u32[]{:S(2)}) collective-permute-start(bf16[128,1024]{1,0:T(8,128)(2,1)S(1)} %convolution_convert_fusion), channel_id=1, source_target_pairs={{0,1},{1,0},{2,3},{3,2},{4,5},{5,4},{6,7},{7,6},{8,9},{9,8},{10,11... | collective-permute-start | bytes 786440 | tf_op jit(solution)/shard_map/ppermute | solution.py:234
  126.7 6.2 %collective-permute-start.31 = (bf16[32,1024]{1,0:T(8,128)(2,1)S(1)}, bf16[32,1024]{1,0:T(8,128)(2,1)S(1)}, u32[]{:S(2)}, u32[]{:S(2)}) collective-permute-start(bf16[32,1024]{1,0:T(8,128)(2,1)S(1)} %get-tuple-element.40), channel_id=1, source_target_pairs={{0,6},{1,7},{2,4},{3,5},{4,2},{5,3},{6,0},{7,1},{8,14},{9,15},{10,... | collective-permute-start | bytes 196616 | tf_op jit(solution)/shard_map/ppermute | solution.py:202
  128.7 5.5 %collective-permute-start.32 = (bf16[32,1024]{1,0:T(8,128)(2,1)S(1)}, bf16[32,1024]{1,0:T(8,128)(2,1)S(1)}, u32[]{:S(2)}, u32[]{:S(2)}) collective-permute-start(bf16[32,1024]{1,0:T(8,128)(2,1)S(1)} %get-tuple-element.42), channel_id=1, source_target_pairs={{0,4},{1,5},{2,6},{3,7},{4,0},{5,1},{6,2},{7,3},{8,12},{9,13},{10,... | collective-permute-start | bytes 196616 | tf_op jit(solution)/shard_map/ppermute | solution.py:202
  129.3 5.0 %collective-permute-start.33 = (bf16[32,1024]{1,0:T(8,128)(2,1)S(1)}, bf16[32,1024]{1,0:T(8,128)(2,1)S(1)}, u32[]{:S(2)}, u32[]{:S(2)}) collective-permute-start(bf16[32,1024]{1,0:T(8,128)(2,1)S(1)} %get-tuple-element.41), channel_id=1, source_target_pairs={{0,2},{1,3},{2,0},{3,1},{4,6},{5,7},{6,4},{7,5},{8,10},{9,11},{10,... | collective-permute-start | bytes 196616 | tf_op jit(solution)/shard_map/ppermute | solution.py:202
  135.8 6.1 %collective-permute-start.34 = (bf16[32,1024]{1,0:T(8,128)(2,1)S(1)}, bf16[32,1024]{1,0:T(8,128)(2,1)S(1)}, u32[]{:S(2)}, u32[]{:S(2)}) collective-permute-start(bf16[32,1024]{1,0:T(8,128)(2,1)S(1)} %get-tuple-element.59), channel_id=1, source_target_pairs={{0,6},{1,7},{2,4},{3,5},{4,2},{5,3},{6,0},{7,1},{8,14},{9,15},{10,... | collective-permute-start | bytes 196616 | tf_op jit(solution)/shard_map/ppermute | solution.py:214
  137.9 5.6 %collective-permute-start.35 = (bf16[32,1024]{1,0:T(8,128)(2,1)S(1)}, bf16[32,1024]{1,0:T(8,128)(2,1)S(1)}, u32[]{:S(2)}, u32[]{:S(2)}) collective-permute-start(bf16[32,1024]{1,0:T(8,128)(2,1)S(1)} %get-tuple-element.59), channel_id=1, source_target_pairs={{0,4},{1,5},{2,6},{3,7},{4,0},{5,1},{6,2},{7,3},{8,12},{9,13},{10,... | collective-permute-start | bytes 196616 | tf_op jit(solution)/shard_map/ppermute | solution.py:214
  138.5 5.0 %collective-permute-start.36 = (bf16[32,1024]{1,0:T(8,128)(2,1)S(1)}, bf16[32,1024]{1,0:T(8,128)(2,1)S(1)}, u32[]{:S(2)}, u32[]{:S(2)}) collective-permute-start(bf16[32,1024]{1,0:T(8,128)(2,1)S(1)} %get-tuple-element.59), channel_id=1, source_target_pairs={{0,2},{1,3},{2,0},{3,1},{4,6},{5,7},{6,4},{7,5},{8,10},{9,11},{10,... | collective-permute-start | bytes 196616 | tf_op jit(solution)/shard_map/ppermute | solution.py:214
  143.5 7.2 %copy-start.3 = (bf16[128,1024]{1,0:T(8,128)(2,1)}, bf16[128,1024]{1,0:T(8,128)(2,1)S(1)}, u32[]{:S(2)}) copy-start(bf16[128,1024]{1,0:T(8,128)(2,1)S(1)} %constant_dynamic-update-slice_fusion.refs_6_) | copy-start | bytes 786436
  143.5 6.4 %collective-permute-start.37 = (bf16[128,1024]{1,0:T(8,128)(2,1)S(1)}, bf16[128,1024]{1,0:T(8,128)(2,1)S(1)}, u32[]{:S(2)}, u32[]{:S(2)}) collective-permute-start(bf16[128,1024]{1,0:T(8,128)(2,1)S(1)} %constant_dynamic-update-slice_fusion.refs_6_), channel_id=1, source_target_pairs={{0,1},{1,0},{2,3},{3,2},{4,5},{5,4},{6,7},{7,6},{8,9},{9,8},{10,11... | collective-permute-start | bytes 786440 | tf_op jit(solution)/shard_map/ppermute | solution.py:245
  144.8 10.3 %collective-permute-start.39 = (bf16[128,2048]{1,0:T(8,128)(2,1)S(1)}, bf16[128,2048]{1,0:T(8,128)(2,1)S(1)}, u32[]{:S(2)}, u32[]{:S(2)}) collective-permute-start(bf16[128,2048]{1,0:T(8,128)(2,1)S(1)} %subtract_convert_fusion), channel_id=1, source_target_pairs={{0,8},{8,16},{16,24},{24,0},{1,9},{9,17},{17,25},{25,1},{2,10},{10... | collective-permute-start | bytes 1572872 | tf_op jit(solution)/shard_map/ppermute | solution.py:250
  149.9 1.5 copy-start.11
  150.7 8.7 %collective-permute-start.38 = (bf16[128,2048]{1,0:T(8,128)(2,1)S(1)}, bf16[128,2048]{1,0:T(8,128)(2,1)S(1)}, u32[]{:S(2)}, u32[]{:S(2)}) collective-permute-start(bf16[128,2048]{1,0:T(8,128)(2,1)S(1)} %subtract_convert_fusion.1), channel_id=1, source_target_pairs={{0,8},{8,16},{16,24},{24,0},{1,9},{9,17},{17,25},{25,1},{2,10},{10... | collective-permute-start | bytes 1572872 | tf_op jit(solution)/shard_map/ppermute | solution.py:250
